TPU v7x, 128 devices: a whole 4x4x4 slice. The times are simulated.
128 devices in a mesh: gz: 4 (over z), gx: 32 (over y, x, core).
Axes of the slice: x: 4, y: 4, z: 4, core: 2. Of those that a mesh axis runs over, the one named last changes fastest.
Arguments:
- features: bfloat16 [4, 6144, 6144], P('gz', 'gx'), may hold values from -6 to 6
- active_count: int32 [4, 32], P('gz', 'gx'), may hold values from 48 to 192, as said below
- neighbors: int32 [4, 27, 6144], P('gz', None, 'gx'), may hold values from -1 to 623
- owner: int32 [4, 6144], P('gz', 'gx'), may hold values from 0 to 127, as said below
- arrival_cell: int32 [4, 12288], P('gz', 'gx'), may hold values from -1 to 191, as said below
- w_enc: bfloat16 [27, 96, 96], replicated, may hold values from -0.125 to 0.125
- w_down: bfloat16 [768, 96], replicated, may hold values from -0.21875 to 0.21875
- w_mid: bfloat16 [27, 96, 96], replicated, may hold values from -0.125 to 0.125
- w_up: bfloat16 [96, 768], replicated, may hold values from -0.625 to 0.625
- w_dec: bfloat16 [27, 96, 96], replicated, may hold values from -0.125 to 0.125
Outputs:
- decoded: bfloat16 [4, 6144, 6144], P('gz', 'gx')
Inputs may be any that keep to these rules, and one draw needn't show every extreme that they name: `active_count`: at least 48; some device has exactly 192 active bricks and some exactly 48. Every device sends either no brick or exactly 3 bricks to each owner, and every owner receives exactly 192 bricks in all. `arrival_cell`: row o, slot s * 3 + r is the cell of the r-th brick (in brick order) that device s sends to owner o, or -1 if s sends none to o; each owner's cells 0 to 191 each occur once.
All inputs are finite; a program needn't handle non-finite values.
Results may differ from a plain program's by a relative error of at most 0.0095.
Values may be sent and summed in bfloat16 or wider, within the bound.
A program may use at most 128 MiB of HBM per device.

v0:
```python
import jax
import jax.numpy as jnp
from jax import lax
from jax.sharding import PartitionSpec as P


def padded_2(block, sides, width):
    for axis, dim in sides:
        count = lax.axis_size(axis)
        forward = [(i, i + 1) for i in range(count - 1)]
        backward = [(target, source) for source, target in forward]
        low = lax.ppermute(
            lax.slice_in_dim(block, block.shape[dim] - width, None, axis=dim), axis, forward
        )
        high = lax.ppermute(lax.slice_in_dim(block, 0, width, axis=dim), axis, backward)
        block = jnp.concatenate([low, block, high], axis=dim)
    return block


def to_cells(vox, chans):
    count = vox.shape[0]
    parts = vox.reshape(count, 2, 2, 2, 2, 2, 2, chans).transpose(0, 1, 3, 5, 2, 4, 6, 7)
    return parts.reshape(count, 8, 8 * chans)


def from_cells(cells, chans):
    count = cells.shape[0]
    parts = cells.reshape(count, 2, 2, 2, 2, 2, 2, chans).transpose(0, 1, 4, 2, 5, 3, 6, 7)
    return parts.reshape(count, 64, chans)


def coarse_mix(vox, weight):
    chans = weight.shape[1]
    padded = jnp.pad(vox, ((0, 0), (1, 1), (1, 1), (1, 1), (0, 0)))
    total = jnp.zeros((vox.shape[0] * 64, chans), jnp.float32)
    for dz in range(3):
        for dy in range(3):
            for dx in range(3):
                piece = padded[:, dz : dz + 4, dy : dy + 4, dx : dx + 4].reshape(-1, chans)
                total = total + jnp.dot(
                    piece, weight[(dz * 3 + dy) * 3 + dx], preferred_element_type=jnp.float32
                )
    return total


def select_rows(index, count, values):
    columns = jnp.arange(count, dtype=jnp.int32)
    picker = (index[:, None] == columns[None, :]).astype(jnp.bfloat16)
    return jnp.dot(picker, values, preferred_element_type=jnp.float32).astype(jnp.bfloat16)


def fine_conv(field, table, weight):
    bricks = field.shape[0]
    chans = weight.shape[1]
    boundary = bricks // 4
    face = field[:boundary][None, None]
    cycle = padded_2(face, (("gz", 0), ("gx", 1)), 1)
    empty_row = jnp.zeros((1, field.shape[1]), jnp.bfloat16)
    extended = jnp.concatenate(
        [field, cycle.reshape(9 * boundary, field.shape[1]), empty_row], axis=0
    )
    zero_index = bricks + 9 * boundary
    safe = jnp.where(table < 0, zero_index, table)
    tables = safe.reshape(9, 3, bricks)
    weights = weight.reshape(9, 3, chans, chans)

    def step(total, pair):
        rows, group = pair
        picked = jnp.take(extended, rows.reshape(-1), axis=0)
        picked = picked.reshape(3, bricks * 64, chans)
        return (
            total + jnp.einsum("kvc,kcd->vd", picked, group, preferred_element_type=jnp.float32),
            None,
        )

    start = jnp.zeros((bricks * 64, chans), jnp.float32)
    total, unused = lax.scan(step, start, (tables, weights))
    return total.reshape(bricks, 64 * chans)


def relay_out(buffer, layers, slabs):
    width = buffer.shape[1]
    moved = lax.all_to_all(
        buffer.reshape(layers * slabs, -1, width),
        ("gz", "gx"),
        split_axis=0,
        concat_axis=0,
        tiled=True,
    )
    return moved.reshape(-1, width)


def relay_back(buffer, layers, slabs):
    width = buffer.shape[1]
    moved = lax.all_to_all(
        buffer.reshape(layers * slabs, -1, width),
        ("gz", "gx"),
        split_axis=0,
        concat_axis=0,
        tiled=True,
    )
    return moved.reshape(-1, width)


def on_device(
    features, active_count, neighbors, owner, arrival_cell, w_enc, w_down, w_mid, w_up, w_dec
):
    layers = lax.axis_size("gz")
    slabs = lax.axis_size("gx")
    devices = layers * slabs
    bricks = features.shape[1]
    chans = w_enc.shape[1]
    capacity = arrival_cell.shape[1] // devices
    slot_count = devices * capacity
    blank = jnp.zeros((), jnp.bfloat16)
    live = (jnp.arange(bricks, dtype=jnp.int32) < active_count[0, 0])[:, None]
    x0 = jnp.where(live, features[0], blank)
    conv_one = fine_conv(x0, neighbors[0], w_enc)
    encoded = jnp.where(live, x0.astype(jnp.float32) + jax.nn.relu(conv_one), 0.0).astype(
        jnp.bfloat16
    )
    cells = to_cells(encoded.reshape(bricks, 64, chans), chans)
    pooled = jnp.dot(cells.reshape(-1, 8 * chans), w_down, preferred_element_type=jnp.float32)
    pooled = jnp.where(live, pooled.reshape(bricks, 8 * chans), 0.0).astype(jnp.bfloat16)
    target = owner[0]
    later = (
        jnp.arange(bricks, dtype=jnp.int32)[None, :] < jnp.arange(bricks, dtype=jnp.int32)[:, None]
    )
    same = target[:, None] == target[None, :]
    rank = jnp.sum(jnp.logical_and(same, later).astype(jnp.int32), axis=1)
    outgoing_slot = target * capacity + rank
    slot_ids = jnp.arange(slot_count, dtype=jnp.int32)
    scatter_table = (slot_ids[:, None] == outgoing_slot[None, :]).astype(jnp.bfloat16)
    outgoing = jnp.dot(scatter_table, pooled, preferred_element_type=jnp.float32).astype(
        jnp.bfloat16
    )
    incoming = relay_out(outgoing, layers, slabs)
    arrivals = arrival_cell[0]
    cell_ids = jnp.arange(bricks, dtype=jnp.int32)
    landing_table = (cell_ids[:, None] == arrivals[None, :]).astype(jnp.bfloat16)
    coarse = jnp.dot(landing_table, incoming, preferred_element_type=jnp.float32).astype(
        jnp.bfloat16
    )
    coarse_bricks = bricks // 8
    vox = from_cells(coarse.reshape(coarse_bricks, 8, 8 * chans), chans).reshape(
        coarse_bricks, 4, 4, 4, chans
    )
    mixed = coarse_mix(vox, w_mid).reshape(coarse_bricks, 4, 4, 4, chans)
    middle = (vox.astype(jnp.float32) + jax.nn.relu(mixed)).astype(jnp.bfloat16)
    middle_cells = to_cells(middle.reshape(coarse_bricks, 64, chans), chans).reshape(
        bricks, 8 * chans
    )
    reply = select_rows(arrivals, bricks, middle_cells)
    returned = relay_back(reply, layers, slabs)
    back = select_rows(outgoing_slot, slot_count, returned)
    lifted = jnp.dot(back.reshape(bricks * 8, chans), w_up, preferred_element_type=jnp.float32)
    lifted = from_cells(lifted.reshape(bricks, 8, 8 * chans), chans).reshape(bricks, 64 * chans)
    restored = jnp.where(live, encoded.astype(jnp.float32) + lifted, 0.0).astype(jnp.bfloat16)
    conv_two = fine_conv(restored, neighbors[0], w_dec)
    decoded = jnp.where(live, restored.astype(jnp.float32) + jax.nn.relu(conv_two), 0.0).astype(
        jnp.bfloat16
    )
    return decoded[None]


def solution(mesh):
    placed = (
        P("gz", "gx", None),
        P("gz", "gx"),
        P("gz", None, "gx"),
        P("gz", "gx"),
        P("gz", "gx"),
        P(),
        P(),
        P(),
        P(),
        P(),
    )
    return jax.shard_map(
        on_device, mesh=mesh, in_specs=placed, out_specs=P("gz", "gx", None), check_vma=False
    )
```

profile of v0, /device:TPU:40, one launch (start us, length us, event | category | flops | bytes accessed | tf_op | source)
XLA Modules:
  0.0 1249.6 jit_solution(1064163392058361258)
XLA Ops:
  67.9 477.2 %while.22 = (s32[]{:T(128)}, f32[12288,96]{0,1:T(8,128)}, s32[9,3,192]{2,1,0:T(4,128)S(1)}, bf16[625,6144]{1,0:T(8,128)(2,1)}, bf16[9,3,96,96]{2,3,1,0:T(8,128)(2,1)S(1)}, /*index=5*/s32[]{:T(128)}, s32[]{:T(128)}) while((s32[]{:T(128)}, f32[12288,96]{0,1:T(8,128)}, s32[9,3,192]{2,1,0:T(4,128)S(1)}, bf16[625,6144]{1,0:T(8,128)(2,1)}, ...), condition=%wide.region_1.3_spmd.clone, body=%wide.region_0.2_spmd.clone.sunk | while | flops 685381696 | bytes 59082212 | solution.py:77
  68.2 20.6 %gather_fusion = bf16[576,6144]{1,0:T(8,128)(2,1)} fusion(bf16[625,6144]{1,0:T(8,128)(2,1)} %get-tuple-element.225, s32[1024]{0:T(1024)S(1)} %pad_clamp_fusion.4), kind=kCustom, calls=%fused_computation.clone.clone.1 | custom fusion | bytes 14158080 | tf_op jit(solution)/shard_map/while/body/eval_jaxpr/jit(_take)/gather | solution.py:69
  120.0 20.6 %gather_fusion = bf16[576,6144]{1,0:T(8,128)(2,1)} fusion(bf16[625,6144]{1,0:T(8,128)(2,1)} %get-tuple-element.225, s32[1024]{0:T(1024)S(1)} %pad_clamp_fusion.4), kind=kCustom, calls=%fused_computation.clone.clone.1 | custom fusion | bytes 14158080 | tf_op jit(solution)/shard_map/while/body/eval_jaxpr/jit(_take)/gather | solution.py:69
  147.2 15.7 %reshape.305 = bf16[3,12288,96]{2,1,0:T(8,128)(2,1)} reshape(bf16[576,6144]{1,0:T(8,128)(2,1)} %broadcast_select_fusion.5) | data formatting | bytes 14155776 | tf_op jit(solution)/shard_map/while/body/eval_jaxpr/reshape | solution.py:70
  173.1 20.6 %gather_fusion = bf16[576,6144]{1,0:T(8,128)(2,1)} fusion(bf16[625,6144]{1,0:T(8,128)(2,1)} %get-tuple-element.225, s32[1024]{0:T(1024)S(1)} %pad_clamp_fusion.4), kind=kCustom, calls=%fused_computation.clone.clone.1 | custom fusion | bytes 14158080 | tf_op jit(solution)/shard_map/while/body/eval_jaxpr/jit(_take)/gather | solution.py:69
  200.3 15.7 %reshape.305 = bf16[3,12288,96]{2,1,0:T(8,128)(2,1)} reshape(bf16[576,6144]{1,0:T(8,128)(2,1)} %broadcast_select_fusion.5) | data formatting | bytes 14155776 | tf_op jit(solution)/shard_map/while/body/eval_jaxpr/reshape | solution.py:70
  226.3 20.6 %gather_fusion = bf16[576,6144]{1,0:T(8,128)(2,1)} fusion(bf16[625,6144]{1,0:T(8,128)(2,1)} %get-tuple-element.225, s32[1024]{0:T(1024)S(1)} %pad_clamp_fusion.4), kind=kCustom, calls=%fused_computation.clone.clone.1 | custom fusion | bytes 14158080 | tf_op jit(solution)/shard_map/while/body/eval_jaxpr/jit(_take)/gather | solution.py:69
  253.5 15.7 %reshape.305 = bf16[3,12288,96]{2,1,0:T(8,128)(2,1)} reshape(bf16[576,6144]{1,0:T(8,128)(2,1)} %broadcast_select_fusion.5) | data formatting | bytes 14155776 | tf_op jit(solution)/shard_map/while/body/eval_jaxpr/reshape | solution.py:70
  279.4 20.6 %gather_fusion = bf16[576,6144]{1,0:T(8,128)(2,1)} fusion(bf16[625,6144]{1,0:T(8,128)(2,1)} %get-tuple-element.225, s32[1024]{0:T(1024)S(1)} %pad_clamp_fusion.4), kind=kCustom, calls=%fused_computation.clone.clone.1 | custom fusion | bytes 14158080 | tf_op jit(solution)/shard_map/while/body/eval_jaxpr/jit(_take)/gather | solution.py:69
  306.6 15.7 %reshape.305 = bf16[3,12288,96]{2,1,0:T(8,128)(2,1)} reshape(bf16[576,6144]{1,0:T(8,128)(2,1)} %broadcast_select_fusion.5) | data formatting | bytes 14155776 | tf_op jit(solution)/shard_map/while/body/eval_jaxpr/reshape | solution.py:70
  332.6 20.6 %gather_fusion = bf16[576,6144]{1,0:T(8,128)(2,1)} fusion(bf16[625,6144]{1,0:T(8,128)(2,1)} %get-tuple-element.225, s32[1024]{0:T(1024)S(1)} %pad_clamp_fusion.4), kind=kCustom, calls=%fused_computation.clone.clone.1 | custom fusion | bytes 14158080 | tf_op jit(solution)/shard_map/while/body/eval_jaxpr/jit(_take)/gather | solution.py:69
  385.8 20.6 %gather_fusion = bf16[576,6144]{1,0:T(8,128)(2,1)} fusion(bf16[625,6144]{1,0:T(8,128)(2,1)} %get-tuple-element.225, s32[1024]{0:T(1024)S(1)} %pad_clamp_fusion.4), kind=kCustom, calls=%fused_computation.clone.clone.1 | custom fusion | bytes 14158080 | tf_op jit(solution)/shard_map/while/body/eval_jaxpr/jit(_take)/gather | solution.py:69
  438.9 20.6 %gather_fusion = bf16[576,6144]{1,0:T(8,128)(2,1)} fusion(bf16[625,6144]{1,0:T(8,128)(2,1)} %get-tuple-element.225, s32[1024]{0:T(1024)S(1)} %pad_clamp_fusion.4), kind=kCustom, calls=%fused_computation.clone.clone.1 | custom fusion | bytes 14158080 | tf_op jit(solution)/shard_map/while/body/eval_jaxpr/jit(_take)/gather | solution.py:69
  466.1 15.7 %reshape.305 = bf16[3,12288,96]{2,1,0:T(8,128)(2,1)} reshape(bf16[576,6144]{1,0:T(8,128)(2,1)} %broadcast_select_fusion.5) | data formatting | bytes 14155776 | tf_op jit(solution)/shard_map/while/body/eval_jaxpr/reshape | solution.py:70
  492.1 20.6 %gather_fusion = bf16[576,6144]{1,0:T(8,128)(2,1)} fusion(bf16[625,6144]{1,0:T(8,128)(2,1)} %get-tuple-element.225, s32[1024]{0:T(1024)S(1)} %pad_clamp_fusion.4), kind=kCustom, calls=%fused_computation.clone.clone.1 | custom fusion | bytes 14158080 | tf_op jit(solution)/shard_map/while/body/eval_jaxpr/jit(_take)/gather | solution.py:69
  519.2 15.7 %reshape.305 = bf16[3,12288,96]{2,1,0:T(8,128)(2,1)} reshape(bf16[576,6144]{1,0:T(8,128)(2,1)} %broadcast_select_fusion.5) | data formatting | bytes 14155776 | tf_op jit(solution)/shard_map/while/body/eval_jaxpr/reshape | solution.py:70
  742.7 479.4 %while.23 = (s32[]{:T(128)}, f32[12288,96]{0,1:T(8,128)}, s32[9,3,192]{2,1,0:T(4,128)S(1)}, bf16[625,6144]{1,0:T(8,128)(2,1)}, bf16[9,3,96,96]{2,3,1,0:T(8,128)(2,1)S(1)}, /*index=5*/s32[]{:T(128)}, s32[]{:T(128)}) while((s32[]{:T(128)}, f32[12288,96]{0,1:T(8,128)}, s32[9,3,192]{2,1,0:T(4,128)S(1)}, bf16[625,6144]{1,0:T(8,128)(2,1)}, ...), condition=%wide.region_4.6_spmd.clone, body=%wide.region_3.5_spmd.clone.sunk | while | flops 685381696 | bytes 59082212 | solution.py:77
  743.0 20.6 %gather_fusion.1 = bf16[576,6144]{1,0:T(8,128)(2,1)} fusion(bf16[625,6144]{1,0:T(8,128)(2,1)} %get-tuple-element.246, s32[1024]{0:T(1024)S(1)} %pad_clamp_fusion.5), kind=kCustom, calls=%fused_computation.1.clone.clone.1 | custom fusion | bytes 14158080 | tf_op jit(solution)/shard_map/while/body/eval_jaxpr/jit(_take)/gather | solution.py:69
  770.2 15.7 %reshape.309 = bf16[3,12288,96]{2,1,0:T(8,128)(2,1)} reshape(bf16[576,6144]{1,0:T(8,128)(2,1)} %broadcast_select_fusion.6) | data formatting | bytes 14155776 | tf_op jit(solution)/shard_map/while/body/eval_jaxpr/reshape | solution.py:70
  794.9 20.6 %gather_fusion.1 = bf16[576,6144]{1,0:T(8,128)(2,1)} fusion(bf16[625,6144]{1,0:T(8,128)(2,1)} %get-tuple-element.246, s32[1024]{0:T(1024)S(1)} %pad_clamp_fusion.5), kind=kCustom, calls=%fused_computation.1.clone.clone.1 | custom fusion | bytes 14158080 | tf_op jit(solution)/shard_map/while/body/eval_jaxpr/jit(_take)/gather | solution.py:69
  822.1 15.7 %reshape.309 = bf16[3,12288,96]{2,1,0:T(8,128)(2,1)} reshape(bf16[576,6144]{1,0:T(8,128)(2,1)} %broadcast_select_fusion.6) | data formatting | bytes 14155776 | tf_op jit(solution)/shard_map/while/body/eval_jaxpr/reshape | solution.py:70
  848.3 20.6 %gather_fusion.1 = bf16[576,6144]{1,0:T(8,128)(2,1)} fusion(bf16[625,6144]{1,0:T(8,128)(2,1)} %get-tuple-element.246, s32[1024]{0:T(1024)S(1)} %pad_clamp_fusion.5), kind=kCustom, calls=%fused_computation.1.clone.clone.1 | custom fusion | bytes 14158080 | tf_op jit(solution)/shard_map/while/body/eval_jaxpr/jit(_take)/gather | solution.py:69
  875.5 15.7 %reshape.309 = bf16[3,12288,96]{2,1,0:T(8,128)(2,1)} reshape(bf16[576,6144]{1,0:T(8,128)(2,1)} %broadcast_select_fusion.6) | data formatting | bytes 14155776 | tf_op jit(solution)/shard_map/while/body/eval_jaxpr/reshape | solution.py:70
  901.8 20.6 %gather_fusion.1 = bf16[576,6144]{1,0:T(8,128)(2,1)} fusion(bf16[625,6144]{1,0:T(8,128)(2,1)} %get-tuple-element.246, s32[1024]{0:T(1024)S(1)} %pad_clamp_fusion.5), kind=kCustom, calls=%fused_computation.1.clone.clone.1 | custom fusion | bytes 14158080 | tf_op jit(solution)/shard_map/while/body/eval_jaxpr/jit(_take)/gather | solution.py:69
  955.2 20.6 %gather_fusion.1 = bf16[576,6144]{1,0:T(8,128)(2,1)} fusion(bf16[625,6144]{1,0:T(8,128)(2,1)} %get-tuple-element.246, s32[1024]{0:T(1024)S(1)} %pad_clamp_fusion.5), kind=kCustom, calls=%fused_computation.1.clone.clone.1 | custom fusion | bytes 14158080 | tf_op jit(solution)/shard_map/while/body/eval_jaxpr/jit(_take)/gather | solution.py:69
  982.3 15.7 %reshape.309 = bf16[3,12288,96]{2,1,0:T(8,128)(2,1)} reshape(bf16[576,6144]{1,0:T(8,128)(2,1)} %broadcast_select_fusion.6) | data formatting | bytes 14155776 | tf_op jit(solution)/shard_map/while/body/eval_jaxpr/reshape | solution.py:70
  1008.6 20.6 %gather_fusion.1 = bf16[576,6144]{1,0:T(8,128)(2,1)} fusion(bf16[625,6144]{1,0:T(8,128)(2,1)} %get-tuple-element.246, s32[1024]{0:T(1024)S(1)} %pad_clamp_fusion.5), kind=kCustom, calls=%fused_computation.1.clone.clone.1 | custom fusion | bytes 14158080 | tf_op jit(solution)/shard_map/while/body/eval_jaxpr/jit(_take)/gather | solution.py:69
  1035.7 15.7 %reshape.309 = bf16[3,12288,96]{2,1,0:T(8,128)(2,1)} reshape(bf16[576,6144]{1,0:T(8,128)(2,1)} %broadcast_select_fusion.6) | data formatting | bytes 14155776 | tf_op jit(solution)/shard_map/while/body/eval_jaxpr/reshape | solution.py:70
  1062.0 20.6 %gather_fusion.1 = bf16[576,6144]{1,0:T(8,128)(2,1)} fusion(bf16[625,6144]{1,0:T(8,128)(2,1)} %get-tuple-element.246, s32[1024]{0:T(1024)S(1)} %pad_clamp_fusion.5), kind=kCustom, calls=%fused_computation.1.clone.clone.1 | custom fusion | bytes 14158080 | tf_op jit(solution)/shard_map/while/body/eval_jaxpr/jit(_take)/gather | solution.py:69
  1115.4 20.6 %gather_fusion.1 = bf16[576,6144]{1,0:T(8,128)(2,1)} fusion(bf16[625,6144]{1,0:T(8,128)(2,1)} %get-tuple-element.246, s32[1024]{0:T(1024)S(1)} %pad_clamp_fusion.5), kind=kCustom, calls=%fused_computation.1.clone.clone.1 | custom fusion | bytes 14158080 | tf_op jit(solution)/shard_map/while/body/eval_jaxpr/jit(_take)/gather | solution.py:69
  1142.6 15.7 %reshape.309 = bf16[3,12288,96]{2,1,0:T(8,128)(2,1)} reshape(bf16[576,6144]{1,0:T(8,128)(2,1)} %broadcast_select_fusion.6) | data formatting | bytes 14155776 | tf_op jit(solution)/shard_map/while/body/eval_jaxpr/reshape | solution.py:70
  1168.8 20.6 %gather_fusion.1 = bf16[576,6144]{1,0:T(8,128)(2,1)} fusion(bf16[625,6144]{1,0:T(8,128)(2,1)} %get-tuple-element.246, s32[1024]{0:T(1024)S(1)} %pad_clamp_fusion.5), kind=kCustom, calls=%fused_computation.1.clone.clone.1 | custom fusion | bytes 14158080 | tf_op jit(solution)/shard_map/while/body/eval_jaxpr/jit(_take)/gather | solution.py:69
  (321 shorter events, 688.9 us)
Async XLA Ops:
  0.0 577.1 %copy-start = (bf16[768,96]{0,1:T(8,128)(2,1)S(1)}, bf16[768,96]{0,1:T(8,128)(2,1)}, u32[]{:S(2)}) copy-start(bf16[768,96]{0,1:T(8,128)(2,1)} %param.22) | copy-start | bytes 442372
  0.7 23.9 %copy-start.23 = (pred[192]{0:T(512)(128)(4,1)}, pred[192]{0:T(512)(128)(4,1)S(1)}, u32[]{:S(2)}) copy-start(pred[192]{0:T(512)(128)(4,1)S(1)} %iota_compare_fusion.9) | copy-start | bytes 580
  0.7 28.8 %copy-start.3 = (bf16[1,192,6144]{2,1,0:T(8,128)(2,1)S(1)}, bf16[1,192,6144]{2,1,0:T(8,128)(2,1)}, u32[]{:S(2)}) copy-start(bf16[1,192,6144]{2,1,0:T(8,128)(2,1)} %param.16) | copy-start | bytes 7077892
  4.2 29.5 %copy-start.16 = (s32[1,27,192]{2,0,1:T(1,128)S(1)}, s32[1,27,192]{2,0,1:T(1,128)}, u32[]{:S(2)}) copy-start(s32[1,27,192]{2,0,1:T(1,128)} %param.18) | copy-start | bytes 62212
  4.2 31.1 %copy-start.19 = (s32[1,192]{1,0:T(1,128)S(1)}, s32[1,192]{1,0:T(1,128)}, u32[]{:S(2)}) copy-start(s32[1,192]{1,0:T(1,128)} %param.19) | copy-start | bytes 2308
  4.2 17.1 %collective-permute-start.1 = (bf16[1,1,48,6144]{3,2,1,0:T(8,128)(2,1)S(1)}, bf16[1,1,48,6144]{3,2,1,0:T(8,128)(2,1)S(1)}, u32[]{:S(2)}, u32[]{:S(2)}) collective-permute-start(bf16[1,1,48,6144]{3,2,1,0:T(8,128)(2,1)S(1)} %slice_bitcast_fusion.1), channel_id=1, source_target_pairs={{32,0},{64,32},{96,64},{33,1},{65,33},{97,65},{34,2},{66,34},{98,6... | collective-permute-start | bytes 1769480 | tf_op jit(solution)/shard_map/ppermute | solution.py:15
  6.3 16.9 %collective-permute-start = (bf16[1,1,48,6144]{3,2,1,0:T(8,128)(2,1)S(1)}, bf16[1,1,48,6144]{3,2,1,0:T(8,128)(2,1)S(1)}, u32[]{:S(2)}, u32[]{:S(2)}) collective-permute-start(bf16[1,1,48,6144]{3,2,1,0:T(8,128)(2,1)S(1)} %slice_bitcast_fusion.1), channel_id=1, source_target_pairs={{0,32},{32,64},{64,96},{1,33},{33,65},{65,97},{2,34},{34,66},{66,9... | collective-permute-start | bytes 1769480 | tf_op jit(solution)/shard_map/ppermute | solution.py:12
  24.6 23.3 %collective-permute-start.3 = (bf16[3,1,48,6144]{3,2,1,0:T(8,128)(2,1)}, bf16[3,1,48,6144]{3,2,1,0:T(8,128)(2,1)}, u32[]{:S(2)}, u32[]{:S(2)}) collective-permute-start(bf16[3,1,48,6144]{3,2,1,0:T(8,128)(2,1)} %pad_maximum_fusion.2), channel_id=1, source_target_pairs={{1,0},{2,1},{3,2},{4,3},{5,4},{6,5},{7,6},{8,7},{9,8},{10,9},{11,1... | collective-permute-start | bytes 5308424 | tf_op jit(solution)/shard_map/ppermute | solution.py:15
  27.6 26.3 %collective-permute-start.2 = (bf16[3,1,48,6144]{3,2,1,0:T(8,128)(2,1)}, bf16[3,1,48,6144]{3,2,1,0:T(8,128)(2,1)}, u32[]{:S(2)}, u32[]{:S(2)}) collective-permute-start(bf16[3,1,48,6144]{3,2,1,0:T(8,128)(2,1)} %pad_maximum_fusion.2), channel_id=1, source_target_pairs={{0,1},{1,2},{2,3},{3,4},{4,5},{5,6},{6,7},{7,8},{8,9},{9,10},{10,1... | collective-permute-start | bytes 5308424 | tf_op jit(solution)/shard_map/ppermute | solution.py:12
  35.3 24.1 %copy-start.17 = (bf16[625]{0:T(1024)(128)(2,1)}, bf16[625]{0:T(1024)(128)(2,1)S(1)}, u32[]{:S(2)}) copy-start(bf16[625]{0:T(1024)(128)(2,1)S(1)} %pad.18.clone) | copy-start | bytes 3754
  35.5 23.9 %copy-start.21 = (s32[192]{0:T(256)}, s32[192]{0:T(256)S(1)}, u32[]{:S(2)}) copy-start(s32[192]{0:T(256)S(1)} %convert_reduce_fusion) | copy-start | bytes 2308
  36.1 23.4 %copy-start.8 = (bf16[192,6144]{1,0:T(8,128)(2,1)S(1)}, bf16[192,6144]{1,0:T(8,128)(2,1)}, u32[]{:S(2)}) copy-start(bf16[192,6144]{1,0:T(8,128)(2,1)} %copy-done.7) | copy-start | bytes 7077892
  551.4 5.9 copy-start.6
  551.4 5.9 copy-start.24
  568.1 10.1 copy-start.27
  577.1 10.3 copy-start.26
  579.6 22.5 %all-to-all-start = ((bf16[128,3,768]{2,1,0:T(4,128)(2,1)}), bf16[128,3,768]{2,1,0:T(4,128)(2,1)S(1)}, u32[]{:S(2)}, u32[]{:S(2)}) async-start(bf16[128,3,768]{2,1,0:T(4,128)(2,1)} %reshape.228), calls=%async_computation | async-start | bytes 1572864 | tf_op jit(solution)/shard_map/all_to_all | solution.py:83
  620.6 10.1 copy-start.15
  620.6 10.3 copy-start.20
  620.6 10.3 copy-start.22
  624.3 21.1 %all-to-all-start.1 = ((bf16[128,3,768]{2,1,0:T(4,128)(2,1)}), bf16[128,3,768]{2,1,0:T(4,128)(2,1)S(1)}, u32[]{:S(2)}, u32[]{:S(2)}) async-start(bf16[128,3,768]{2,1,0:T(4,128)(2,1)} %reshape.257), calls=%async_computation.1 | async-start | bytes 1572864 | tf_op jit(solution)/shard_map/all_to_all | solution.py:95
  662.7 10.1 copy-start.4
  679.4 25.5 %copy-start.13 = (bf16[27,96,96]{2,1,0:T(8,128)(2,1)S(1)}, bf16[27,96,96]{2,1,0:T(8,128)(2,1)}, u32[]{:S(2)}) copy-start(bf16[27,96,96]{2,1,0:T(8,128)(2,1)} %param.25) | copy-start | bytes 1492996
  679.4 16.4 %collective-permute-start.5 = (bf16[1,1,48,6144]{3,2,1,0:T(8,128)(2,1)S(1)}, bf16[1,1,48,6144]{3,2,1,0:T(8,128)(2,1)S(1)}, u32[]{:S(2)}, u32[]{:S(2)}) collective-permute-start(bf16[1,1,48,6144]{3,2,1,0:T(8,128)(2,1)S(1)} %slice_bitcast_fusion), channel_id=1, source_target_pairs={{32,0},{64,32},{96,64},{33,1},{65,33},{97,65},{34,2},{66,34},{98,6... | collective-permute-start | bytes 1769480 | tf_op jit(solution)/shard_map/ppermute | solution.py:15
  682.6 15.9 %collective-permute-start.4 = (bf16[1,1,48,6144]{3,2,1,0:T(8,128)(2,1)S(1)}, bf16[1,1,48,6144]{3,2,1,0:T(8,128)(2,1)S(1)}, u32[]{:S(2)}, u32[]{:S(2)}) collective-permute-start(bf16[1,1,48,6144]{3,2,1,0:T(8,128)(2,1)S(1)} %slice_bitcast_fusion), channel_id=1, source_target_pairs={{0,32},{32,64},{64,96},{1,33},{33,65},{65,97},{2,34},{34,66},{66,9... | collective-permute-start | bytes 1769480 | tf_op jit(solution)/shard_map/ppermute | solution.py:12
  700.0 23.3 %collective-permute-start.7 = (bf16[3,1,48,6144]{3,2,1,0:T(8,128)(2,1)}, bf16[3,1,48,6144]{3,2,1,0:T(8,128)(2,1)}, u32[]{:S(2)}, u32[]{:S(2)}) collective-permute-start(bf16[3,1,48,6144]{3,2,1,0:T(8,128)(2,1)} %pad_maximum_fusion.3), channel_id=1, source_target_pairs={{1,0},{2,1},{3,2},{4,3},{5,4},{6,5},{7,6},{8,7},{9,8},{10,9},{11,1... | collective-permute-start | bytes 5308424 | tf_op jit(solution)/shard_map/ppermute | solution.py:15
  702.9 26.3 %collective-permute-start.6 = (bf16[3,1,48,6144]{3,2,1,0:T(8,128)(2,1)}, bf16[3,1,48,6144]{3,2,1,0:T(8,128)(2,1)}, u32[]{:S(2)}, u32[]{:S(2)}) collective-permute-start(bf16[3,1,48,6144]{3,2,1,0:T(8,128)(2,1)} %pad_maximum_fusion.3), channel_id=1, source_target_pairs={{0,1},{1,2},{2,3},{3,4},{4,5},{5,6},{6,7},{7,8},{8,9},{9,10},{10,1... | collective-permute-start | bytes 5308424 | tf_op jit(solution)/shard_map/ppermute | solution.py:12
  722.9 11.4 copy-start.10
  722.9 11.4 copy-start.18
  1233.1 7.8 copy-start.5
  1233.1 7.8 copy-start.25
  1241.0 8.4 copy-start.1
  (6 other events, 11.1 us)
where the time goes:
time: 1260 us; the launch traced here: 1250 us
  local copies, waits for them, and re-layouts  762 us (60%)
  matrix products  198 us (16%)
  other arithmetic  180 us (14%)
  waiting for transfers between devices  71.8 us (6%)
  starting transfers between devices  35.8 us (3%)
    gather x18, local copies, waits for them, and re-layouts, step(): picked = jnp.take(extended, rows.reshape(-1), axis=0)  371 us
    reshape x18, local copies, waits for them, and re-layouts, step(): picked = picked.reshape(3, bricks * 64, chans)  282 us
    dot_general x18, matrix products, step(): jnp.einsum('kvc,kcd->vd', picked, group, preferred_element_type=jnp.float32)  184 us
    select_n x36, other arithmetic, step(): picked = jnp.take(extended, rows.reshape(-1), axis=0)  118 us
    ppermute x4, waiting for transfers between devices, padded_2(): lax.ppermute(lax.slice_in_dim(block, 0, width, axis=dim), axis, backward)  33.9 us
  transfers between devices with their start and end apart: 10, of which 10 were waited for; matrix products, arithmetic and copies ran while one was open for 3% of the time, Pallas kernels for 0%

commit v1 on v0

--- a/solution.py
+++ b/solution.py
@@ -1,7 +1,107 @@
+import functools
+
 import jax
 import jax.numpy as jnp
 from jax import lax
+from jax.experimental import pallas as pl
+from jax.experimental.pallas import tpu as pltpu
 from jax.sharding import PartitionSpec as P
+
+
+ORDER = [[(q - i) % 4 for q in range(4)] for i in range(4)]
+CUT = (96, 64, 32)
+
+def conv_kernel(nb, chunks, staged, table, count, w_ref, own_hbm, halo_hbm, out_ref, rot, gbuf, sem):
+    step = pl.program_id(0)
+    bricks = own_hbm.shape[0]
+    total = bricks + halo_hbm.shape[0]
+    lane = lax.broadcasted_iota(jnp.int32, (16, 128), 1)
+
+    @pl.when(step == 0)
+    def _():
+        a = pltpu.make_async_copy(own_hbm, rot.at[0, pl.ds(0, bricks)], sem.at[0])
+        b = pltpu.make_async_copy(halo_hbm, rot.at[0, pl.ds(bricks, total - bricks)], sem.at[1])
+        a.start(); b.start();
+        for j in range(4):
+            rot[j, total] = jnp.zeros((3, 16, 128), jnp.bfloat16)
+        a.wait(); b.wait()
+        def rotate(n, c):
+            tiles = [rot[0, n, t] for t in range(3)]
+            for j in range(1, 4):
+                amount = (96 * j) % 128
+                rolled = [pltpu.roll(x.astype(jnp.float32), amount, 1).astype(jnp.bfloat16) for x in tiles]
+                for u in range(3):
+                    hi = (128 * u + 127 - 96 * j) // 128 % 3
+                    lo = (128 * u - 96 * j) // 128 % 3
+                    edge = amount
+                    rot[j, n, u] = jnp.where(lane >= edge, rolled[hi], rolled[lo])
+            return c
+        lax.fori_loop(0, total, rotate, 0, unroll=8)
+
+    def gather(c, b):
+        base = (step * nb + b) * 28
+        lanes = [[] for _ in range(4)]
+        for g in chunks[c]:
+            loads = [[rot[j, table[base + 4 * g + j], t] for t in range(3)] for j in range(4)]
+            for i in range(4):
+                for u in range(3):
+                    lanes[i].append(jnp.where(lane < CUT[u], loads[ORDER[i][u]][u], loads[ORDER[i][u + 1]][u]))
+        return lanes
+
+    acc = [None] * 4
+    for c in range(len(chunks)):
+        got = [gather(c, b) for b in range(nb)]
+        for i in range(4):
+            if staged:
+                for b in range(nb):
+                    for u, x in enumerate(got[b][i]):
+                        gbuf[c % 2, i, b * 16:(b + 1) * 16, u * 128:(u + 1) * 128] = x
+                lhs = gbuf[c % 2, i, :, :128 * 3 * len(chunks[c])]
+            else:
+                lhs = jnp.concatenate([jnp.concatenate(got[b][i], axis=1) for b in range(nb)], axis=0)
+            pieces = []
+            for g in chunks[c]:
+                for q in range(4):
+                    k = 4 * g + ORDER[i][q]
+                    pieces.append(w_ref[k] if k < 27 else jnp.zeros((96, 128), jnp.bfloat16))
+            rhs = jnp.concatenate(pieces, axis=0)
+            part = jnp.dot(lhs, rhs, preferred_element_type=jnp.float32)
+            acc[i] = part if acc[i] is None else acc[i] + part
+    r1 = pltpu.roll(acc[1], 96, 1)
+    r2 = pltpu.roll(acc[2], 64, 1)
+    r3 = pltpu.roll(acc[3], 32, 1)
+    rows = lax.broadcasted_iota(jnp.int32, (nb * 16, 128), 0) // 16 + step * nb
+    lanes = lax.broadcasted_iota(jnp.int32, (nb * 16, 128), 1)
+    live = rows < count[0]
+    tiles = (jnp.where(lanes < 96, acc[0], r1), jnp.where(lanes < 64, r1, r2), jnp.where(lanes < 32, r2, r3))
+    for u in range(3):
+        own = rot[0, pl.ds(step * nb, nb), u].reshape(nb * 16, 128).astype(jnp.float32)
+        val = jnp.where(live, own + jnp.maximum(tiles[u], 0.0), 0.0).astype(jnp.bfloat16)
+        out_ref[:, u] = val.reshape(nb, 16, 128)
+
+def conv(table, count, w, own, halo, nb=16, chunks=((0,1),(2,3),(4,5),(6,)), staged=False):
+    bricks = own.shape[0]
+    total = bricks + halo.shape[0]
+    kc = max(len(c) for c in chunks) * 384
+    return pl.pallas_call(
+        functools.partial(conv_kernel, nb, chunks, staged),
+        grid=(bricks // nb,),
+        out_shape=jax.ShapeDtypeStruct((bricks, 3, 16, 128), jnp.bfloat16),
+        in_specs=[pl.BlockSpec(memory_space=pltpu.SMEM), pl.BlockSpec(memory_space=pltpu.SMEM),
+                  pl.BlockSpec((27, 96, 128), lambda s: (0, 0, 0)),
+                  pl.BlockSpec(memory_space=pl.ANY), pl.BlockSpec(memory_space=pl.ANY)],
+        out_specs=pl.BlockSpec((nb, 3, 16, 128), lambda s: (s, 0, 0, 0)),
+        scratch_shapes=[pltpu.VMEM((4, total + 1, 3, 16, 128), jnp.bfloat16),
+                        pltpu.VMEM((2, 4, nb * 16, kc), jnp.bfloat16) if staged else pltpu.VMEM((8, 128), jnp.float32),
+                        pltpu.SemaphoreType.DMA((2,))],
+        compiler_params=pltpu.CompilerParams(vmem_limit_bytes=56 * 1024 * 1024),
+        name="conv",
+    )(table, count, w, own, halo)
+
+def dense(x):
+    return x.reshape(x.shape[0], 16, 3, 128).transpose(0, 2, 1, 3)
+def undense(x):
+    return x.transpose(0, 2, 1, 3).reshape(x.shape[0], 6144)
 
 
 def padded_2(block, sides, width):
@@ -49,33 +149,11 @@
     return jnp.dot(picker, values, preferred_element_type=jnp.float32).astype(jnp.bfloat16)
 
 
-def fine_conv(field, table, weight):
+def fine_conv(field, table, active, weight):
     bricks = field.shape[0]
-    chans = weight.shape[1]
     boundary = bricks // 4
-    face = field[:boundary][None, None]
-    cycle = padded_2(face, (("gz", 0), ("gx", 1)), 1)
-    empty_row = jnp.zeros((1, field.shape[1]), jnp.bfloat16)
-    extended = jnp.concatenate(
-        [field, cycle.reshape(9 * boundary, field.shape[1]), empty_row], axis=0
-    )
-    zero_index = bricks + 9 * boundary
-    safe = jnp.where(table < 0, zero_index, table)
-    tables = safe.reshape(9, 3, bricks)
-    weights = weight.reshape(9, 3, chans, chans)
-
-    def step(total, pair):
-        rows, group = pair
-        picked = jnp.take(extended, rows.reshape(-1), axis=0)
-        picked = picked.reshape(3, bricks * 64, chans)
-        return (
-            total + jnp.einsum("kvc,kcd->vd", picked, group, preferred_element_type=jnp.float32),
-            None,
-        )
-
-    start = jnp.zeros((bricks * 64, chans), jnp.float32)
-    total, unused = lax.scan(step, start, (tables, weights))
-    return total.reshape(bricks, 64 * chans)
+    cycle = padded_2(field[:boundary][None, None], (("gz", 0), ("gx", 1)), 1)
+    return conv(table, active, weight, field, cycle.reshape(9 * boundary, 3, 16, 128))
 
 
 def relay_out(buffer, layers, slabs):
@@ -115,10 +193,13 @@
     blank = jnp.zeros((), jnp.bfloat16)
     live = (jnp.arange(bricks, dtype=jnp.int32) < active_count[0, 0])[:, None]
     x0 = jnp.where(live, features[0], blank)
-    conv_one = fine_conv(x0, neighbors[0], w_enc)
-    encoded = jnp.where(live, x0.astype(jnp.float32) + jax.nn.relu(conv_one), 0.0).astype(
-        jnp.bfloat16
-    )
+    zero_index = bricks + 9 * (bricks // 4)
+    table = jnp.where(neighbors[0] < 0, zero_index, neighbors[0])
+    table = jnp.pad(table, ((0, 1), (0, 0)), constant_values=zero_index).T.reshape(-1)
+    active = active_count[0]
+    wide = ((0, 0), (0, 0), (0, 128 - chans))
+    encoded_dense = fine_conv(dense(x0), table, active, jnp.pad(w_enc, wide))
+    encoded = undense(encoded_dense)
     cells = to_cells(encoded.reshape(bricks, 64, chans), chans)
     pooled = jnp.dot(cells.reshape(-1, 8 * chans), w_down, preferred_element_type=jnp.float32)
     pooled = jnp.where(live, pooled.reshape(bricks, 8 * chans), 0.0).astype(jnp.bfloat16)
@@ -156,10 +237,7 @@
     lifted = jnp.dot(back.reshape(bricks * 8, chans), w_up, preferred_element_type=jnp.float32)
     lifted = from_cells(lifted.reshape(bricks, 8, 8 * chans), chans).reshape(bricks, 64 * chans)
     restored = jnp.where(live, encoded.astype(jnp.float32) + lifted, 0.0).astype(jnp.bfloat16)
-    conv_two = fine_conv(restored, neighbors[0], w_dec)
-    decoded = jnp.where(live, restored.astype(jnp.float32) + jax.nn.relu(conv_two), 0.0).astype(
-        jnp.bfloat16
-    )
+    decoded = undense(fine_conv(dense(restored), table, active, jnp.pad(w_dec, wide)))
     return decoded[None]
 
 

time: 1260 us -> 318 us (0.25)
  local copies, waits for them, and re-layouts: 762 us -> 62.3 us
  matrix products: 198 us -> 11.4 us
  other arithmetic: 180 us -> 14.8 us
  Pallas kernels: 0 us -> 86.4 us
  waiting for transfers between devices: 71.8 us -> 93.5 us
    gather x18 -> x0, local copies, waits for them, and re-layouts: 371 us -> none  [step(): picked = jnp.take(extended, rows.reshape(-1), axis=0)]
    reshape x36 -> x1, local copies, waits for them, and re-layouts: 283 us -> 0.72 us  [on_device(): jnp.pad(table, ((0, 1), (0, 0)), constant_values=zero_index).T.reshape(-1)]
    dot_general x18 -> x0, matrix products: 184 us -> none  [step(): jnp.einsum('kvc,kcd->vd', picked, group, preferred_element_type=jnp.float32)]
    select_n x38 -> x1, other arithmetic: 120 us -> 0.01 us  [on_device(): table = jnp.where(neighbors[0] < 0, zero_index, neighbors[0])]
    pallas_call x0 -> x2, Pallas kernels: none -> 86.4 us  [conv(): pl.pallas_call(functools.partial(conv_kernel, nb, chunks, staged), grid=(...]
    ppermute x4, waiting for transfers between devices: 16.4 us -> 55.1 us  [padded_2(): lax.ppermute(lax.slice_in_dim(block, block.shape[dim] - width, None, axis...]
    ppermute x4, waiting for transfers between devices: 33.9 us -> 9.08 us  [padded_2(): lax.ppermute(lax.slice_in_dim(block, 0, width, axis=dim), axis, backward)]
    max x3 -> x0, local copies, waits for them, and re-layouts: 23.2 us -> none  [the longest x2 15.4 us: on_device(): jax.nn.relu(conv_one)]
  transfers between devices with their start and end apart: 10 -> 10, of which waited for: 10 -> 10; matrix products, arithmetic and copies ran while one was open for 3% -> 1% of each run, Pallas kernels for 0% -> 0%
where the time goes in v1:
time: 318 us; the launch traced here: 314 us
  waiting for transfers between devices  93.5 us (29%)
  Pallas kernels  86.4 us (27%)
  local copies, waits for them, and re-layouts  62.3 us (20%)
  starting transfers between devices  44.4 us (14%)
  other arithmetic  14.8 us (5%)
  matrix products  11.4 us (4%)
    pallas_call x2, Pallas kernels, conv(): pl.pallas_call(functools.partial(conv_kernel, nb, chunks, staged), grid=(...  86.4 us
    ppermute x4, waiting for transfers between devices, padded_2(): lax.ppermute(lax.slice_in_dim(block, block.shape[dim] - width, None, axis...  55.1 us
    ppermute x4, starting transfers between devices, padded_2(): lax.ppermute(lax.slice_in_dim(block, 0, width, axis=dim), axis, backward)  17.5 us
    all_to_all x1, waiting for transfers between devices, relay_out(): lax.all_to_all(buffer.reshape(layers * slabs, -1, width), ('gz', 'gx'), s...  14.7 us
    all_to_all x1, waiting for transfers between devices, relay_back(): lax.all_to_all(buffer.reshape(layers * slabs, -1, width), ('gz', 'gx'), s...  14.6 us
    all_to_all x1, starting transfers between devices, relay_out(): lax.all_to_all(buffer.reshape(layers * slabs, -1, width), ('gz', 'gx'), s...  10.6 us
    ppermute x4, starting transfers between devices, padded_2(): lax.ppermute(lax.slice_in_dim(block, block.shape[dim] - width, None, axis...  9.84 us
    concatenate x4, other arithmetic, padded_2(): block = jnp.concatenate([low, block, high], axis=dim)  9.67 us
  transfers between devices with their start and end apart: 10, of which 10 were waited for; matrix products, arithmetic and copies ran while one was open for 1% of the time, Pallas kernels for 0%

profile of v1, /device:TPU:40, one launch (start us, length us, event | category | flops | bytes accessed | tf_op | source)
XLA Modules:
  0.0 314.2 jit_solution(10011105453146197786)
XLA Ops:
  0.7 6.1 %squeeze.100 = bf16[192,16,3,128]{3,2,1,0:T(4,128)(2,1)S(1)} reshape(bf16[1,192,6144]{2,1,0:T(8,128)(2,1)} %param.10) | data formatting | bytes 4718592 | tf_op jit(solution)/shard_map/squeeze | solution.py:195
  9.4 4.0 %collective-permute-start = (bf16[1,1,48,3,16,128]{5,4,3,2,1,0:T(8,128)(2,1)S(1)}, bf16[1,1,48,3,16,128]{5,4,3,2,1,0:T(8,128)(2,1)S(1)}, u32[]{:S(2)}, u32[]{:S(2)}) collective-permute-start(bf16[1,1,48,3,16,128]{5,4,3,2,1,0:T(8,128)(2,1)S(1)} %slice_bitcast_fusion.1), channel_id=1, source_target_pairs={{0,32},{32,64},{64,96},{1,33},{33,65},{65,97},{2,34},{34,66},{66,9... | collective-permute-start | bytes 1769480 | tf_op jit(solution)/shard_map/ppermute | solution.py:112
  13.3 2.0 collective-permute-start.1
  15.4 11.1 %collective-permute-done = bf16[1,1,48,3,16,128]{5,4,3,2,1,0:T(8,128)(2,1)S(1)} collective-permute-done((bf16[1,1,48,3,16,128]{5,4,3,2,1,0:T(8,128)(2,1)S(1)}, bf16[1,1,48,3,16,128]{5,4,3,2,1,0:T(8,128)(2,1)S(1)}, u32[]{:S(2)}, u32[]{:S(2)}) %collective-permute-start) | collective-permute-done | bytes 589856 | tf_op jit(solution)/shard_map/ppermute | solution.py:112
  26.5 3.6 %collective-permute-done.1 = bf16[1,1,48,3,16,128]{5,4,3,2,1,0:T(8,128)(2,1)S(1)} collective-permute-done((bf16[1,1,48,3,16,128]{5,4,3,2,1,0:T(8,128)(2,1)S(1)}, bf16[1,1,48,3,16,128]{5,4,3,2,1,0:T(8,128)(2,1)S(1)}, u32[]{:S(2)}, u32[]{:S(2)}) %collective-permute-start.1) | collective-permute-done | bytes 589856 | tf_op jit(solution)/shard_map/ppermute | solution.py:115
  31.4 1.9 collective-permute-start.2
  33.4 5.8 %collective-permute-start.3 = (bf16[3,1,48,3,16,128]{5,4,3,2,1,0:T(8,128)(2,1)}, bf16[3,1,48,3,16,128]{5,4,3,2,1,0:T(8,128)(2,1)}, u32[]{:S(2)}, u32[]{:S(2)}) collective-permute-start(bf16[3,1,48,3,16,128]{5,4,3,2,1,0:T(8,128)(2,1)} %pad_maximum_fusion.2), channel_id=1, source_target_pairs={{1,0},{2,1},{3,2},{4,3},{5,4},{6,5},{7,6},{8,7},{9,8},{10,9},{11,1... | collective-permute-start | bytes 5308424 | tf_op jit(solution)/shard_map/ppermute | solution.py:115
  41.2 16.5 %collective-permute-done.2 = bf16[3,1,48,3,16,128]{5,4,3,2,1,0:T(8,128)(2,1)} collective-permute-done((bf16[3,1,48,3,16,128]{5,4,3,2,1,0:T(8,128)(2,1)}, bf16[3,1,48,3,16,128]{5,4,3,2,1,0:T(8,128)(2,1)}, u32[]{:S(2)}, u32[]{:S(2)}) %collective-permute-start.2) | collective-permute-done | bytes 1769504 | tf_op jit(solution)/shard_map/ppermute | solution.py:112
  59.5 5.1 %pad_maximum_fusion = bf16[3,3,48,3,16,128]{5,4,3,2,1,0:T(8,128)(2,1)} fusion(bf16[3,1,48,3,16,128]{5,4,3,2,1,0:T(8,128)(2,1)} %collective-permute-done.3, bf16[1,1,48,3,16,128]{5,4,3,2,1,0:T(8,128)(2,1)S(1)} %collective-permute-done.1, bf16[1,1,48,3,16,128]{5,4,3,2,1,0:T(8,128)(2,1)S(1)} %slice_bitcast_fusion.1, ...), kind=kLoop, calls=%fused_computation.26 | loop fusion | flops 10616832 | bytes 10616832 | tf_op jit(solution)/shard_map/concatenate | solution.py:116
  64.6 43.2 %conv.2 = bf16[192,3,16,128]{3,2,1,0:T(8,128)(2,1)} custom-call(s32[5376]{0:T(1024)} %reshape.144.table, s32[1]{0:T(128)} %bitcast.185.count, bf16[27,96,128]{2,1,0:T(8,128)(2,1)} %pad.17.w_ref, bf16[192,3,16,128]{3,2,1,0:T(8,128)(2,1)} %copy-done.3, bf16[432,3,16,128]{3,2,1,0:T(8,128)(2,1)} %bitcast.190), custom_call_target="tpu_custom_call" | custom-call | tf_op jit(solution)/shard_map/conv/pallas_call | solution.py:86
  107.8 3.8 %copy.71 = bf16[192,16,3,128]{0,3,2,1:T(8,128)(2,1)S(1)} copy(bf16[192,16,3,128]{3,1,2,0:T(8,128)(2,1)} %bitcast.191) | data formatting | bytes 4718592 | tf_op jit(solution)/shard_map/transpose | solution.py:104
  111.6 7.4 %copy.72 = bf16[192,2,2,2,2,2,2,96]{7,6,5,4,3,2,1,0:T(2,128)(2,1)} copy(bf16[192,2,2,2,2,2,2,96]{0,7,6,3,5,2,4,1:T(8,128)(2,1)S(1)} %bitcast.192) | data formatting | bytes 4718592 | tf_op jit(solution)/shard_map/transpose | solution.py:122
  119.0 9.0 %reshape_reshape.17 = bf16[1536,768]{1,0:T(8,128)(2,1)S(1)} reshape(bf16[192,2,2,2,2,2,2,96]{7,6,5,4,3,2,1,0:T(2,128)(2,1)} %copy.72) | data formatting | bytes 4718592 | tf_op jit(solution)/shard_map/reshape;reshape | solution.py:204
  130.5 10.6 %all-to-all-start = ((bf16[128,3,768]{2,1,0:T(4,128)(2,1)}), bf16[128,3,768]{2,1,0:T(4,128)(2,1)S(1)}, u32[]{:S(2)}, u32[]{:S(2)}) async-start(bf16[128,3,768]{2,1,0:T(4,128)(2,1)} %reshape.147), calls=%async_computation | async-start | bytes 1572864 | tf_op jit(solution)/shard_map/all_to_all | solution.py:161
  141.2 14.7 %all-to-all-done = bf16[128,3,768]{2,1,0:T(4,128)(2,1)S(1)} async-done(((bf16[128,3,768]{2,1,0:T(4,128)(2,1)}), bf16[128,3,768]{2,1,0:T(4,128)(2,1)S(1)}, u32[]{:S(2)}, u32[]{:S(2)}) %all-to-all-start) | async-done | bytes 589856 | tf_op jit(solution)/shard_map/all_to_all | solution.py:161
  157.7 2.2 pad_slice_fusion
  177.7 6.4 %all-to-all-start.1 = ((bf16[128,3,768]{2,1,0:T(4,128)(2,1)}), bf16[128,3,768]{2,1,0:T(4,128)(2,1)S(1)}, u32[]{:S(2)}, u32[]{:S(2)}) async-start(bf16[128,3,768]{2,1,0:T(4,128)(2,1)} %reshape.176), calls=%async_computation.1 | async-start | bytes 1572864 | tf_op jit(solution)/shard_map/all_to_all | solution.py:173
  184.3 14.6 %all-to-all-done.1 = bf16[128,3,768]{2,1,0:T(4,128)(2,1)S(1)} async-done(((bf16[128,3,768]{2,1,0:T(4,128)(2,1)}), bf16[128,3,768]{2,1,0:T(4,128)(2,1)S(1)}, u32[]{:S(2)}, u32[]{:S(2)}) %all-to-all-start.1) | async-done | bytes 589856 | tf_op jit(solution)/shard_map/all_to_all | solution.py:173
  201.2 3.4 %copy.107 = f32[192,2,2,2,2,2,2,96]{0,7,6,5,4,3,2,1:T(8,128)} copy(f32[192,2,2,2,2,2,2,96]{0,7,6,4,2,5,3,1:T(8,128)S(1)} %convolution_bitcast_fusion) | data formatting | bytes 9437184 | tf_op jit(solution)/shard_map/transpose | solution.py:128
  204.6 6.5 %copy.108 = f32[192,16,3,128]{3,1,2,0:T(8,128)} copy(f32[192,16,3,128]{0,3,2,1:T(8,128)} %bitcast.188) | data formatting | bytes 9437184 | tf_op jit(solution)/shard_map/reshape;reshape | solution.py:238
  211.1 2.9 fusion.1.own_hbm
  214.1 2.1 collective-permute-start.4
  216.2 4.0 %collective-permute-start.5 = (bf16[1,1,48,3,16,128]{5,4,3,2,1,0:T(8,128)(2,1)S(1)}, bf16[1,1,48,3,16,128]{5,4,3,2,1,0:T(8,128)(2,1)S(1)}, u32[]{:S(2)}, u32[]{:S(2)}) collective-permute-start(bf16[1,1,48,3,16,128]{5,4,3,2,1,0:T(8,128)(2,1)S(1)} %slice_bitcast_fusion), channel_id=1, source_target_pairs={{32,0},{64,32},{96,64},{33,1},{65,33},{97,65},{34,2},{66,34},{98,6... | collective-permute-start | bytes 1769480 | tf_op jit(solution)/shard_map/ppermute | solution.py:115
  220.1 10.3 %collective-permute-done.4 = bf16[1,1,48,3,16,128]{5,4,3,2,1,0:T(8,128)(2,1)S(1)} collective-permute-done((bf16[1,1,48,3,16,128]{5,4,3,2,1,0:T(8,128)(2,1)S(1)}, bf16[1,1,48,3,16,128]{5,4,3,2,1,0:T(8,128)(2,1)S(1)}, u32[]{:S(2)}, u32[]{:S(2)}) %collective-permute-start.4) | collective-permute-done | bytes 589856 | tf_op jit(solution)/shard_map/ppermute | solution.py:112
  230.5 2.0 collective-permute-done.5
  232.7 1.9 collective-permute-start.6
  234.6 5.8 %collective-permute-start.7 = (bf16[3,1,48,3,16,128]{5,4,3,2,1,0:T(8,128)(2,1)S(1)}, bf16[3,1,48,3,16,128]{5,4,3,2,1,0:T(8,128)(2,1)S(1)}, u32[]{:S(2)}, u32[]{:S(2)}) collective-permute-start(bf16[3,1,48,3,16,128]{5,4,3,2,1,0:T(8,128)(2,1)S(1)} %pad_maximum_fusion.3), channel_id=1, source_target_pairs={{1,0},{2,1},{3,2},{4,3},{5,4},{6,5},{7,6},{8,7},{9,8},{10,9},{11,1... | collective-permute-start | bytes 5308424 | tf_op jit(solution)/shard_map/ppermute | solution.py:115
  241.5 17.2 %collective-permute-done.6 = bf16[3,1,48,3,16,128]{5,4,3,2,1,0:T(8,128)(2,1)S(1)} collective-permute-done((bf16[3,1,48,3,16,128]{5,4,3,2,1,0:T(8,128)(2,1)S(1)}, bf16[3,1,48,3,16,128]{5,4,3,2,1,0:T(8,128)(2,1)S(1)}, u32[]{:S(2)}, u32[]{:S(2)}) %collective-permute-start.6) | collective-permute-done | bytes 1769504 | tf_op jit(solution)/shard_map/ppermute | solution.py:112
  260.4 2.9 pad_maximum_fusion.1
  263.3 43.2 %conv.3 = bf16[192,3,16,128]{3,2,1,0:T(8,128)(2,1)} custom-call(s32[5376]{0:T(1024)} %reshape.144.table, s32[1]{0:T(128)} %bitcast.186.count, bf16[27,96,128]{2,1,0:T(8,128)(2,1)} %pad.16.w_ref, bf16[192,3,16,128]{3,2,1,0:T(8,128)(2,1)} %copy-done.4, bf16[432,3,16,128]{3,2,1,0:T(8,128)(2,1)} %bitcast.189), custom_call_target="tpu_custom_call" | custom-call | tf_op jit(solution)/shard_map/conv/pallas_call | solution.py:86
  306.6 3.4 %copy.109 = bf16[192,16,3,128]{3,2,1,0:T(4,128)(2,1)S(1)} copy(bf16[192,16,3,128]{3,1,2,0:T(8,128)(2,1)} %bitcast.193) | data formatting | bytes 4718592 | tf_op jit(solution)/shard_map/transpose | solution.py:104
  310.0 4.2 %broadcast_in_dim_reshape.3 = bf16[1,192,6144]{2,1,0:T(8,128)(2,1)} reshape(bf16[192,16,3,128]{3,2,1,0:T(4,128)(2,1)S(1)} %copy.109) | data formatting | bytes 4718592 | tf_op jit(solution)/shard_map/broadcast_in_dim;reshape | solution.py:241
  (116 shorter events, 35.1 us)
Async XLA Ops:
  0.0 128.0 %copy-start = (bf16[768,96]{0,1:T(8,128)(2,1)S(1)}, bf16[768,96]{0,1:T(8,128)(2,1)}, u32[]{:S(2)}) copy-start(bf16[768,96]{0,1:T(8,128)(2,1)} %param.16) | copy-start | bytes 442372
  7.9 1.4 copy-start.3
  9.3 29.8 %copy-start.9 = (s32[1,27,192]{2,0,1:T(1,128)S(1)}, s32[1,27,192]{2,0,1:T(1,128)}, u32[]{:S(2)}) copy-start(s32[1,27,192]{2,0,1:T(1,128)} %param.12) | copy-start | bytes 62212
  9.3 30.7 %copy-start.5 = (bf16[27,96,96]{2,1,0:T(8,128)(2,1)S(1)}, bf16[27,96,96]{2,1,0:T(8,128)(2,1)}, u32[]{:S(2)}) copy-start(bf16[27,96,96]{2,1,0:T(8,128)(2,1)} %param.15) | copy-start | bytes 1492996
  9.3 31.7 %copy-start.10 = (s32[1,192]{1,0:T(1,128)S(1)}, s32[1,192]{1,0:T(1,128)}, u32[]{:S(2)}) copy-start(s32[1,192]{1,0:T(1,128)} %param.13) | copy-start | bytes 2308
  9.4 17.1 %collective-permute-start = (bf16[1,1,48,3,16,128]{5,4,3,2,1,0:T(8,128)(2,1)S(1)}, bf16[1,1,48,3,16,128]{5,4,3,2,1,0:T(8,128)(2,1)S(1)}, u32[]{:S(2)}, u32[]{:S(2)}) collective-permute-start(bf16[1,1,48,3,16,128]{5,4,3,2,1,0:T(8,128)(2,1)S(1)} %slice_bitcast_fusion.1), channel_id=1, source_target_pairs={{0,32},{32,64},{64,96},{1,33},{33,65},{65,97},{2,34},{34,66},{66,9... | collective-permute-start | bytes 1769480 | tf_op jit(solution)/shard_map/ppermute | solution.py:112
  13.3 16.7 %collective-permute-start.1 = (bf16[1,1,48,3,16,128]{5,4,3,2,1,0:T(8,128)(2,1)S(1)}, bf16[1,1,48,3,16,128]{5,4,3,2,1,0:T(8,128)(2,1)S(1)}, u32[]{:S(2)}, u32[]{:S(2)}) collective-permute-start(bf16[1,1,48,3,16,128]{5,4,3,2,1,0:T(8,128)(2,1)S(1)} %slice_bitcast_fusion.1), channel_id=1, source_target_pairs={{32,0},{64,32},{96,64},{33,1},{65,33},{97,65},{34,2},{66,34},{98,6... | collective-permute-start | bytes 1769480 | tf_op jit(solution)/shard_map/ppermute | solution.py:115
  31.4 26.3 %collective-permute-start.2 = (bf16[3,1,48,3,16,128]{5,4,3,2,1,0:T(8,128)(2,1)}, bf16[3,1,48,3,16,128]{5,4,3,2,1,0:T(8,128)(2,1)}, u32[]{:S(2)}, u32[]{:S(2)}) collective-permute-start(bf16[3,1,48,3,16,128]{5,4,3,2,1,0:T(8,128)(2,1)} %pad_maximum_fusion.2), channel_id=1, source_target_pairs={{0,1},{1,2},{2,3},{3,4},{4,5},{5,6},{6,7},{7,8},{8,9},{9,10},{10,1... | collective-permute-start | bytes 5308424 | tf_op jit(solution)/shard_map/ppermute | solution.py:112
  33.4 26.1 %collective-permute-start.3 = (bf16[3,1,48,3,16,128]{5,4,3,2,1,0:T(8,128)(2,1)}, bf16[3,1,48,3,16,128]{5,4,3,2,1,0:T(8,128)(2,1)}, u32[]{:S(2)}, u32[]{:S(2)}) collective-permute-start(bf16[3,1,48,3,16,128]{5,4,3,2,1,0:T(8,128)(2,1)} %pad_maximum_fusion.2), channel_id=1, source_target_pairs={{1,0},{2,1},{3,2},{4,3},{5,4},{6,5},{7,6},{8,7},{9,8},{10,9},{11,1... | collective-permute-start | bytes 5308424 | tf_op jit(solution)/shard_map/ppermute | solution.py:115
  128.8 12.4 %copy-start.11 = (s32[1,384]{1,0:T(1,128)S(1)}, s32[1,384]{1,0:T(1,128)}, u32[]{:S(2)}) copy-start(s32[1,384]{1,0:T(1,128)} %param.14) | copy-start | bytes 4612
  130.5 25.4 %all-to-all-start = ((bf16[128,3,768]{2,1,0:T(4,128)(2,1)}), bf16[128,3,768]{2,1,0:T(4,128)(2,1)S(1)}, u32[]{:S(2)}, u32[]{:S(2)}) async-start(bf16[128,3,768]{2,1,0:T(4,128)(2,1)} %reshape.147), calls=%async_computation | async-start | bytes 1572864 | tf_op jit(solution)/shard_map/all_to_all | solution.py:161
  164.9 1.2 copy-start.7
  175.9 8.2 %copy-start.8 = (bf16[96,768]{1,0:T(8,128)(2,1)S(1)}, bf16[96,768]{1,0:T(8,128)(2,1)}, u32[]{:S(2)}) copy-start(bf16[96,768]{1,0:T(8,128)(2,1)} %param.18) | copy-start | bytes 442372
  177.7 21.2 %all-to-all-start.1 = ((bf16[128,3,768]{2,1,0:T(4,128)(2,1)}), bf16[128,3,768]{2,1,0:T(4,128)(2,1)S(1)}, u32[]{:S(2)}, u32[]{:S(2)}) async-start(bf16[128,3,768]{2,1,0:T(4,128)(2,1)} %reshape.176), calls=%async_computation.1 | async-start | bytes 1572864 | tf_op jit(solution)/shard_map/all_to_all | solution.py:173
  204.6 6.5 %copy-start.2 = (bf16[192,3,16,128]{3,2,1,0:T(8,128)(2,1)S(1)}, bf16[192,3,16,128]{3,2,1,0:T(8,128)(2,1)}, u32[]{:S(2)}) copy-start(bf16[192,3,16,128]{3,2,1,0:T(8,128)(2,1)} %conv.2) | copy-start | bytes 7077892
  214.0 27.4 %copy-start.4 = (bf16[192,3,16,128]{3,2,1,0:T(8,128)(2,1)}, bf16[192,3,16,128]{3,2,1,0:T(8,128)(2,1)S(1)}, u32[]{:S(2)}) copy-start(bf16[192,3,16,128]{3,2,1,0:T(8,128)(2,1)S(1)} %fusion.1.own_hbm) | copy-start | bytes 7077892
  214.0 26.4 %copy-start.6 = (bf16[27,96,96]{2,1,0:T(8,128)(2,1)S(1)}, bf16[27,96,96]{2,1,0:T(8,128)(2,1)}, u32[]{:S(2)}) copy-start(bf16[27,96,96]{2,1,0:T(8,128)(2,1)} %param.19) | copy-start | bytes 1492996
  214.1 16.4 %collective-permute-start.4 = (bf16[1,1,48,3,16,128]{5,4,3,2,1,0:T(8,128)(2,1)S(1)}, bf16[1,1,48,3,16,128]{5,4,3,2,1,0:T(8,128)(2,1)S(1)}, u32[]{:S(2)}, u32[]{:S(2)}) collective-permute-start(bf16[1,1,48,3,16,128]{5,4,3,2,1,0:T(8,128)(2,1)S(1)} %slice_bitcast_fusion), channel_id=1, source_target_pairs={{0,32},{32,64},{64,96},{1,33},{33,65},{65,97},{2,34},{34,66},{66,9... | collective-permute-start | bytes 1769480 | tf_op jit(solution)/shard_map/ppermute | solution.py:112
  216.2 16.3 %collective-permute-start.5 = (bf16[1,1,48,3,16,128]{5,4,3,2,1,0:T(8,128)(2,1)S(1)}, bf16[1,1,48,3,16,128]{5,4,3,2,1,0:T(8,128)(2,1)S(1)}, u32[]{:S(2)}, u32[]{:S(2)}) collective-permute-start(bf16[1,1,48,3,16,128]{5,4,3,2,1,0:T(8,128)(2,1)S(1)} %slice_bitcast_fusion), channel_id=1, source_target_pairs={{32,0},{64,32},{96,64},{33,1},{65,33},{97,65},{34,2},{66,34},{98,6... | collective-permute-start | bytes 1769480 | tf_op jit(solution)/shard_map/ppermute | solution.py:115
  232.7 26.0 %collective-permute-start.6 = (bf16[3,1,48,3,16,128]{5,4,3,2,1,0:T(8,128)(2,1)S(1)}, bf16[3,1,48,3,16,128]{5,4,3,2,1,0:T(8,128)(2,1)S(1)}, u32[]{:S(2)}, u32[]{:S(2)}) collective-permute-start(bf16[3,1,48,3,16,128]{5,4,3,2,1,0:T(8,128)(2,1)S(1)} %pad_maximum_fusion.3), channel_id=1, source_target_pairs={{0,1},{1,2},{2,3},{3,4},{4,5},{5,6},{6,7},{7,8},{8,9},{9,10},{10,1... | collective-permute-start | bytes 5308424 | tf_op jit(solution)/shard_map/ppermute | solution.py:112
  234.6 25.8 %collective-permute-start.7 = (bf16[3,1,48,3,16,128]{5,4,3,2,1,0:T(8,128)(2,1)S(1)}, bf16[3,1,48,3,16,128]{5,4,3,2,1,0:T(8,128)(2,1)S(1)}, u32[]{:S(2)}, u32[]{:S(2)}) collective-permute-start(bf16[3,1,48,3,16,128]{5,4,3,2,1,0:T(8,128)(2,1)S(1)} %pad_maximum_fusion.3), channel_id=1, source_target_pairs={{1,0},{2,1},{3,2},{4,3},{5,4},{6,5},{7,6},{8,7},{9,8},{10,9},{11,1... | collective-permute-start | bytes 5308424 | tf_op jit(solution)/shard_map/ppermute | solution.py:115
  306.6 7.6 %copy-start.1 = (bf16[768,96]{0,1:T(8,128)(2,1)S(1)}, bf16[768,96]{0,1:T(8,128)(2,1)}, u32[]{:S(2)}) copy-start(bf16[768,96]{0,1:T(8,128)(2,1)} %param.16) | copy-start | bytes 442372

commit v2 on v0

v2 whole, which is shorter than its diff:
```python
import functools
import itertools

import jax
import jax.numpy as jnp
from jax import lax
from jax.experimental import pallas as pl
from jax.experimental.pallas import tpu as pltpu
from jax.sharding import PartitionSpec as P

TAPS = 27
ORDER = [[(q - i) % 4 for q in range(4)] for i in range(4)]
CUT = (96, 64, 32)
BLOCK = 32
CHUNKS = ((0, 1), (2, 3), (4, 5), (6,))
MIB = 1024 * 1024
BF16 = jnp.bfloat16
F32 = jnp.float32


def swap_halves(a, b):
    low = lax.broadcasted_iota(jnp.int32, a[0].shape, a[0].ndim - 1) < 64
    turn = lambda x: pltpu.roll(x, 64, x.ndim - 1)
    a1, a2, b0, b1 = turn(a[1]), turn(a[2]), turn(b[0]), turn(b[1])
    first = (a[0], jnp.where(low, a[1], b0), jnp.where(low, b0, b1))
    second = (jnp.where(low, a1, a2), jnp.where(low, a2, b[1]), b[2])
    return first, second


def group_of(cz, sz, cy):
    return ((cz * 2 + sz) * 2 + cy) * 2, sz * 8 + cz * 4 + cy * 2


def to_dense(x):
    rows = [None] * 16
    for cz, sz, cy in itertools.product(range(2), repeat=3):
        g, r = group_of(cz, sz, cy)
        part = lambda s: [x[:, (g + s) * 384 + t * 128 : (g + s) * 384 + (t + 1) * 128] for t in range(3)]
        rows[r], rows[r + 1] = swap_halves(part(0), part(1))
    return [jnp.swapaxes(jnp.stack([row[t] for row in rows], axis=0), 0, 1) for t in range(3)]


def from_dense(tiles):
    rows = [jnp.swapaxes(x, 0, 1) for x in tiles]
    out = [None] * 16
    for cz, sz, cy in itertools.product(range(2), repeat=3):
        g, r = group_of(cz, sz, cy)
        out[g], out[g + 1] = swap_halves([x[r] for x in rows], [x[r + 1] for x in rows])
    return jnp.concatenate([y for x in out for y in x], axis=1)


def dense_kernel(count, x_ref, o_ref):
    first = pl.program_id(0) * 16
    rows = lax.broadcasted_iota(jnp.int32, x_ref.shape, 0) + first
    x = jnp.where(rows < count[0], x_ref[...], jnp.zeros((), BF16))
    for t, y in enumerate(to_dense(x)):
        o_ref[:, t] = y


def make_dense(count, x):
    bricks = x.shape[0]
    return pl.pallas_call(
        dense_kernel,
        grid=(bricks // 16,),
        out_shape=jax.ShapeDtypeStruct((bricks, 3, 16, 128), BF16),
        in_specs=[pl.BlockSpec(memory_space=pltpu.SMEM), pl.BlockSpec((16, x.shape[1]), lambda i: (i, 0))],
        out_specs=pl.BlockSpec((16, 3, 16, 128), lambda i: (i, 0, 0, 0)),
        name="densify",
    )(count, x)


def rotate_range(rot, start, stop):
    wide = lax.broadcasted_iota(jnp.int32, (128, 128), 1)

    def body(m, carry):
        n = pl.multiple_of(m * 8, 8)
        tiles = [rot[0, pl.ds(n, 8), t].reshape(128, 128) for t in range(3)]
        done = []
        for j in range(1, 4):
            amount = (96 * j) % 128
            rolled = [pltpu.roll(x, amount, 1) for x in tiles]
            for u in range(3):
                hi = (128 * u + 127 - 96 * j) // 128 % 3
                lo = (128 * u - 96 * j) // 128 % 3
                done.append((j, u, jnp.where(wide >= amount, rolled[hi], rolled[lo]).reshape(8, 16, 128)))
        for j, u, x in done:
            rot[j, pl.ds(n, 8), u] = x
        return carry

    lax.fori_loop(start // 8, stop // 8, body, 0)


def conv_block(step, table, w_ref, rot):
    lane = lax.broadcasted_iota(jnp.int32, (16, 128), 1)

    def gather(c, b):
        base = (step * BLOCK + b) * 28
        lanes = [[] for _ in range(4)]
        for g in CHUNKS[c]:
            loads = [[rot[j, table[base + 4 * g + j], t] for t in range(3)] for j in range(4)]
            for i in range(4):
                for u in range(3):
                    a, b2 = loads[ORDER[i][u]][u], loads[ORDER[i][u + 1]][u]
                    lanes[i].append(jnp.where(lane < CUT[u], a, b2))
        return lanes

    acc = [None] * 4
    for c in range(len(CHUNKS)):
        got = [gather(c, b) for b in range(BLOCK)]
        for i in range(4):
            lhs = jnp.concatenate([jnp.concatenate(x[i], axis=1) for x in got], axis=0)
            taps = [4 * g + ORDER[i][q] for g in CHUNKS[c] for q in range(4)]
            rhs = jnp.concatenate([w_ref[k] if k < TAPS else jnp.zeros((96, 128), BF16) for k in taps], axis=0)
            part = jnp.dot(lhs, rhs, preferred_element_type=F32)
            acc[i] = part if acc[i] is None else acc[i] + part
    r1 = pltpu.roll(acc[1], 96, 1)
    r2 = pltpu.roll(acc[2], 64, 1)
    r3 = pltpu.roll(acc[3], 32, 1)
    lanes = lax.broadcasted_iota(jnp.int32, acc[0].shape, 1)
    return (jnp.where(lanes < 96, acc[0], r1), jnp.where(lanes < 64, r1, r2), jnp.where(lanes < 32, r2, r3))


def load_field(own, halos, rot, sems):
    bricks = own.shape[0]
    part = halos[0].shape[0]
    total = bricks + len(halos) * part
    copies = [pltpu.make_async_copy(own, rot.at[0, pl.ds(0, bricks)], sems.at[0])]
    for d, piece in enumerate(halos):
        copies.append(pltpu.make_async_copy(piece, rot.at[0, pl.ds(bricks + d * part, part)], sems.at[d + 1]))
    for copy in copies:
        copy.start()
    for j in range(4):
        rot[j, total] = jnp.zeros((3, 16, 128), BF16)
    copies[0].wait()
    rotate_range(rot, 0, bricks)
    for copy in copies[1:]:
        copy.wait()
    rotate_range(rot, bricks, total)


def encode_kernel(table, count, send_slot, w_ref, wd_ref, own, *rest):
    halos, (enc_ref, out_ref, rot, pooled, sems) = rest[:8], rest[8:]
    step = pl.program_id(0)
    bricks = own.shape[0]

    @pl.when(step == 0)
    def _():
        load_field(own, halos, rot, sems)
        pooled[bricks] = jnp.zeros((8, 128), F32)

    tiles = conv_block(step, table, w_ref, rot)
    shape = tiles[0].shape
    live = lax.broadcasted_iota(jnp.int32, shape, 0) // 16 + step * BLOCK < count[0]
    values = []
    for u in range(3):
        mine = rot[0, pl.ds(step * BLOCK, BLOCK), u].reshape(shape).astype(F32)
        value = jnp.where(live, mine + jnp.maximum(tiles[u], 0.0), 0.0).astype(BF16)
        enc_ref[:, u] = value.reshape(BLOCK, 16, 128)
        values.append(value)
    sums = jnp.dot(jnp.concatenate(values, axis=1), wd_ref[...], preferred_element_type=F32)
    sums = sums.reshape(BLOCK, 16, 256)
    sums = sums[:, :8, :128] + sums[:, 8:, 128:]
    pooled[pl.ds(step * BLOCK, BLOCK)] = sums

    @pl.when(step == pl.num_programs(0) - 1)
    def _():
        def place(s, carry):
            out_ref[s] = pooled[send_slot[s]].astype(BF16)
            return carry

        lax.fori_loop(0, out_ref.shape[0], place, 0, unroll=8)


def field_scratch(own, halos):
    total = own.shape[0] + len(halos) * halos[0].shape[0]
    return pltpu.VMEM((4, total + 1, 3, 16, 128), BF16)


SMEM = pl.BlockSpec(memory_space=pltpu.SMEM)
VMEM = pl.BlockSpec(memory_space=pltpu.VMEM)
ANY = pl.BlockSpec(memory_space=pl.ANY)


def encode(table, count, send_slot, w, wd, own, halos):
    bricks = own.shape[0]
    slots = send_slot.shape[0]
    return pl.pallas_call(
        encode_kernel,
        grid=(bricks // BLOCK,),
        out_shape=(
            jax.ShapeDtypeStruct((bricks, 3, 16, 128), BF16),
            jax.ShapeDtypeStruct((slots, 8, 128), BF16),
        ),
        in_specs=[SMEM, SMEM, SMEM, VMEM, VMEM, ANY] + [ANY] * len(halos),
        out_specs=(pl.BlockSpec((BLOCK, 3, 16, 128), lambda i: (i, 0, 0, 0)), VMEM),
        scratch_shapes=[
            field_scratch(own, halos),
            pltpu.VMEM((bricks + 1, 8, 128), F32),
            pltpu.SemaphoreType.DMA((9,)),
        ],
        compiler_params=pltpu.CompilerParams(vmem_limit_bytes=56 * MIB),
        name="encode",
    )(table, count, send_slot, w, wd, own, *halos)


def raw_kernel(table, w_ref, own, *rest):
    halos, (out_ref, rot, sems) = rest[:8], rest[8:]
    step = pl.program_id(0)

    @pl.when(step == 0)
    def _():
        load_field(own, halos, rot, sems)

    for u, tile in enumerate(conv_block(step, table, w_ref, rot)):
        out_ref[:, u] = tile.reshape(BLOCK, 16, 128)


def raw_conv(table, w, own, halos):
    bricks = own.shape[0]
    return pl.pallas_call(
        raw_kernel,
        grid=(bricks // BLOCK,),
        out_shape=jax.ShapeDtypeStruct((bricks, 3, 16, 128), F32),
        in_specs=[SMEM, VMEM, ANY] + [ANY] * len(halos),
        out_specs=pl.BlockSpec((BLOCK, 3, 16, 128), lambda i: (i, 0, 0, 0)),
        scratch_shapes=[field_scratch(own, halos), pltpu.SemaphoreType.DMA((9,))],
        compiler_params=pltpu.CompilerParams(vmem_limit_bytes=56 * MIB),
        cost_estimate=pl.CostEstimate(flops=40_000_000_000, bytes_accessed=13_000_000, transcendentals=0),
        name="raw_conv",
    )(table, w, own, *halos)


def coarse_kernel(from_slot, to_place, w_ref, in_ref, out_ref, cells, grid, turned):
    places = from_slot.shape[0]
    groups = places // 8
    grid[...] = jnp.zeros(grid.shape, BF16)

    def land(p, carry):
        cells[pl.ds(pl.multiple_of(p * 8, 8), 8)] = in_ref[from_slot[p]].astype(F32)
        return carry

    lax.fori_loop(0, places, land, 0, unroll=8)
    voxels = list(itertools.product(range(4), repeat=3))

    def base(z, y, x):
        t = (z // 2) * 4 + (y // 2) * 2 + x // 2
        c = (z % 2) * 4 + (y % 2) * 2 + x % 2
        return t * places + c

    zero = jnp.zeros((32 - groups, 128), F32)
    for z, y, x in voxels:
        piece = cells[pl.ds(base(z, y, x), groups, stride=8)]
        grid[z + 1, y + 1, x + 1] = jnp.concatenate([piece, zero], axis=0).astype(BF16)

    for z in range(4):
        acc = None
        for k0 in range(0, TAPS + 1, 2):
            sides = []
            for k in (k0, min(k0 + 1, TAPS - 1)):
                dz, dy, dx = k // 9, k // 3 % 3, k % 3
                sides.append(grid[z + dz, dy : dy + 4, dx : dx + 4].reshape(16 * 32, 128))
            second = w_ref[k0 + 1] if k0 + 1 < TAPS else jnp.zeros((128, 128), BF16)
            rhs = jnp.concatenate([w_ref[k0], second], axis=0)
            part = jnp.dot(jnp.concatenate(sides, axis=1), rhs, preferred_element_type=F32)
            acc = part if acc is None else acc + part
        acc = acc.reshape(16, 32, 128)
        for y in range(4):
            for x in range(4):
                here = grid[z + 1, y + 1, x + 1].astype(F32) + jnp.maximum(acc[y * 4 + x], 0.0)
                turned[pl.ds(base(z, y, x), groups, stride=8)] = here[:groups]
    turned[pl.ds(places * 8, 8)] = jnp.zeros((8, 128), F32)

    def reply(s, carry):
        out_ref[s] = turned[pl.ds(pl.multiple_of(to_place[s] * 8, 8), 8)].astype(BF16)
        return carry

    lax.fori_loop(0, out_ref.shape[0], reply, 0, unroll=8)


def coarse(from_slot, to_place, w, incoming):
    places = from_slot.shape[0]
    return pl.pallas_call(
        coarse_kernel,
        out_shape=jax.ShapeDtypeStruct(incoming.shape, BF16),
        in_specs=[SMEM, SMEM, VMEM, VMEM],
        out_specs=VMEM,
        scratch_shapes=[
            pltpu.VMEM((places * 8, 128), F32),
            pltpu.VMEM((6, 6, 6, 32, 128), BF16),
            pltpu.VMEM((places * 8 + 8, 128), F32),
        ],
        compiler_params=pltpu.CompilerParams(vmem_limit_bytes=32 * MIB),
        name="coarse_mix",
    )(from_slot, to_place, w, incoming)


def back_kernel(slot, count, in_ref, out_ref):
    def take(b, carry):
        value = in_ref[slot[b]]
        out_ref[b] = jnp.where(b < count[0], value, jnp.zeros_like(value))
        return carry

    lax.fori_loop(0, out_ref.shape[0], take, 0, unroll=8)


def take_back(slot, count, returned):
    return pl.pallas_call(
        back_kernel,
        out_shape=jax.ShapeDtypeStruct((slot.shape[0], 8, 128), BF16),
        in_specs=[SMEM, SMEM, VMEM],
        out_specs=VMEM,
        name="take_back",
    )(slot, count, returned)


def decode_kernel(table, count, w_ref, up_ref, own_ref, raw_ref, enc_ref, *rest):
    halos, (out_ref, cells) = rest[:8], rest[8:]
    step = pl.program_id(0)
    bricks = own_ref.shape[0]
    part = halos[0].shape[0]
    total = bricks + 8 * part

    @pl.when(step == 0)
    def _():
        cells[pl.ds(0, bricks)] = own_ref[...].astype(F32)
        for d, piece in enumerate(halos):
            cells[pl.ds(bricks + d * part, part)] = piece[...].astype(F32)
        cells[total] = jnp.zeros((8, 128), F32)

    block = enc_ref.shape[0]
    acc = None
    for g in range(7):
        columns = []
        for j in range(4):
            rows = [cells[table[(step * block + b) * 28 + 4 * g + j]] for b in range(block)]
            columns.append(jnp.concatenate(rows, axis=0).astype(BF16))
        lhs = jnp.concatenate(columns, axis=1)
        part_sum = jnp.dot(lhs, w_ref[g * 512 : (g + 1) * 512], preferred_element_type=F32)
        acc = part_sum if acc is None else acc + part_sum
    mine = cells[pl.ds(step * block, block)].reshape(block * 8, 128).astype(BF16)
    lifted = jnp.dot(mine, up_ref[...], preferred_element_type=F32)
    live = lax.broadcasted_iota(jnp.int32, (block, 8, 128), 0) + step * block < count[0]
    tiles = []
    for u in range(3):
        halves = []
        coded = enc_ref[:, u].astype(F32)
        for h in range(2):
            lanes = slice(h * 384 + u * 128, h * 384 + (u + 1) * 128)
            restored = coded[:, h * 8 : h * 8 + 8] + lifted[:, lanes].reshape(block, 8, 128)
            restored = restored.astype(BF16).astype(F32)
            mixed = raw_ref[:, u, h * 8 : h * 8 + 8] + acc[:, lanes].reshape(block, 8, 128)
            halves.append(jnp.where(live, restored + jnp.maximum(mixed, 0.0), 0.0))
        tiles.append(jnp.concatenate(halves, axis=1).astype(BF16))
    out_ref[...] = from_dense(tiles)


def decode(table, count, w, up, own, raw, enc, halos):
    bricks = own.shape[0]
    total = bricks + 8 * halos[0].shape[0]
    block = 16
    blocked = lambda: pl.BlockSpec((block, 3, 16, 128), lambda i: (i, 0, 0, 0))
    return pl.pallas_call(
        decode_kernel,
        grid=(bricks // block,),
        out_shape=jax.ShapeDtypeStruct((bricks, 6144), BF16),
        in_specs=[SMEM, SMEM, VMEM, VMEM, VMEM, blocked(), blocked()] + [VMEM] * 8,
        out_specs=pl.BlockSpec((block, 6144), lambda i: (i, 0)),
        scratch_shapes=[pltpu.VMEM((total + 1, 8, 128), F32)],
        compiler_params=pltpu.CompilerParams(vmem_limit_bytes=48 * MIB),
        name="decode",
    )(table, count, w, up, own, raw, enc, *halos)


def halo(face):
    def sides(block, axis):
        count = lax.axis_size(axis)
        forward = [(i, i + 1) for i in range(count - 1)]
        backward = [(target, source) for source, target in forward]
        return lax.ppermute(block, axis, forward), lax.ppermute(block, axis, backward)

    below, above = sides(face, "gz")
    left, right = sides(face, "gx")
    below_left, below_right = sides(below, "gx")
    above_left, above_right = sides(above, "gx")
    return [below_left, below, below_right, left, right, above_left, above, above_right]


def relay(buffer, devices):
    moved = lax.all_to_all(
        buffer.reshape(devices, -1, 128), ("gz", "gx"), split_axis=0, concat_axis=0, tiled=True
    )
    return moved.reshape(-1, 8, 128)


def on_device(
    features, active_count, neighbors, owner, arrival_cell, w_enc, w_down, w_mid, w_up, w_dec
):
    devices = lax.axis_size("gz") * lax.axis_size("gx")
    bricks = features.shape[1]
    boundary = bricks // 4
    chans = w_enc.shape[1]
    spare = 128 - chans
    capacity = arrival_cell.shape[1] // devices
    slot_count = devices * capacity
    count = active_count[0]
    n = neighbors[0]
    m = n - bricks
    side = m // boundary
    n = jnp.where(m >= 4 * boundary, jnp.where(side == 4, m - 4 * boundary, n - boundary), n)
    empty = bricks + 8 * boundary
    table = jnp.pad(jnp.where(n < 0, empty, n), ((0, 1), (0, 0)), constant_values=empty)
    table = table.T.reshape(-1)
    target = owner[0]
    index = jnp.arange(bricks, dtype=jnp.int32)
    same = jnp.logical_and(target[:, None] == target[None, :], index[None, :] < index[:, None])
    slot = target * capacity + jnp.sum(same.astype(jnp.int32), axis=1)
    slot_ids = jnp.arange(slot_count, dtype=jnp.int32)
    send_slot = jnp.min(jnp.where(slot_ids[:, None] == slot[None, :], index[None, :], bricks), axis=1)
    arrivals = arrival_cell[0]
    to_place = jnp.where(arrivals < 0, bricks, arrivals % 8 * (bricks // 8) + arrivals // 8)
    from_slot = jnp.sum(
        jnp.where(index[:, None] == to_place[None, :], slot_ids[None, :], 0), axis=1
    )
    lanes = ((0, 0), (0, 0), (0, spare))
    pooling = jnp.pad(w_down.reshape(2, 4 * chans, chans), lanes)
    pooling = pooling.transpose(1, 0, 2).reshape(4 * chans, 256)
    both = ((0, 0), (0, spare), (0, spare))
    raising = jnp.pad(w_up, ((0, spare), (0, 0)))

    x = make_dense(count, features[0])
    encoded, outgoing = encode(
        table, count, send_slot, jnp.pad(w_enc, lanes), pooling, x, halo(x[:boundary])
    )
    incoming = relay(outgoing, devices)
    encoded_halo = halo(encoded[:boundary])
    reply = coarse(from_slot, to_place, jnp.pad(w_mid, both), incoming)
    returned = relay(reply, devices)
    raw = raw_conv(table, jnp.pad(w_dec, lanes), encoded, encoded_halo)
    lift = jnp.einsum(
        "cse,ked->kcsd", w_up.reshape(chans, 8, chans), w_dec, preferred_element_type=F32
    )
    lift = jnp.pad(lift.astype(BF16).reshape(TAPS, chans, 8 * chans), ((0, 1), (0, spare), (0, 0)))
    lift = lift.reshape(28 * 128, 8 * chans)
    back = take_back(slot, count, returned)
    decoded = decode(
        table, count, lift, raising, back, raw, encoded, halo(back[:boundary])
    )
    return decoded[None]


def solution(mesh):
    placed = (
        P("gz", "gx", None),
        P("gz", "gx"),
        P("gz", None, "gx"),
        P("gz", "gx"),
        P("gz", "gx"),
        P(),
        P(),
        P(),
        P(),
        P(),
    )
    return jax.shard_map(
        on_device, mesh=mesh, in_specs=placed, out_specs=P("gz", "gx", None), check_vma=False
    )
```

time: 1260 us -> 256 us (0.20)
  local copies, waits for them, and re-layouts: 762 us -> 22.2 us
  matrix products: 198 us -> 3.93 us
  other arithmetic: 180 us -> 1.67 us
  Pallas kernels: 0 us -> 114 us
  starting transfers between devices: 35.8 us -> 101 us
  waiting for transfers between devices: 71.8 us -> 10.9 us
    gather x18 -> x0, local copies, waits for them, and re-layouts: 371 us -> none  [step(): picked = jnp.take(extended, rows.reshape(-1), axis=0)]
    reshape x41 -> x5, local copies, waits for them, and re-layouts: 287 us -> 8.04 us  [the longest x1 6.82 us: on_device(): lift.astype(BF16).reshape(TAPS, chans, 8 * chans)]
    dot_general x51 -> x1, matrix products: 198 us -> 3.93 us  [on_device(): jnp.einsum('cse,ked->kcsd', w_up.reshape(chans, 8, chans), w_dec, preferr...]
    select_n x38 -> x2, other arithmetic: 120 us -> 0.05 us  [the longest x1 0.04 us: on_device(): jnp.where(n < 0, empty, n)]
    pallas_call x0 -> x6, Pallas kernels: none -> 114 us  [the longest x1 41.8 us: encode(): pl.pallas_call(encode_kernel, grid=(bricks // BLOCK,), out_shape=(jax.Sha...]
    ppermute x8 -> x24, starting transfers between devices: 21.6 us -> 82.9 us  [the longest x12 54.3 us: sides(): lax.ppermute(block, axis, backward)]
    ppermute x8 -> x24, waiting for transfers between devices: 50.3 us -> 6.97 us  [the longest x12 5.28 us: sides(): lax.ppermute(block, axis, forward)]
    concatenate x6 -> x0, other arithmetic: 30.4 us -> none  [the longest x2 16.9 us: fine_conv(): jnp.concatenate([field, cycle.reshape(9 * boundary, field.shape[1]), empt...]
  transfers between devices with their start and end apart: 10 -> 26, of which waited for: 10 -> 4; matrix products, arithmetic and copies ran while one was open for 3% -> 10% of each run, Pallas kernels for 0% -> 18%
where the time goes in v2:
time: 256 us; the launch traced here: 255 us
  Pallas kernels  114 us (45%)
  starting transfers between devices  101 us (39%)
  local copies, waits for them, and re-layouts  22.2 us (9%)
  waiting for transfers between devices  10.9 us (4%)
  matrix products  3.93 us (2%)
    ppermute x12, starting transfers between devices, sides(): lax.ppermute(block, axis, backward)  54.3 us
    pallas_call x1, Pallas kernels, encode(): pl.pallas_call(encode_kernel, grid=(bricks // BLOCK,), out_shape=(jax.Sha...  41.8 us
    pallas_call x1, Pallas kernels, raw_conv(): pl.pallas_call(raw_kernel, grid=(bricks // BLOCK,), out_shape=jax.ShapeDt...  37 us
    ppermute x12, starting transfers between devices, sides(): lax.ppermute(block, axis, forward)  28.7 us
    pallas_call x1, Pallas kernels, decode(): pl.pallas_call(decode_kernel, grid=(bricks // block,), out_shape=jax.Shap...  17.9 us
    all_to_all x2, starting transfers between devices, relay(): lax.all_to_all(buffer.reshape(devices, -1, 128), ('gz', 'gx'), split_axis...  17.8 us
    pallas_call x1, Pallas kernels, make_dense(): pl.pallas_call(dense_kernel, grid=(bricks // 16,), out_shape=jax.ShapeDty...  8.21 us
    reshape x1, local copies, waits for them, and re-layouts, on_device(): lift.astype(BF16).reshape(TAPS, chans, 8 * chans)  6.82 us
  transfers between devices with their start and end apart: 26, of which 4 were waited for; matrix products, arithmetic and copies ran while one was open for 10% of the time, Pallas kernels for 18%

profile of v2, /device:TPU:40, one launch (start us, length us, event | category | flops | bytes accessed | tf_op | source)
XLA Modules:
  0.0 254.8 jit_solution(10988165360341327227)
XLA Ops:
  0.7 8.2 %densify.1.own = bf16[192,3,16,128]{3,2,1,0:T(8,128)(2,1)} custom-call(s32[1]{0:T(128)} %bitcast.54.count, bf16[192,6144]{1,0:T(8,128)(2,1)} %bitcast.62), custom_call_target="tpu_custom_call" | custom-call | tf_op jit(solution)/shard_map/densify/pallas_call | solution.py:62
  9.0 1.9 slice.12
  10.9 3.8 %collective-permute-start = (bf16[48,3,16,128]{3,2,1,0:T(8,128)(2,1)}, bf16[48,3,16,128]{3,2,1,0:T(8,128)(2,1)S(1)}, u32[]{:S(2)}, u32[]{:S(2)}) collective-permute-start(bf16[48,3,16,128]{3,2,1,0:T(8,128)(2,1)} %slice.12), channel_id=1, source_target_pairs={{0,32},{32,64},{64,96},{1,33},{33,65},{65,97},{2,34},{34,66},{66,9... | collective-permute-start | bytes 1769480 | tf_op jit(solution)/shard_map/ppermute | solution.py:379
  14.7 2.0 collective-permute-start.5
  18.7 5.8 %collective-permute-start.4 = (bf16[48,3,16,128]{3,2,1,0:T(8,128)(2,1)}, bf16[48,3,16,128]{3,2,1,0:T(8,128)(2,1)S(1)}, u32[]{:S(2)}, u32[]{:S(2)}) collective-permute-start(bf16[48,3,16,128]{3,2,1,0:T(8,128)(2,1)} %slice.12), channel_id=1, source_target_pairs={{1,0},{2,1},{3,2},{4,3},{5,4},{6,5},{7,6},{8,7},{9,8},{10,9},{11,1... | collective-permute-start | bytes 1769480 | tf_op jit(solution)/shard_map/ppermute | solution.py:379
  24.5 3.6 %collective-permute-done.rest_1_ = bf16[48,3,16,128]{3,2,1,0:T(8,128)(2,1)S(1)} collective-permute-done((bf16[48,3,16,128]{3,2,1,0:T(8,128)(2,1)}, bf16[48,3,16,128]{3,2,1,0:T(8,128)(2,1)S(1)}, u32[]{:S(2)}, u32[]{:S(2)}) %collective-permute-start) | collective-permute-done | bytes 589856 | tf_op jit(solution)/shard_map/ppermute | solution.py:379
  30.0 5.8 %collective-permute-start.2 = (bf16[48,3,16,128]{3,2,1,0:T(8,128)(2,1)S(1)}, bf16[48,3,16,128]{3,2,1,0:T(8,128)(2,1)}, u32[]{:S(2)}, u32[]{:S(2)}) collective-permute-start(bf16[48,3,16,128]{3,2,1,0:T(8,128)(2,1)S(1)} %collective-permute-done.rest_1_), channel_id=1, source_target_pairs={{1,0},{2,1},{3,2},{4,3},{5,4},{6,5},{7,6},{8,7},{9,8},{10,9},{11,1... | collective-permute-start | bytes 1769480 | tf_op jit(solution)/shard_map/ppermute | solution.py:379
  37.7 5.8 %collective-permute-start.7 = (bf16[48,3,16,128]{3,2,1,0:T(8,128)(2,1)S(1)}, bf16[48,3,16,128]{3,2,1,0:T(8,128)(2,1)}, u32[]{:S(2)}, u32[]{:S(2)}) collective-permute-start(bf16[48,3,16,128]{3,2,1,0:T(8,128)(2,1)S(1)} %collective-permute-done.5.rest_6_), channel_id=1, source_target_pairs={{1,0},{2,1},{3,2},{4,3},{5,4},{6,5},{7,6},{8,7},{9,8},{10,9},{11,1... | collective-permute-start | bytes 1769480 | tf_op jit(solution)/shard_map/ppermute | solution.py:379
  50.9 41.8 %encode.1 = (bf16[192,3,16,128]{3,2,1,0:T(8,128)(2,1)}, bf16[384,8,128]{2,1,0:T(8,128)(2,1)}) custom-call(s32[5376]{0:T(1024)} %reshape.32.table, s32[1]{0:T(128)} %bitcast.55.count, s32[384]{0:T(512)} %select_reduce_fusion.send_slot, bf16[27,96,128]{2,1,0:T(8,128)(2,1)} %pad.31.w_ref, bf16[384,256]{1,0:T(8,128)(2,1)} %bitcast.65, ...), custom_call_target="tpu_custom_call" | custom-call | tf_op jit(solution)/shard_map/encode/pallas_call | solution.py:187
  92.7 11.1 %all-to-all-start = ((bf16[128,24,128]{2,1,0:T(8,128)(2,1)}), bf16[128,24,128]{2,1,0:T(8,128)(2,1)S(1)}, u32[]{:S(2)}, u32[]{:S(2)}) async-start(bf16[128,24,128]{2,1,0:T(8,128)(2,1)} %bitcast.63), calls=%async_computation | async-start | bytes 1572864 | tf_op jit(solution)/shard_map/all_to_all | solution.py:389
  103.9 2.0 slice.10
  105.8 3.6 %collective-permute-start.8 = (bf16[48,3,16,128]{3,2,1,0:T(8,128)(2,1)}, bf16[48,3,16,128]{3,2,1,0:T(8,128)(2,1)}, u32[]{:S(2)}, u32[]{:S(2)}) collective-permute-start(bf16[48,3,16,128]{3,2,1,0:T(8,128)(2,1)} %slice.10), channel_id=1, source_target_pairs={{0,32},{32,64},{64,96},{1,33},{33,65},{65,97},{2,34},{34,66},{66,9... | collective-permute-start | bytes 1769480 | tf_op jit(solution)/shard_map/ppermute | solution.py:379
  109.5 3.0 %collective-permute-start.13 = (bf16[48,3,16,128]{3,2,1,0:T(8,128)(2,1)}, bf16[48,3,16,128]{3,2,1,0:T(8,128)(2,1)}, u32[]{:S(2)}, u32[]{:S(2)}) collective-permute-start(bf16[48,3,16,128]{3,2,1,0:T(8,128)(2,1)} %slice.10), channel_id=1, source_target_pairs={{32,0},{64,32},{96,64},{33,1},{65,33},{97,65},{34,2},{66,34},{98,6... | collective-permute-start | bytes 1769480 | tf_op jit(solution)/shard_map/ppermute | solution.py:379
  114.8 3.9 %all-to-all-done = bf16[128,24,128]{2,1,0:T(8,128)(2,1)S(1)} async-done(((bf16[128,24,128]{2,1,0:T(8,128)(2,1)}), bf16[128,24,128]{2,1,0:T(8,128)(2,1)S(1)}, u32[]{:S(2)}, u32[]{:S(2)}) %all-to-all-start) | async-done | bytes 786464 | tf_op jit(solution)/shard_map/all_to_all | solution.py:389
  118.7 6.7 %coarse_mix.1 = bf16[384,8,128]{2,1,0:T(8,128)(2,1)} custom-call(s32[192]{0:T(256)S(1)} %select_reduce_fusion.1.from_slot, s32[384]{0:T(512)S(1)} %fusion.10.to_place, bf16[27,128,128]{2,1,0:T(8,128)(2,1)S(1)} %pad.30.w_ref, bf16[384,8,128]{2,1,0:T(8,128)(2,1)S(1)} %bitcast.58), custom_call_target="tpu_custom_call" | custom-call | tf_op jit(solution)/shard_map/coarse_mix/pallas_call | solution.py:282
  125.4 6.7 %all-to-all-start.1 = ((bf16[128,24,128]{2,1,0:T(8,128)(2,1)}), bf16[128,24,128]{2,1,0:T(8,128)(2,1)S(1)}, u32[]{:S(2)}, u32[]{:S(2)}) async-start(bf16[128,24,128]{2,1,0:T(8,128)(2,1)} %bitcast.14), calls=%async_computation.1 | async-start | bytes 1572864 | tf_op jit(solution)/shard_map/all_to_all | solution.py:389
  132.1 4.3 %collective-permute-start.12 = (bf16[48,3,16,128]{3,2,1,0:T(8,128)(2,1)}, bf16[48,3,16,128]{3,2,1,0:T(8,128)(2,1)S(1)}, u32[]{:S(2)}, u32[]{:S(2)}) collective-permute-start(bf16[48,3,16,128]{3,2,1,0:T(8,128)(2,1)} %slice.10), channel_id=1, source_target_pairs={{1,0},{2,1},{3,2},{4,3},{5,4},{6,5},{7,6},{8,7},{9,8},{10,9},{11,1... | collective-permute-start | bytes 1769480 | tf_op jit(solution)/shard_map/ppermute | solution.py:379
  136.5 2.3 collective-permute-start.10
  138.8 2.1 collective-permute-start.14
  141.1 5.6 %collective-permute-start.15 = (bf16[48,3,16,128]{3,2,1,0:T(8,128)(2,1)}, bf16[48,3,16,128]{3,2,1,0:T(8,128)(2,1)}, u32[]{:S(2)}, u32[]{:S(2)}) collective-permute-start(bf16[48,3,16,128]{3,2,1,0:T(8,128)(2,1)} %collective-permute-done.13.rest_6_), channel_id=1, source_target_pairs={{1,0},{2,1},{3,2},{4,3},{5,4},{6,5},{7,6},{8,7},{9,8},{10,9},{11,1... | collective-permute-start | bytes 1769480 | tf_op jit(solution)/shard_map/ppermute | solution.py:379
  150.1 2.3 take_back.1.own_ref
  153.4 3.6 %collective-permute-start.16 = (bf16[48,8,128]{2,1,0:T(8,128)(2,1)S(1)}, bf16[48,8,128]{2,1,0:T(8,128)(2,1)S(1)}, u32[]{:S(2)}, u32[]{:S(2)}) collective-permute-start(bf16[48,8,128]{2,1,0:T(8,128)(2,1)S(1)} %slice.13), channel_id=1, source_target_pairs={{0,32},{32,64},{64,96},{1,33},{33,65},{65,97},{2,34},{34,66},{66,9... | collective-permute-start | bytes 294920 | tf_op jit(solution)/shard_map/ppermute | solution.py:379
  157.0 2.2 collective-permute-start.21
  159.3 2.1 collective-permute-start.19
  161.4 3.9 %convolution_convert_fusion = bf16[27,96,96,8]{2,1,3,0:T(8,128)(2,1)} fusion(bf16[27,96,96]{2,1,0:T(8,128)(2,1)S(1)} %copy-done.4, bf16[96,8,96]{2,1,0:T(8,128)(2,1)S(1)} %reshape.33), kind=kOutput, calls=%fused_computation | convolution fusion | flops 384196608 | bytes 4626432 | tf_op jit(solution)/shard_map/cse,ked->kcsd/dot_general | solution.py:439
  166.3 6.8 %copy.23 = bf16[27,96,768]{2,1,0:T(8,128)(2,1)} copy(bf16[27,96,768]{1,2,0:T(8,128)(2,1)} %bitcast.60) | data formatting | bytes 7962624 | tf_op jit(solution)/shard_map/reshape | solution.py:442
  173.1 5.2 %pad.28 = bf16[28,128,768]{2,1,0:T(8,128)(2,1)} pad(bf16[27,96,768]{2,1,0:T(8,128)(2,1)} %copy.23, bf16[]{:T(256)} %constant.57.clone.1), padding=0_1x0_32x0_0 | pad | bytes 9486338 | tf_op jit(solution)/shard_map/jit(_pad)/pad | solution.py:442
  178.3 6.0 %collective-permute-start.20 = (bf16[48,8,128]{2,1,0:T(8,128)(2,1)S(1)}, bf16[48,8,128]{2,1,0:T(8,128)(2,1)S(1)}, u32[]{:S(2)}, u32[]{:S(2)}) collective-permute-start(bf16[48,8,128]{2,1,0:T(8,128)(2,1)S(1)} %slice.13), channel_id=1, source_target_pairs={{1,0},{2,1},{3,2},{4,3},{5,4},{6,5},{7,6},{8,7},{9,8},{10,9},{11,1... | collective-permute-start | bytes 294920 | tf_op jit(solution)/shard_map/ppermute | solution.py:379
  186.3 5.8 %collective-permute-start.18 = (bf16[48,8,128]{2,1,0:T(8,128)(2,1)S(1)}, bf16[48,8,128]{2,1,0:T(8,128)(2,1)S(1)}, u32[]{:S(2)}, u32[]{:S(2)}) collective-permute-start(bf16[48,8,128]{2,1,0:T(8,128)(2,1)S(1)} %collective-permute-done.16.rest_1_), channel_id=1, source_target_pairs={{1,0},{2,1},{3,2},{4,3},{5,4},{6,5},{7,6},{8,7},{9,8},{10,9},{11,1... | collective-permute-start | bytes 294920 | tf_op jit(solution)/shard_map/ppermute | solution.py:379
  194.0 5.8 %collective-permute-start.23 = (bf16[48,8,128]{2,1,0:T(8,128)(2,1)S(1)}, bf16[48,8,128]{2,1,0:T(8,128)(2,1)S(1)}, u32[]{:S(2)}, u32[]{:S(2)}) collective-permute-start(bf16[48,8,128]{2,1,0:T(8,128)(2,1)S(1)} %collective-permute-done.21.rest_6_), channel_id=1, source_target_pairs={{1,0},{2,1},{3,2},{4,3},{5,4},{6,5},{7,6},{8,7},{9,8},{10,9},{11,1... | collective-permute-start | bytes 294920 | tf_op jit(solution)/shard_map/ppermute | solution.py:379
  199.8 37.0 %raw_conv.1.raw_ref = f32[192,3,16,128]{3,2,1,0:T(8,128)} custom-call(s32[5376]{0:T(1024)} %reshape.32.table, bf16[27,96,128]{2,1,0:T(8,128)(2,1)} %pad.33.w_ref, bf16[192,3,16,128]{3,2,1,0:T(8,128)(2,1)} %get-tuple-element.8.own.enc_ref, bf16[48,3,16,128]{3,2,1,0:T(8,128)(2,1)} %collective-permute-done.9.rest_0_, ...), custom_call_target="tpu_custom_call" | custom-call | flops 40000000000 | bytes 13000000 | tf_op jit(solution)/shard_map/raw_conv/pallas_call | solution.py:220
  236.9 17.9 %decode.1 = bf16[192,6144]{1,0:T(8,128)(2,1)} custom-call(s32[5376]{0:T(1024)S(1)} %copy-done.2, s32[1]{0:T(128)} %bitcast.57.count, bf16[3584,768]{1,0:T(8,128)(2,1)} %bitcast.59, bf16[128,768]{1,0:T(8,128)(2,1)S(1)} %pad.29.up_ref, bf16[192,8,128]{2,1,0:T(8,128)(2,1)S(1)} %copy-done.1, f32[192,3,16,128]{3,2,1,0:T(8,128)} %raw_conv.1.raw_ref, ...), custom_call_target="tpu_custom_call" | custom-call | tf_op jit(solution)/shard_map/decode/pallas_call | solution.py:362
  (88 shorter events, 24.8 us)
Async XLA Ops:
  10.9 17.2 %collective-permute-start = (bf16[48,3,16,128]{3,2,1,0:T(8,128)(2,1)}, bf16[48,3,16,128]{3,2,1,0:T(8,128)(2,1)S(1)}, u32[]{:S(2)}, u32[]{:S(2)}) collective-permute-start(bf16[48,3,16,128]{3,2,1,0:T(8,128)(2,1)} %slice.12), channel_id=1, source_target_pairs={{0,32},{32,64},{64,96},{1,33},{33,65},{65,97},{2,34},{34,66},{66,9... | collective-permute-start | bytes 1769480 | tf_op jit(solution)/shard_map/ppermute | solution.py:379
  14.7 21.0 %collective-permute-start.5 = (bf16[48,3,16,128]{3,2,1,0:T(8,128)(2,1)}, bf16[48,3,16,128]{3,2,1,0:T(8,128)(2,1)S(1)}, u32[]{:S(2)}, u32[]{:S(2)}) collective-permute-start(bf16[48,3,16,128]{3,2,1,0:T(8,128)(2,1)} %slice.12), channel_id=1, source_target_pairs={{32,0},{64,32},{96,64},{33,1},{65,33},{97,65},{34,2},{66,34},{98,6... | collective-permute-start | bytes 1769480 | tf_op jit(solution)/shard_map/ppermute | solution.py:379
  16.8 20.9 %collective-permute-start.3 = (bf16[48,3,16,128]{3,2,1,0:T(8,128)(2,1)}, bf16[48,3,16,128]{3,2,1,0:T(8,128)(2,1)}, u32[]{:S(2)}, u32[]{:S(2)}) collective-permute-start(bf16[48,3,16,128]{3,2,1,0:T(8,128)(2,1)} %slice.12), channel_id=1, source_target_pairs={{0,1},{1,2},{2,3},{3,4},{4,5},{5,6},{6,7},{7,8},{8,9},{9,10},{10,1... | collective-permute-start | bytes 1769480 | tf_op jit(solution)/shard_map/ppermute | solution.py:379
  18.7 28.8 %collective-permute-start.4 = (bf16[48,3,16,128]{3,2,1,0:T(8,128)(2,1)}, bf16[48,3,16,128]{3,2,1,0:T(8,128)(2,1)S(1)}, u32[]{:S(2)}, u32[]{:S(2)}) collective-permute-start(bf16[48,3,16,128]{3,2,1,0:T(8,128)(2,1)} %slice.12), channel_id=1, source_target_pairs={{1,0},{2,1},{3,2},{4,3},{5,4},{6,5},{7,6},{8,7},{9,8},{10,9},{11,1... | collective-permute-start | bytes 1769480 | tf_op jit(solution)/shard_map/ppermute | solution.py:379
  28.1 19.4 %collective-permute-start.1 = (bf16[48,3,16,128]{3,2,1,0:T(8,128)(2,1)S(1)}, bf16[48,3,16,128]{3,2,1,0:T(8,128)(2,1)S(1)}, u32[]{:S(2)}, u32[]{:S(2)}) collective-permute-start(bf16[48,3,16,128]{3,2,1,0:T(8,128)(2,1)S(1)} %collective-permute-done.rest_1_), channel_id=1, source_target_pairs={{0,1},{1,2},{2,3},{3,4},{4,5},{5,6},{6,7},{7,8},{8,9},{9,10},{10,1... | collective-permute-start | bytes 1769480 | tf_op jit(solution)/shard_map/ppermute | solution.py:379
  30.0 17.5 %collective-permute-start.2 = (bf16[48,3,16,128]{3,2,1,0:T(8,128)(2,1)S(1)}, bf16[48,3,16,128]{3,2,1,0:T(8,128)(2,1)}, u32[]{:S(2)}, u32[]{:S(2)}) collective-permute-start(bf16[48,3,16,128]{3,2,1,0:T(8,128)(2,1)S(1)} %collective-permute-done.rest_1_), channel_id=1, source_target_pairs={{1,0},{2,1},{3,2},{4,3},{5,4},{6,5},{7,6},{8,7},{9,8},{10,9},{11,1... | collective-permute-start | bytes 1769480 | tf_op jit(solution)/shard_map/ppermute | solution.py:379
  35.8 13.4 %collective-permute-start.6 = (bf16[48,3,16,128]{3,2,1,0:T(8,128)(2,1)S(1)}, bf16[48,3,16,128]{3,2,1,0:T(8,128)(2,1)}, u32[]{:S(2)}, u32[]{:S(2)}) collective-permute-start(bf16[48,3,16,128]{3,2,1,0:T(8,128)(2,1)S(1)} %collective-permute-done.5.rest_6_), channel_id=1, source_target_pairs={{0,1},{1,2},{2,3},{3,4},{4,5},{5,6},{6,7},{7,8},{8,9},{9,10},{10,1... | collective-permute-start | bytes 1769480 | tf_op jit(solution)/shard_map/ppermute | solution.py:379
  37.7 13.1 %collective-permute-start.7 = (bf16[48,3,16,128]{3,2,1,0:T(8,128)(2,1)S(1)}, bf16[48,3,16,128]{3,2,1,0:T(8,128)(2,1)}, u32[]{:S(2)}, u32[]{:S(2)}) collective-permute-start(bf16[48,3,16,128]{3,2,1,0:T(8,128)(2,1)S(1)} %collective-permute-done.5.rest_6_), channel_id=1, source_target_pairs={{1,0},{2,1},{3,2},{4,3},{5,4},{6,5},{7,6},{8,7},{9,8},{10,9},{11,1... | collective-permute-start | bytes 1769480 | tf_op jit(solution)/shard_map/ppermute | solution.py:379
  50.8 61.6 %copy-start.15 = (s32[1,384]{1,0:T(1,128)S(1)}, s32[1,384]{1,0:T(1,128)}, u32[]{:S(2)}) copy-start(s32[1,384]{1,0:T(1,128)} %param.14) | copy-start | bytes 4612
  50.9 63.7 %copy-start.6 = (bf16[27,96,96]{2,1,0:T(8,128)(2,1)S(1)}, bf16[27,96,96]{2,1,0:T(8,128)(2,1)}, u32[]{:S(2)}) copy-start(bf16[27,96,96]{2,1,0:T(8,128)(2,1)} %param.17) | copy-start | bytes 1492996
  92.7 68.7 %copy-start.4 = (bf16[27,96,96]{2,1,0:T(8,128)(2,1)S(1)}, bf16[27,96,96]{2,1,0:T(8,128)(2,1)}, u32[]{:S(2)}) copy-start(bf16[27,96,96]{2,1,0:T(8,128)(2,1)} %param.19) | copy-start | bytes 1492996
  92.7 26.0 %all-to-all-start = ((bf16[128,24,128]{2,1,0:T(8,128)(2,1)}), bf16[128,24,128]{2,1,0:T(8,128)(2,1)S(1)}, u32[]{:S(2)}, u32[]{:S(2)}) async-start(bf16[128,24,128]{2,1,0:T(8,128)(2,1)} %bitcast.63), calls=%async_computation | async-start | bytes 1572864 | tf_op jit(solution)/shard_map/all_to_all | solution.py:389
  105.8 30.6 %collective-permute-start.8 = (bf16[48,3,16,128]{3,2,1,0:T(8,128)(2,1)}, bf16[48,3,16,128]{3,2,1,0:T(8,128)(2,1)}, u32[]{:S(2)}, u32[]{:S(2)}) collective-permute-start(bf16[48,3,16,128]{3,2,1,0:T(8,128)(2,1)} %slice.10), channel_id=1, source_target_pairs={{0,32},{32,64},{64,96},{1,33},{33,65},{65,97},{2,34},{34,66},{66,9... | collective-permute-start | bytes 1769480 | tf_op jit(solution)/shard_map/ppermute | solution.py:379
  109.5 29.3 %collective-permute-start.13 = (bf16[48,3,16,128]{3,2,1,0:T(8,128)(2,1)}, bf16[48,3,16,128]{3,2,1,0:T(8,128)(2,1)}, u32[]{:S(2)}, u32[]{:S(2)}) collective-permute-start(bf16[48,3,16,128]{3,2,1,0:T(8,128)(2,1)} %slice.10), channel_id=1, source_target_pairs={{32,0},{64,32},{96,64},{33,1},{65,33},{97,65},{34,2},{66,34},{98,6... | collective-permute-start | bytes 1769480 | tf_op jit(solution)/shard_map/ppermute | solution.py:379
  112.6 34.2 %collective-permute-start.11 = (bf16[48,3,16,128]{3,2,1,0:T(8,128)(2,1)}, bf16[48,3,16,128]{3,2,1,0:T(8,128)(2,1)}, u32[]{:S(2)}, u32[]{:S(2)}) collective-permute-start(bf16[48,3,16,128]{3,2,1,0:T(8,128)(2,1)} %slice.10), channel_id=1, source_target_pairs={{0,1},{1,2},{2,3},{3,4},{4,5},{5,6},{6,7},{7,8},{8,9},{9,10},{10,1... | collective-permute-start | bytes 1769480 | tf_op jit(solution)/shard_map/ppermute | solution.py:379
  125.4 23.8 %all-to-all-start.1 = ((bf16[128,24,128]{2,1,0:T(8,128)(2,1)}), bf16[128,24,128]{2,1,0:T(8,128)(2,1)S(1)}, u32[]{:S(2)}, u32[]{:S(2)}) async-start(bf16[128,24,128]{2,1,0:T(8,128)(2,1)} %bitcast.14), calls=%async_computation.1 | async-start | bytes 1572864 | tf_op jit(solution)/shard_map/all_to_all | solution.py:389
  132.1 21.2 %collective-permute-start.12 = (bf16[48,3,16,128]{3,2,1,0:T(8,128)(2,1)}, bf16[48,3,16,128]{3,2,1,0:T(8,128)(2,1)S(1)}, u32[]{:S(2)}, u32[]{:S(2)}) collective-permute-start(bf16[48,3,16,128]{3,2,1,0:T(8,128)(2,1)} %slice.10), channel_id=1, source_target_pairs={{1,0},{2,1},{3,2},{4,3},{5,4},{6,5},{7,6},{8,7},{9,8},{10,9},{11,1... | collective-permute-start | bytes 1769480 | tf_op jit(solution)/shard_map/ppermute | solution.py:379
  136.5 20.6 %collective-permute-start.10 = (bf16[48,3,16,128]{3,2,1,0:T(8,128)(2,1)}, bf16[48,3,16,128]{3,2,1,0:T(8,128)(2,1)S(1)}, u32[]{:S(2)}, u32[]{:S(2)}) collective-permute-start(bf16[48,3,16,128]{3,2,1,0:T(8,128)(2,1)} %collective-permute-done.8.rest_1_), channel_id=1, source_target_pairs={{1,0},{2,1},{3,2},{4,3},{5,4},{6,5},{7,6},{8,7},{9,8},{10,9},{11,1... | collective-permute-start | bytes 1769480 | tf_op jit(solution)/shard_map/ppermute | solution.py:379
  138.8 20.5 %collective-permute-start.14 = (bf16[48,3,16,128]{3,2,1,0:T(8,128)(2,1)}, bf16[48,3,16,128]{3,2,1,0:T(8,128)(2,1)}, u32[]{:S(2)}, u32[]{:S(2)}) collective-permute-start(bf16[48,3,16,128]{3,2,1,0:T(8,128)(2,1)} %collective-permute-done.13.rest_6_), channel_id=1, source_target_pairs={{0,1},{1,2},{2,3},{3,4},{4,5},{5,6},{6,7},{7,8},{8,9},{9,10},{10,1... | collective-permute-start | bytes 1769480 | tf_op jit(solution)/shard_map/ppermute | solution.py:379
  141.1 37.2 %collective-permute-start.15 = (bf16[48,3,16,128]{3,2,1,0:T(8,128)(2,1)}, bf16[48,3,16,128]{3,2,1,0:T(8,128)(2,1)}, u32[]{:S(2)}, u32[]{:S(2)}) collective-permute-start(bf16[48,3,16,128]{3,2,1,0:T(8,128)(2,1)} %collective-permute-done.13.rest_6_), channel_id=1, source_target_pairs={{1,0},{2,1},{3,2},{4,3},{5,4},{6,5},{7,6},{8,7},{9,8},{10,9},{11,1... | collective-permute-start | bytes 1769480 | tf_op jit(solution)/shard_map/ppermute | solution.py:379
  146.7 39.6 %collective-permute-start.9 = (bf16[48,3,16,128]{3,2,1,0:T(8,128)(2,1)}, bf16[48,3,16,128]{3,2,1,0:T(8,128)(2,1)}, u32[]{:S(2)}, u32[]{:S(2)}) collective-permute-start(bf16[48,3,16,128]{3,2,1,0:T(8,128)(2,1)} %collective-permute-done.8.rest_1_), channel_id=1, source_target_pairs={{0,1},{1,2},{2,3},{3,4},{4,5},{5,6},{6,7},{7,8},{8,9},{9,10},{10,1... | collective-permute-start | bytes 1769480 | tf_op jit(solution)/shard_map/ppermute | solution.py:379
  153.4 31.0 %collective-permute-start.16 = (bf16[48,8,128]{2,1,0:T(8,128)(2,1)S(1)}, bf16[48,8,128]{2,1,0:T(8,128)(2,1)S(1)}, u32[]{:S(2)}, u32[]{:S(2)}) collective-permute-start(bf16[48,8,128]{2,1,0:T(8,128)(2,1)S(1)} %slice.13), channel_id=1, source_target_pairs={{0,32},{32,64},{64,96},{1,33},{33,65},{65,97},{2,34},{34,66},{66,9... | collective-permute-start | bytes 294920 | tf_op jit(solution)/shard_map/ppermute | solution.py:379
  157.0 35.0 %collective-permute-start.21 = (bf16[48,8,128]{2,1,0:T(8,128)(2,1)S(1)}, bf16[48,8,128]{2,1,0:T(8,128)(2,1)S(1)}, u32[]{:S(2)}, u32[]{:S(2)}) collective-permute-start(bf16[48,8,128]{2,1,0:T(8,128)(2,1)S(1)} %slice.13), channel_id=1, source_target_pairs={{32,0},{64,32},{96,64},{33,1},{65,33},{97,65},{34,2},{66,34},{98,6... | collective-permute-start | bytes 294920 | tf_op jit(solution)/shard_map/ppermute | solution.py:379
  159.3 34.7 %collective-permute-start.19 = (bf16[48,8,128]{2,1,0:T(8,128)(2,1)S(1)}, bf16[48,8,128]{2,1,0:T(8,128)(2,1)S(1)}, u32[]{:S(2)}, u32[]{:S(2)}) collective-permute-start(bf16[48,8,128]{2,1,0:T(8,128)(2,1)S(1)} %slice.13), channel_id=1, source_target_pairs={{0,1},{1,2},{2,3},{3,4},{4,5},{5,6},{6,7},{7,8},{8,9},{9,10},{10,1... | collective-permute-start | bytes 294920 | tf_op jit(solution)/shard_map/ppermute | solution.py:379
  178.3 58.5 %copy-start = (bf16[192,3,16,128]{3,2,1,0:T(8,128)(2,1)S(1)}, bf16[192,3,16,128]{3,2,1,0:T(8,128)(2,1)}, u32[]{:S(2)}) copy-start(bf16[192,3,16,128]{3,2,1,0:T(8,128)(2,1)} %get-tuple-element.8.own.enc_ref) | copy-start | bytes 7077892
  178.3 58.6 %copy-start.1 = (bf16[192,8,128]{2,1,0:T(8,128)(2,1)S(1)}, bf16[192,8,128]{2,1,0:T(8,128)(2,1)}, u32[]{:S(2)}) copy-start(bf16[192,8,128]{2,1,0:T(8,128)(2,1)} %take_back.1.own_ref) | copy-start | bytes 1179652
  178.3 58.6 %copy-start.2 = (s32[5376]{0:T(1024)S(1)}, s32[5376]{0:T(1024)}, u32[]{:S(2)}) copy-start(s32[5376]{0:T(1024)} %reshape.32.table) | copy-start | bytes 64516
  178.3 58.5 %collective-permute-start.20 = (bf16[48,8,128]{2,1,0:T(8,128)(2,1)S(1)}, bf16[48,8,128]{2,1,0:T(8,128)(2,1)S(1)}, u32[]{:S(2)}, u32[]{:S(2)}) collective-permute-start(bf16[48,8,128]{2,1,0:T(8,128)(2,1)S(1)} %slice.13), channel_id=1, source_target_pairs={{1,0},{2,1},{3,2},{4,3},{5,4},{6,5},{7,6},{8,7},{9,8},{10,9},{11,1... | collective-permute-start | bytes 294920 | tf_op jit(solution)/shard_map/ppermute | solution.py:379
  184.4 52.5 %collective-permute-start.17 = (bf16[48,8,128]{2,1,0:T(8,128)(2,1)S(1)}, bf16[48,8,128]{2,1,0:T(8,128)(2,1)S(1)}, u32[]{:S(2)}, u32[]{:S(2)}) collective-permute-start(bf16[48,8,128]{2,1,0:T(8,128)(2,1)S(1)} %collective-permute-done.16.rest_1_), channel_id=1, source_target_pairs={{0,1},{1,2},{2,3},{3,4},{4,5},{5,6},{6,7},{7,8},{8,9},{9,10},{10,1... | collective-permute-start | bytes 294920 | tf_op jit(solution)/shard_map/ppermute | solution.py:379
  186.3 50.5 %collective-permute-start.18 = (bf16[48,8,128]{2,1,0:T(8,128)(2,1)S(1)}, bf16[48,8,128]{2,1,0:T(8,128)(2,1)S(1)}, u32[]{:S(2)}, u32[]{:S(2)}) collective-permute-start(bf16[48,8,128]{2,1,0:T(8,128)(2,1)S(1)} %collective-permute-done.16.rest_1_), channel_id=1, source_target_pairs={{1,0},{2,1},{3,2},{4,3},{5,4},{6,5},{7,6},{8,7},{9,8},{10,9},{11,1... | collective-permute-start | bytes 294920 | tf_op jit(solution)/shard_map/ppermute | solution.py:379
  192.1 44.8 %collective-permute-start.22 = (bf16[48,8,128]{2,1,0:T(8,128)(2,1)S(1)}, bf16[48,8,128]{2,1,0:T(8,128)(2,1)S(1)}, u32[]{:S(2)}, u32[]{:S(2)}) collective-permute-start(bf16[48,8,128]{2,1,0:T(8,128)(2,1)S(1)} %collective-permute-done.21.rest_6_), channel_id=1, source_target_pairs={{0,1},{1,2},{2,3},{3,4},{4,5},{5,6},{6,7},{7,8},{8,9},{9,10},{10,1... | collective-permute-start | bytes 294920 | tf_op jit(solution)/shard_map/ppermute | solution.py:379
  194.0 42.8 %collective-permute-start.23 = (bf16[48,8,128]{2,1,0:T(8,128)(2,1)S(1)}, bf16[48,8,128]{2,1,0:T(8,128)(2,1)S(1)}, u32[]{:S(2)}, u32[]{:S(2)}) collective-permute-start(bf16[48,8,128]{2,1,0:T(8,128)(2,1)S(1)} %collective-permute-done.21.rest_6_), channel_id=1, source_target_pairs={{1,0},{2,1},{3,2},{4,3},{5,4},{6,5},{7,6},{8,7},{9,8},{10,9},{11,1... | collective-permute-start | bytes 294920 | tf_op jit(solution)/shard_map/ppermute | solution.py:379
  (12 other events, 309.4 us)

commit v3 on v2

--- a/solution.py
+++ b/solution.py
@@ -49,24 +49,95 @@
     return jnp.concatenate([y for x in out for y in x], axis=1)
 
 
-def dense_kernel(count, x_ref, o_ref):
-    first = pl.program_id(0) * 16
-    rows = lax.broadcasted_iota(jnp.int32, x_ref.shape, 0) + first
-    x = jnp.where(rows < count[0], x_ref[...], jnp.zeros((), BF16))
-    for t, y in enumerate(to_dense(x)):
-        o_ref[:, t] = y
-
-
-def make_dense(count, x):
-    bricks = x.shape[0]
-    return pl.pallas_call(
-        dense_kernel,
-        grid=(bricks // 16,),
-        out_shape=jax.ShapeDtypeStruct((bricks, 3, 16, 128), BF16),
-        in_specs=[pl.BlockSpec(memory_space=pltpu.SMEM), pl.BlockSpec((16, x.shape[1]), lambda i: (i, 0))],
-        out_specs=pl.BlockSpec((16, 3, 16, 128), lambda i: (i, 0, 0, 0)),
-        name="densify",
-    )(count, x)
+OFFSETS = tuple((dz, dx) for dz in (-1, 0, 1) for dx in (-1, 0, 1) if (dz, dx) != (0, 0))
+MESH = pl.DeviceIdType.MESH
+
+
+class Exchange:
+    def __init__(self, own, landing, send, recv, chunks):
+        self.own, self.landing, self.send, self.recv, self.chunks = own, landing, send, recv, chunks
+        self.z, self.x = lax.axis_index("gz"), lax.axis_index("gx")
+        self.layers, self.slabs = lax.axis_size("gz"), lax.axis_size("gx")
+
+    def has(self, dz, dx):
+        checks = []
+        if dz:
+            checks.append(self.z > 0 if dz < 0 else self.z < self.layers - 1)
+        if dx:
+            checks.append(self.x > 0 if dx < 0 else self.x < self.slabs - 1)
+        return checks[0] if len(checks) == 1 else jnp.logical_and(*checks)
+
+    def sends(self, slot):
+        dz, dx = OFFSETS[slot]
+        if dz and dx:
+            sides = [self.z > 0 if dz < 0 else self.z < self.layers - 1]
+            sides.append(self.x < self.slabs - 1 if dx < 0 else self.x > 0)
+            return jnp.logical_and(*sides)
+        return self.has(-dz, -dx)
+
+    def copy(self, slot, c):
+        dz, dx = OFFSETS[slot]
+        if dz and dx:
+            source, target = self.landing(OFFSETS.index((dz, 0)), c), (self.z, self.x - dx)
+        else:
+            source, target = self.own(c), (self.z - dz, self.x - dx)
+        return pltpu.make_async_remote_copy(
+            src_ref=source,
+            dst_ref=self.landing(slot, c),
+            send_sem=self.send.at[slot, c],
+            recv_sem=self.recv.at[slot, c],
+            device_id=target,
+            device_id_type=MESH,
+        )
+
+    def greet(self):
+        barrier = pltpu.get_barrier_semaphore()
+        for dz, dx in ((-1, 0), (1, 0), (0, -1), (0, 1)):
+
+            @pl.when(self.has(dz, dx))
+            def _():
+                pl.semaphore_signal(
+                    barrier, inc=1, device_id=(self.z + dz, self.x + dx), device_id_type=MESH
+                )
+
+    def meet(self):
+        peers = sum(self.has(dz, dx).astype(jnp.int32) for dz, dx in ((-1, 0), (1, 0), (0, -1), (0, 1)))
+        pl.semaphore_wait(pltpu.get_barrier_semaphore(), peers)
+
+    def start(self):
+        for c in range(self.chunks):
+            for slot in (1, 6, 3, 4):
+
+                @pl.when(self.sends(slot))
+                def _():
+                    self.copy(slot, c).start()
+
+    def forward(self, c):
+        for slot, corners in ((1, (0, 2)), (6, (5, 7))):
+
+            @pl.when(self.has(*OFFSETS[slot]))
+            def _():
+                self.copy(slot, c).wait_recv()
+
+            for corner in corners:
+
+                @pl.when(self.sends(corner))
+                def _():
+                    self.copy(corner, c).start()
+
+    def arrive(self, slot):
+        @pl.when(self.has(*OFFSETS[slot]))
+        def _():
+            for c in range(self.chunks):
+                self.copy(slot, c).wait_recv()
+
+    def finish(self):
+        for slot in range(8):
+
+            @pl.when(self.sends(slot))
+            def _():
+                for c in range(self.chunks):
+                    self.copy(slot, c).wait_send()
 
 
 def rotate_range(rot, start, stop):
@@ -120,33 +191,70 @@
     return (jnp.where(lanes < 96, acc[0], r1), jnp.where(lanes < 64, r1, r2), jnp.where(lanes < 32, r2, r3))
 
 
-def load_field(own, halos, rot, sems):
-    bricks = own.shape[0]
-    part = halos[0].shape[0]
-    total = bricks + len(halos) * part
-    copies = [pltpu.make_async_copy(own, rot.at[0, pl.ds(0, bricks)], sems.at[0])]
-    for d, piece in enumerate(halos):
-        copies.append(pltpu.make_async_copy(piece, rot.at[0, pl.ds(bricks + d * part, part)], sems.at[d + 1]))
-    for copy in copies:
-        copy.start()
-    for j in range(4):
-        rot[j, total] = jnp.zeros((3, 16, 128), BF16)
-    copies[0].wait()
-    rotate_range(rot, 0, bricks)
-    for copy in copies[1:]:
-        copy.wait()
-    rotate_range(rot, bricks, total)
-
-
-def encode_kernel(table, count, send_slot, w_ref, wd_ref, own, *rest):
-    halos, (enc_ref, out_ref, rot, pooled, sems) = rest[:8], rest[8:]
+def encode_kernel(
+    parts, table, count, send_slot, w_ref, wd_ref, x_ref,
+    enc_ref, out_ref, halo_ref, rot, pooled, face, sends, recvs, sends2, recvs2,
+):
     step = pl.program_id(0)
-    bricks = own.shape[0]
+    bricks = x_ref.shape[0]
+    part = bricks // 4
+    size = part // parts
+    total = bricks + 8 * part
+    first = Exchange(
+        lambda c: rot.at[0, pl.ds(c * size, size)],
+        lambda slot, c: rot.at[0, pl.ds(bricks + slot * part + c * size, size)],
+        sends, recvs, parts,
+    )
+    second = Exchange(
+        lambda c: face.at[pl.ds(c * size, size)],
+        lambda slot, c: halo_ref.at[slot, pl.ds(c * size, size)],
+        sends2, recvs2, parts,
+    )
+
+    def fill(slot):
+        begin = bricks + slot * part
+        first.arrive(slot) if OFFSETS[slot][1] else None
+
+        @pl.when(jnp.logical_not(first.has(*OFFSETS[slot])))
+        def _():
+            def clear(n, carry):
+                rot[0, begin + n] = jnp.zeros((3, 16, 128), BF16)
+                return carry
+
+            lax.fori_loop(0, part, clear, 0)
+
+        rotate_range(rot, begin, begin + part)
+
+    def densify(start, stop):
+        def body(m, carry):
+            begin = pl.multiple_of(m * 16, 16)
+            x = x_ref[pl.ds(begin, 16)]
+            live = lax.broadcasted_iota(jnp.int32, x.shape, 0) + begin < count[0]
+            for t, y in enumerate(to_dense(jnp.where(live, x, jnp.zeros((), BF16)))):
+                rot[0, pl.ds(begin, 16), t] = y
+            return carry
+
+        lax.fori_loop(start // 16, stop // 16, body, 0)
 
     @pl.when(step == 0)
     def _():
-        load_field(own, halos, rot, sems)
+        first.greet()
+        densify(0, part)
+        first.meet()
+        first.start()
+        for j in range(4):
+            rot[j, total] = jnp.zeros((3, 16, 128), BF16)
         pooled[bricks] = jnp.zeros((8, 128), F32)
+        densify(part, bricks)
+        first.forward(0)
+        rotate_range(rot, 0, bricks)
+        first.forward(1)
+        fill(3)
+        fill(4)
+        first.forward(2)
+        for slot in (1, 6, 0, 2, 5, 7):
+            fill(slot)
+        first.finish()
 
     tiles = conv_block(step, table, w_ref, rot)
     shape = tiles[0].shape
@@ -162,6 +270,21 @@
     sums = sums[:, :8, :128] + sums[:, 8:, 128:]
     pooled[pl.ds(step * BLOCK, BLOCK)] = sums
 
+    @pl.when(step == 0)
+    def _():
+        face[pl.ds(0, BLOCK)] = enc_ref[...]
+
+    @pl.when(step == 1)
+    def _():
+        face[pl.ds(BLOCK, part - BLOCK)] = enc_ref[: part - BLOCK]
+        second.start()
+
+    for c in range(parts):
+
+        @pl.when(step == c + 2)
+        def _():
+            second.forward(c)
+
     @pl.when(step == pl.num_programs(0) - 1)
     def _():
         def place(s, carry):
@@ -169,6 +292,9 @@
             return carry
 
         lax.fori_loop(0, out_ref.shape[0], place, 0, unroll=8)
+        for slot in (0, 2, 3, 4, 5, 7):
+            second.arrive(slot)
+        second.finish()
 
 
 def field_scratch(own, halos):
@@ -181,35 +307,75 @@
 ANY = pl.BlockSpec(memory_space=pl.ANY)
 
 
-def encode(table, count, send_slot, w, wd, own, halos):
-    bricks = own.shape[0]
+def encode(table, count, send_slot, w, wd, x):
+    bricks = x.shape[0]
+    part = bricks // 4
     slots = send_slot.shape[0]
+    parts = 3
+    sems = pltpu.SemaphoreType.DMA((8, parts))
     return pl.pallas_call(
-        encode_kernel,
+        functools.partial(encode_kernel, parts),
         grid=(bricks // BLOCK,),
         out_shape=(
             jax.ShapeDtypeStruct((bricks, 3, 16, 128), BF16),
             jax.ShapeDtypeStruct((slots, 8, 128), BF16),
+            jax.ShapeDtypeStruct((8, part, 3, 16, 128), BF16),
         ),
-        in_specs=[SMEM, SMEM, SMEM, VMEM, VMEM, ANY] + [ANY] * len(halos),
-        out_specs=(pl.BlockSpec((BLOCK, 3, 16, 128), lambda i: (i, 0, 0, 0)), VMEM),
+        in_specs=[SMEM, SMEM, SMEM, VMEM, VMEM, VMEM],
+        out_specs=(pl.BlockSpec((BLOCK, 3, 16, 128), lambda i: (i, 0, 0, 0)), VMEM, ANY),
         scratch_shapes=[
-            field_scratch(own, halos),
+            pltpu.VMEM((4, bricks + 8 * part + 1, 3, 16, 128), BF16),
             pltpu.VMEM((bricks + 1, 8, 128), F32),
-            pltpu.SemaphoreType.DMA((9,)),
+            pltpu.VMEM((part, 3, 16, 128), BF16),
+            sems, sems, sems, sems,
         ],
-        compiler_params=pltpu.CompilerParams(vmem_limit_bytes=56 * MIB),
+        compiler_params=pltpu.CompilerParams(
+            vmem_limit_bytes=56 * MIB, collective_id=1, has_side_effects=True
+        ),
         name="encode",
-    )(table, count, send_slot, w, wd, own, *halos)
-
-
-def raw_kernel(table, w_ref, own, *rest):
-    halos, (out_ref, rot, sems) = rest[:8], rest[8:]
+    )(table, count, send_slot, w, wd, x)
+
+
+def raw_kernel(table, w_ref, own, halo_ref, out_ref, rot, sems):
     step = pl.program_id(0)
+    bricks = own.shape[0]
+    part = halo_ref.shape[1]
+    total = bricks + 8 * part
+    side = Exchange(None, None, None, None, 1)
 
     @pl.when(step == 0)
     def _():
-        load_field(own, halos, rot, sems)
+        mine = pltpu.make_async_copy(own, rot.at[0, pl.ds(0, bricks)], sems.at[8])
+        mine.start()
+        piece = lambda slot: pltpu.make_async_copy(
+            halo_ref.at[slot], rot.at[0, pl.ds(bricks + slot * part, part)], sems.at[slot]
+        )
+        for slot in range(8):
+
+            @pl.when(side.has(*OFFSETS[slot]))
+            def _():
+                piece(slot).start()
+
+        for j in range(4):
+            rot[j, total] = jnp.zeros((3, 16, 128), BF16)
+        mine.wait()
+        rotate_range(rot, 0, bricks)
+        for slot in range(8):
+            here = side.has(*OFFSETS[slot])
+
+            @pl.when(here)
+            def _():
+                piece(slot).wait()
+
+            @pl.when(jnp.logical_not(here))
+            def _():
+                def clear(n, carry):
+                    rot[0, bricks + slot * part + n] = jnp.zeros((3, 16, 128), BF16)
+                    return carry
+
+                lax.fori_loop(0, part, clear, 0)
+
+        rotate_range(rot, bricks, total)
 
     for u, tile in enumerate(conv_block(step, table, w_ref, rot)):
         out_ref[:, u] = tile.reshape(BLOCK, 16, 128)
@@ -217,17 +383,18 @@
 
 def raw_conv(table, w, own, halos):
     bricks = own.shape[0]
+    total = bricks + 8 * halos.shape[1]
     return pl.pallas_call(
         raw_kernel,
         grid=(bricks // BLOCK,),
         out_shape=jax.ShapeDtypeStruct((bricks, 3, 16, 128), F32),
-        in_specs=[SMEM, VMEM, ANY] + [ANY] * len(halos),
+        in_specs=[SMEM, VMEM, ANY, ANY],
         out_specs=pl.BlockSpec((BLOCK, 3, 16, 128), lambda i: (i, 0, 0, 0)),
-        scratch_shapes=[field_scratch(own, halos), pltpu.SemaphoreType.DMA((9,))],
+        scratch_shapes=[pltpu.VMEM((4, total + 1, 3, 16, 128), BF16), pltpu.SemaphoreType.DMA((9,))],
         compiler_params=pltpu.CompilerParams(vmem_limit_bytes=56 * MIB),
         cost_estimate=pl.CostEstimate(flops=40_000_000_000, bytes_accessed=13_000_000, transcendentals=0),
         name="raw_conv",
-    )(table, w, own, *halos)
+    )(table, w, own, halos)
 
 
 def coarse_kernel(from_slot, to_place, w_ref, in_ref, out_ref, cells, grid, turned):
@@ -294,39 +461,64 @@
     )(from_slot, to_place, w, incoming)
 
 
-def back_kernel(slot, count, in_ref, out_ref):
+def spread_kernel(slot, count, in_ref, out_ref, face, landed, sends, recvs):
+    bricks = slot.shape[0]
+    part = bricks // 4
+    ring = Exchange(lambda c: face, lambda k, c: landed.at[k], sends, recvs, 1)
+    ring.greet()
+
     def take(b, carry):
-        value = in_ref[slot[b]]
-        out_ref[b] = jnp.where(b < count[0], value, jnp.zeros_like(value))
+        value = in_ref[slot[b]].astype(F32)
+        out_ref[b] = jnp.where(b < count[0], value, 0.0)
         return carry
 
-    lax.fori_loop(0, out_ref.shape[0], take, 0, unroll=8)
-
-
-def take_back(slot, count, returned):
+    lax.fori_loop(0, part, take, 0, unroll=8)
+    face[...] = out_ref[pl.ds(0, part)].reshape(face.shape).astype(BF16)
+    ring.meet()
+    ring.start()
+    lax.fori_loop(part, bricks, take, 0, unroll=8)
+    out_ref[bricks + 8 * part] = jnp.zeros((8, 128), F32)
+    ring.forward(0)
+    for k in (3, 4, 1, 6, 0, 2, 5, 7):
+        begin = bricks + k * part
+        here = ring.has(*OFFSETS[k])
+        if OFFSETS[k][1]:
+            ring.arrive(k)
+
+        @pl.when(here)
+        def _():
+            out_ref[pl.ds(begin, part)] = landed[k].astype(F32).reshape(part, 8, 128)
+
+        @pl.when(jnp.logical_not(here))
+        def _():
+            out_ref[pl.ds(begin, part)] = jnp.zeros((part, 8, 128), F32)
+
+    ring.finish()
+
+
+def spread(slot, count, returned):
+    bricks = slot.shape[0]
+    part = bricks // 4
     return pl.pallas_call(
-        back_kernel,
-        out_shape=jax.ShapeDtypeStruct((slot.shape[0], 8, 128), BF16),
+        spread_kernel,
+        out_shape=jax.ShapeDtypeStruct((bricks + 8 * part + 1, 8, 128), F32),
         in_specs=[SMEM, SMEM, VMEM],
         out_specs=VMEM,
-        name="take_back",
+        scratch_shapes=[
+            pltpu.VMEM((part // 2, 16, 128), BF16),
+            pltpu.VMEM((8, part // 2, 16, 128), BF16),
+            pltpu.SemaphoreType.DMA((8, 1)),
+            pltpu.SemaphoreType.DMA((8, 1)),
+        ],
+        compiler_params=pltpu.CompilerParams(
+            vmem_limit_bytes=16 * MIB, collective_id=2, has_side_effects=True
+        ),
+        name="spread",
     )(slot, count, returned)
 
 
-def decode_kernel(table, count, w_ref, up_ref, own_ref, raw_ref, enc_ref, *rest):
-    halos, (out_ref, cells) = rest[:8], rest[8:]
+def decode_kernel(table, count, w_ref, up_ref, cells, raw_ref, enc_ref, out_ref):
     step = pl.program_id(0)
-    bricks = own_ref.shape[0]
-    part = halos[0].shape[0]
-    total = bricks + 8 * part
-
-    @pl.when(step == 0)
-    def _():
-        cells[pl.ds(0, bricks)] = own_ref[...].astype(F32)
-        for d, piece in enumerate(halos):
-            cells[pl.ds(bricks + d * part, part)] = piece[...].astype(F32)
-        cells[total] = jnp.zeros((8, 128), F32)
-
     block = enc_ref.shape[0]
     acc = None
     for g in range(7):
@@ -351,38 +543,22 @@
             mixed = raw_ref[:, u, h * 8 : h * 8 + 8] + acc[:, lanes].reshape(block, 8, 128)
             halves.append(jnp.where(live, restored + jnp.maximum(mixed, 0.0), 0.0))
         tiles.append(jnp.concatenate(halves, axis=1).astype(BF16))
-    out_ref[...] = from_dense(tiles)
-
-
-def decode(table, count, w, up, own, raw, enc, halos):
-    bricks = own.shape[0]
-    total = bricks + 8 * halos[0].shape[0]
-    block = 16
+    for b in range(0, block, 16):
+        out_ref[b : b + 16] = from_dense([x[b : b + 16] for x in tiles])
+
+
+def decode(table, count, w, up, cells, raw, enc, block=48):
+    bricks = enc.shape[0]
     blocked = lambda: pl.BlockSpec((block, 3, 16, 128), lambda i: (i, 0, 0, 0))
     return pl.pallas_call(
         decode_kernel,
         grid=(bricks // block,),
         out_shape=jax.ShapeDtypeStruct((bricks, 6144), BF16),
-        in_specs=[SMEM, SMEM, VMEM, VMEM, VMEM, blocked(), blocked()] + [VMEM] * 8,
+        in_specs=[SMEM, SMEM, VMEM, VMEM, VMEM, blocked(), blocked()],
         out_specs=pl.BlockSpec((block, 6144), lambda i: (i, 0)),
-        scratch_shapes=[pltpu.VMEM((total + 1, 8, 128), F32)],
         compiler_params=pltpu.CompilerParams(vmem_limit_bytes=48 * MIB),
         name="decode",
-    )(table, count, w, up, own, raw, enc, *halos)
-
-
-def halo(face):
-    def sides(block, axis):
-        count = lax.axis_size(axis)
-        forward = [(i, i + 1) for i in range(count - 1)]
-        backward = [(target, source) for source, target in forward]
-        return lax.ppermute(block, axis, forward), lax.ppermute(block, axis, backward)
-
-    below, above = sides(face, "gz")
-    left, right = sides(face, "gx")
-    below_left, below_right = sides(below, "gx")
-    above_left, above_right = sides(above, "gx")
-    return [below_left, below, below_right, left, right, above_left, above, above_right]
+    )(table, count, w, up, cells, raw, enc)
 
 
 def relay(buffer, devices):
@@ -427,12 +603,10 @@
     both = ((0, 0), (0, spare), (0, spare))
     raising = jnp.pad(w_up, ((0, spare), (0, 0)))
 
-    x = make_dense(count, features[0])
-    encoded, outgoing = encode(
-        table, count, send_slot, jnp.pad(w_enc, lanes), pooling, x, halo(x[:boundary])
+    encoded, outgoing, encoded_halo = encode(
+        table, count, send_slot, jnp.pad(w_enc, lanes), pooling, features[0]
     )
     incoming = relay(outgoing, devices)
-    encoded_halo = halo(encoded[:boundary])
     reply = coarse(from_slot, to_place, jnp.pad(w_mid, both), incoming)
     returned = relay(reply, devices)
     raw = raw_conv(table, jnp.pad(w_dec, lanes), encoded, encoded_halo)
@@ -441,10 +615,8 @@
     )
     lift = jnp.pad(lift.astype(BF16).reshape(TAPS, chans, 8 * chans), ((0, 1), (0, spare), (0, 0)))
     lift = lift.reshape(28 * 128, 8 * chans)
-    back = take_back(slot, count, returned)
-    decoded = decode(
-        table, count, lift, raising, back, raw, encoded, halo(back[:boundary])
-    )
+    cells = spread(slot, count, returned)
+    decoded = decode(table, count, lift, raising, cells, raw, encoded)
     return decoded[None]
 
 

time: 256 us -> 189 us (0.74)
  starting transfers between devices: 101 us -> 14.3 us
  Pallas kernels: 114 us -> 134 us
  local copies, waits for them, and re-layouts: 22.2 us -> 18.5 us
    ppermute x24 -> x0, starting transfers between devices: 82.9 us -> none  [the longest x12 54.3 us: sides(): lax.ppermute(block, axis, backward)]
    pallas_call x3 -> x2, Pallas kernels: 52.4 us -> 74.4 us  [the longest x1 62.3 us: encode(): pl.pallas_call(functools.partial(encode_kernel, parts), grid=(bricks // B...]
    all_to_all x2, waiting for transfers between devices: 3.88 us -> 13.3 us  [relay(): lax.all_to_all(buffer.reshape(devices, -1, 128), ('gz', 'gx'), split_axis...]
    ppermute x24 -> x0, waiting for transfers between devices: 6.97 us -> none  [the longest x12 5.28 us: sides(): lax.ppermute(block, axis, forward)]
    slice x3 -> x0, local copies, waits for them, and re-layouts: 4.8 us -> none  [the longest x1 1.96 us: on_device(): encoded_halo = halo(encoded[:boundary])]
    all_to_all x2, starting transfers between devices: 17.8 us -> 14.3 us  [relay(): lax.all_to_all(buffer.reshape(devices, -1, 128), ('gz', 'gx'), split_axis...]
  transfers between devices with their start and end apart: 26 -> 2, of which waited for: 4 -> 1; matrix products, arithmetic and copies ran while one was open for 10% -> 9% of each run, Pallas kernels for 18% -> 20%
where the time goes in v3:
time: 189 us; the launch traced here: 188 us
  Pallas kernels  134 us (71%)
  local copies, waits for them, and re-layouts  18.5 us (10%)
  starting transfers between devices  14.3 us (8%)
  waiting for transfers between devices  13.3 us (7%)
  matrix products  3.89 us (2%)
  other arithmetic  3.39 us (2%)
    pallas_call x1, Pallas kernels, encode(): pl.pallas_call(functools.partial(encode_kernel, parts), grid=(bricks // B...  62.3 us
    pallas_call x1, Pallas kernels, raw_conv(): pl.pallas_call(raw_kernel, grid=(bricks // BLOCK,), out_shape=jax.ShapeDt...  37.1 us
    pallas_call x1, Pallas kernels, decode(): pl.pallas_call(decode_kernel, grid=(bricks // block,), out_shape=jax.Shap...  16 us
    all_to_all x2, starting transfers between devices, relay(): lax.all_to_all(buffer.reshape(devices, -1, 128), ('gz', 'gx'), split_axis...  14.3 us
    all_to_all x2, waiting for transfers between devices, relay(): lax.all_to_all(buffer.reshape(devices, -1, 128), ('gz', 'gx'), split_axis...  13.3 us
    pallas_call x1, Pallas kernels, spread(): pl.pallas_call(spread_kernel, out_shape=jax.ShapeDtypeStruct((bricks + 8...  12.1 us
    reshape x1, local copies, waits for them, and re-layouts, on_device(): lift.astype(BF16).reshape(TAPS, chans, 8 * chans)  6.76 us
    pallas_call x1, Pallas kernels, coarse(): pl.pallas_call(coarse_kernel, out_shape=jax.ShapeDtypeStruct(incoming.sha...  6.65 us
  transfers between devices with their start and end apart: 2, of which 1 were waited for; matrix products, arithmetic and copies ran while one was open for 9% of the time, Pallas kernels for 20%

profile of v3, /device:TPU:40, one launch (start us, length us, event | category | flops | bytes accessed | tf_op | source)
XLA Modules:
  0.0 188.4 jit_solution(15337540380207976976)
XLA Ops:
  0.0 0.9 compare_select_fusion
  0.9 0.1 copy.20
  1.0 0.7 reshape.32.table
  1.7 0.9 convert_reduce_fusion
  2.7 0.7 multiply_add_fusion
  3.4 0.7 select_reduce_fusion.send_slot
  4.7 0.9 reshape.36
  5.7 0.2 copy.24
  5.9 0.2 pad.32
  6.1 0.0 copy-start.6
  6.1 0.7 copy.57
  6.8 2.1 %pad.31.w_ref = bf16[27,96,128]{2,1,0:T(8,128)(2,1)} pad(bf16[27,96,96]{2,1,0:T(8,128)(2,1)} %param.15, bf16[]{:T(256)} %constant.57.clone.1), padding=0_0x0_0x0_32 | pad | bytes 1161218 | tf_op jit(solution)/shard_map/jit(_pad)/pad | solution.py:607
  8.9 62.3 %encode.1 = (bf16[192,3,16,128]{3,2,1,0:T(8,128)(2,1)}, bf16[384,8,128]{2,1,0:T(8,128)(2,1)}, bf16[8,48,3,16,128]{4,3,2,1,0:T(8,128)(2,1)}) custom-call(s32[5376]{0:T(1024)} %reshape.32.table, s32[1]{0:T(128)} %bitcast.54.count, s32[384]{0:T(512)} %select_reduce_fusion.send_slot, bf16[27,96,128]{2,1,0:T(8,128)(2,1)} %pad.31.w_ref, ...), custom_call_target="tpu_custom_call" | custom-call | tf_op jit(solution)/shard_map/encode/pallas_call | solution.py:316
  71.2 8.1 %all-to-all-start = ((bf16[128,24,128]{2,1,0:T(8,128)(2,1)}), bf16[128,24,128]{2,1,0:T(8,128)(2,1)S(1)}, u32[]{:S(2)}, u32[]{:S(2)}) async-start(bf16[128,24,128]{2,1,0:T(8,128)(2,1)} %bitcast.63), calls=%async_computation | async-start | bytes 1572864 | tf_op jit(solution)/shard_map/all_to_all | solution.py:565
  79.3 0.0 copy-done.2
  79.3 1.0 pad.33.w_ref
  80.3 0.0 copy-done.3
  80.3 0.2 pad.30.w_ref
  80.6 0.0 copy-done.6
  80.6 0.1 select_reduce_fusion.1.from_slot
  80.7 13.3 %all-to-all-done = bf16[128,24,128]{2,1,0:T(8,128)(2,1)S(1)} async-done(((bf16[128,24,128]{2,1,0:T(8,128)(2,1)}), bf16[128,24,128]{2,1,0:T(8,128)(2,1)S(1)}, u32[]{:S(2)}, u32[]{:S(2)}) %all-to-all-start) | async-done | bytes 786464 | tf_op jit(solution)/shard_map/all_to_all | solution.py:565
  94.1 6.6 %coarse_mix.1 = bf16[384,8,128]{2,1,0:T(8,128)(2,1)} custom-call(s32[192]{0:T(256)S(1)} %select_reduce_fusion.1.from_slot, s32[384]{0:T(512)S(1)} %fusion.10.to_place, bf16[27,128,128]{2,1,0:T(8,128)(2,1)S(1)} %pad.30.w_ref, bf16[384,8,128]{2,1,0:T(8,128)(2,1)S(1)} %bitcast.58), custom_call_target="tpu_custom_call" | custom-call | tf_op jit(solution)/shard_map/coarse_mix/pallas_call | solution.py:449
  100.7 6.2 %all-to-all-start.1 = ((bf16[128,24,128]{2,1,0:T(8,128)(2,1)}), bf16[128,24,128]{2,1,0:T(8,128)(2,1)S(1)}, u32[]{:S(2)}, u32[]{:S(2)}) async-start(bf16[128,24,128]{2,1,0:T(8,128)(2,1)} %bitcast.14), calls=%async_computation.1 | async-start | bytes 1572864 | tf_op jit(solution)/shard_map/all_to_all | solution.py:565
  106.9 0.0 copy-start.4
  107.0 37.1 %raw_conv.1.raw_ref = f32[192,3,16,128]{3,2,1,0:T(8,128)} custom-call(s32[5376]{0:T(1024)} %reshape.32.table, bf16[27,96,128]{2,1,0:T(8,128)(2,1)} %pad.33.w_ref, bf16[192,3,16,128]{3,2,1,0:T(8,128)(2,1)} %get-tuple-element.9.own.enc_ref, bf16[8,48,3,16,128]{4,3,2,1,0:T(8,128)(2,1)} %get-tuple-element.10.halo_ref), custom_call_target="tpu_custom_call" | custom-call | flops 40000000000 | bytes 13000000 | tf_op jit(solution)/shard_map/raw_conv/pallas_call | solution.py:387
  144.1 0.2 reshape.33
  144.4 3.9 %convolution_convert_fusion = bf16[27,96,96,8]{2,1,3,0:T(8,128)(2,1)} fusion(bf16[27,96,96]{2,1,0:T(8,128)(2,1)S(1)} %copy-done.2, bf16[96,8,96]{2,1,0:T(8,128)(2,1)S(1)} %reshape.33), kind=kOutput, calls=%fused_computation | convolution fusion | flops 384196608 | bytes 4626432 | tf_op jit(solution)/shard_map/cse,ked->kcsd/dot_general | solution.py:613
  148.3 6.8 %copy.23 = bf16[27,96,768]{2,1,0:T(8,128)(2,1)} copy(bf16[27,96,768]{1,2,0:T(8,128)(2,1)} %bitcast.60) | data formatting | bytes 7962624 | tf_op jit(solution)/shard_map/reshape | solution.py:616
  155.0 5.3 %pad.28 = bf16[28,128,768]{2,1,0:T(8,128)(2,1)} pad(bf16[27,96,768]{2,1,0:T(8,128)(2,1)} %copy.23, bf16[]{:T(256)} %constant.57.clone.1), padding=0_1x0_32x0_0 | pad | bytes 9486338 | tf_op jit(solution)/shard_map/jit(_pad)/pad | solution.py:616
  160.3 0.0 all-to-all-done.1
  160.3 12.1 %spread.1.cells = f32[577,8,128]{2,1,0:T(8,128)S(1)} custom-call(s32[192]{0:T(256)S(1)} %multiply_add_fusion.1.slot, s32[1]{0:T(128)} %bitcast.55.count, bf16[384,8,128]{2,1,0:T(8,128)(2,1)S(1)} %bitcast.57), custom_call_target="tpu_custom_call" | custom-call | tf_op jit(solution)/shard_map/spread/pallas_call | solution.py:502
  172.5 16.0 %decode.1 = bf16[192,6144]{1,0:T(8,128)(2,1)} custom-call(s32[5376]{0:T(1024)S(1)} %copy-done.1, s32[1]{0:T(128)} %bitcast.56.count, bf16[3584,768]{1,0:T(8,128)(2,1)} %bitcast.59, bf16[128,768]{1,0:T(8,128)(2,1)S(1)} %pad.29.up_ref, f32[577,8,128]{2,1,0:T(8,128)S(1)} %spread.1.cells, f32[192,3,16,128]{3,2,1,0:T(8,128)} %raw_conv.1.raw_ref, ...), custom_call_target="tpu_custom_call" | custom-call | tf_op jit(solution)/shard_map/decode/pallas_call | solution.py:553
  (14 shorter events, 0.1 us)
Async XLA Ops:
  0.0 79.3 %copy-start.2 = (bf16[27,96,96]{2,1,0:T(8,128)(2,1)S(1)}, bf16[27,96,96]{2,1,0:T(8,128)(2,1)}, u32[]{:S(2)}) copy-start(bf16[27,96,96]{2,1,0:T(8,128)(2,1)} %param.19) | copy-start | bytes 1492996
  0.0 80.3 %copy-start.3 = (bf16[27,96,96]{2,1,0:T(8,128)(2,1)S(1)}, bf16[27,96,96]{2,1,0:T(8,128)(2,1)}, u32[]{:S(2)}) copy-start(bf16[27,96,96]{2,1,0:T(8,128)(2,1)} %param.17) | copy-start | bytes 1492996
  6.1 74.4 %copy-start.6 = (s32[1,384]{1,0:T(1,128)S(1)}, s32[1,384]{1,0:T(1,128)}, u32[]{:S(2)}) copy-start(s32[1,384]{1,0:T(1,128)} %param.14) | copy-start | bytes 4612
  71.2 22.9 %all-to-all-start = ((bf16[128,24,128]{2,1,0:T(8,128)(2,1)}), bf16[128,24,128]{2,1,0:T(8,128)(2,1)S(1)}, u32[]{:S(2)}, u32[]{:S(2)}) async-start(bf16[128,24,128]{2,1,0:T(8,128)(2,1)} %bitcast.63), calls=%async_computation | async-start | bytes 1572864 | tf_op jit(solution)/shard_map/all_to_all | solution.py:565
  100.7 59.6 %all-to-all-start.1 = ((bf16[128,24,128]{2,1,0:T(8,128)(2,1)}), bf16[128,24,128]{2,1,0:T(8,128)(2,1)S(1)}, u32[]{:S(2)}, u32[]{:S(2)}) async-start(bf16[128,24,128]{2,1,0:T(8,128)(2,1)} %bitcast.14), calls=%async_computation.1 | async-start | bytes 1572864 | tf_op jit(solution)/shard_map/all_to_all | solution.py:565
  106.9 37.1 %copy-start.4 = (bf16[96,768]{1,0:T(8,128)(2,1)S(1)}, bf16[96,768]{1,0:T(8,128)(2,1)}, u32[]{:S(2)}) copy-start(bf16[96,768]{1,0:T(8,128)(2,1)} %param.18) | copy-start | bytes 442372
  155.0 5.3 %copy-start.5 = (s32[1,192]{1,0:T(1,128)S(1)}, s32[1,192]{1,0:T(1,128)}, u32[]{:S(2)}) copy-start(s32[1,192]{1,0:T(1,128)} %param.13) | copy-start | bytes 2308
  155.0 17.4 %copy-start = (bf16[192,3,16,128]{3,2,1,0:T(8,128)(2,1)S(1)}, bf16[192,3,16,128]{3,2,1,0:T(8,128)(2,1)}, u32[]{:S(2)}) copy-start(bf16[192,3,16,128]{3,2,1,0:T(8,128)(2,1)} %get-tuple-element.9.own.enc_ref) | copy-start | bytes 7077892
  155.0 17.4 %copy-start.1 = (s32[5376]{0:T(1024)S(1)}, s32[5376]{0:T(1024)}, u32[]{:S(2)}) copy-start(s32[5376]{0:T(1024)} %reshape.32.table) | copy-start | bytes 64516

commit v4 on v3

--- a/solution.py
+++ b/solution.py
@@ -104,8 +104,8 @@
         peers = sum(self.has(dz, dx).astype(jnp.int32) for dz, dx in ((-1, 0), (1, 0), (0, -1), (0, 1)))
         pl.semaphore_wait(pltpu.get_barrier_semaphore(), peers)
 
-    def start(self):
-        for c in range(self.chunks):
+    def start(self, *chunks):
+        for c in chunks:
             for slot in (1, 6, 3, 4):
 
                 @pl.when(self.sends(slot))
@@ -140,35 +140,54 @@
                     self.copy(slot, c).wait_send()
 
 
-def rotate_range(rot, start, stop):
-    wide = lax.broadcasted_iota(jnp.int32, (128, 128), 1)
+def rotate_range(rot, start, stop, size=48):
+    rows = size * 16
+    wide = lax.broadcasted_iota(jnp.int32, (rows, 128), 1)
+    source = lax.broadcasted_iota(jnp.int32, (128, 384), 0)
+    lane = lax.broadcasted_iota(jnp.int32, (128, 384), 1)
+    shift = jnp.where(lane < 128, 96, jnp.where(lane < 256, 64, 32))
+    turn = (source == ((lane - shift) & 127)).astype(F32).astype(BF16)
 
     def body(m, carry):
-        n = pl.multiple_of(m * 8, 8)
-        tiles = [rot[0, pl.ds(n, 8), t].reshape(128, 128) for t in range(3)]
+        n = pl.multiple_of(start + m * size, 16)
+        tiles = [rot[0, pl.ds(n, size), t].reshape(rows, 128) for t in range(3)]
+        turned = jnp.dot(tiles[0], turn, preferred_element_type=F32).astype(BF16)
         done = []
         for j in range(1, 4):
             amount = (96 * j) % 128
-            rolled = [pltpu.roll(x, amount, 1) for x in tiles]
+            rolled = [turned[:, (j - 1) * 128 : j * 128]]
+            rolled += [pltpu.roll(x, amount, 1) for x in tiles[1:]]
             for u in range(3):
                 hi = (128 * u + 127 - 96 * j) // 128 % 3
                 lo = (128 * u - 96 * j) // 128 % 3
-                done.append((j, u, jnp.where(wide >= amount, rolled[hi], rolled[lo]).reshape(8, 16, 128)))
+                done.append((j, u, jnp.where(wide >= amount, rolled[hi], rolled[lo]).reshape(size, 16, 128)))
         for j, u, x in done:
-            rot[j, pl.ds(n, 8), u] = x
+            rot[j, pl.ds(n, size), u] = x
         return carry
 
-    lax.fori_loop(start // 8, stop // 8, body, 0)
+    lax.fori_loop(0, (stop - start) // size, body, 0)
+
+
+def widen(wide, w_ref):
+    wide[...] = jnp.zeros(wide.shape, BF16)
+    for k in range(w_ref.shape[0]):
+        wide[k, : w_ref.shape[1], : w_ref.shape[2]] = w_ref[k]
 
 
 def conv_block(step, table, w_ref, rot):
     lane = lax.broadcasted_iota(jnp.int32, (16, 128), 1)
 
     def gather(c, b):
-        base = (step * BLOCK + b) * 28
+        brick = step * BLOCK + b
         lanes = [[] for _ in range(4)]
         for g in CHUNKS[c]:
-            loads = [[rot[j, table[base + 4 * g + j], t] for t in range(3)] for j in range(4)]
+            loads = []
+            for j in range(4):
+                if 4 * g + j < TAPS:
+                    n = table[4 * g + j, brick]
+                    loads.append([rot[j, n, t] for t in range(3)])
+                else:
+                    loads.append([jnp.zeros((16, 128), BF16)] * 3)
             for i in range(4):
                 for u in range(3):
                     a, b2 = loads[ORDER[i][u]][u], loads[ORDER[i][u + 1]][u]
@@ -181,7 +200,7 @@
         for i in range(4):
             lhs = jnp.concatenate([jnp.concatenate(x[i], axis=1) for x in got], axis=0)
             taps = [4 * g + ORDER[i][q] for g in CHUNKS[c] for q in range(4)]
-            rhs = jnp.concatenate([w_ref[k] if k < TAPS else jnp.zeros((96, 128), BF16) for k in taps], axis=0)
+            rhs = jnp.concatenate([w_ref[k] for k in taps], axis=0)
             part = jnp.dot(lhs, rhs, preferred_element_type=F32)
             acc[i] = part if acc[i] is None else acc[i] + part
     r1 = pltpu.roll(acc[1], 96, 1)
@@ -192,13 +211,14 @@
 
 
 def encode_kernel(
-    parts, table, count, send_slot, w_ref, wd_ref, x_ref,
-    enc_ref, out_ref, halo_ref, rot, pooled, face, sends, recvs, sends2, recvs2,
+    parts, parts2, table, count, send_slot, w_in, wd_in, x_ref,
+    enc_ref, out_ref, halo_ref, rot, pooled, face, w_ref, wd_ref, sends, recvs, sends2, recvs2,
 ):
     step = pl.program_id(0)
     bricks = x_ref.shape[0]
     part = bricks // 4
     size = part // parts
+    size2 = part // parts2
     total = bricks + 8 * part
     first = Exchange(
         lambda c: rot.at[0, pl.ds(c * size, size)],
@@ -206,9 +226,9 @@
         sends, recvs, parts,
     )
     second = Exchange(
-        lambda c: face.at[pl.ds(c * size, size)],
-        lambda slot, c: halo_ref.at[slot, pl.ds(c * size, size)],
-        sends2, recvs2, parts,
+        lambda c: face.at[pl.ds(c * size2, size2)],
+        lambda slot, c: halo_ref.at[slot, pl.ds(c * size2, size2)],
+        sends2, recvs2, parts2,
     )
 
     def fill(slot):
@@ -241,17 +261,28 @@
         first.greet()
         densify(0, part)
         first.meet()
-        first.start()
+        first.start(*range(parts))
         for j in range(4):
             rot[j, total] = jnp.zeros((3, 16, 128), BF16)
         pooled[bricks] = jnp.zeros((8, 128), F32)
-        densify(part, bricks)
+        widen(w_ref, w_in)
+        wd_ref[...] = jnp.zeros(wd_ref.shape, BF16)
+        half, chans = wd_in.shape[0] // 2, wd_in.shape[1]
+        wd_ref[:, :chans] = wd_in[:half]
+        wd_ref[:, 128 : 128 + chans] = wd_in[half:]
+        densify(part, 2 * part)
         first.forward(0)
-        rotate_range(rot, 0, bricks)
+        densify(2 * part, 3 * part)
         first.forward(1)
+        densify(3 * part, bricks)
+        first.forward(2)
+        rotate_range(rot, 0, 2 * part)
+        first.forward(3)
+        rotate_range(rot, 2 * part, bricks)
+        first.forward(4)
         fill(3)
         fill(4)
-        first.forward(2)
+        first.forward(5)
         for slot in (1, 6, 0, 2, 5, 7):
             fill(slot)
         first.finish()
@@ -273,17 +304,21 @@
     @pl.when(step == 0)
     def _():
         face[pl.ds(0, BLOCK)] = enc_ref[...]
+        second.start(0, 1)
 
     @pl.when(step == 1)
     def _():
         face[pl.ds(BLOCK, part - BLOCK)] = enc_ref[: part - BLOCK]
-        second.start()
-
-    for c in range(parts):
-
-        @pl.when(step == c + 2)
-        def _():
-            second.forward(c)
+        second.start(2)
+
+    @pl.when(step == 2)
+    def _():
+        second.forward(0)
+
+    @pl.when(step == 3)
+    def _():
+        second.forward(1)
+        second.forward(2)
 
     @pl.when(step == pl.num_programs(0) - 1)
     def _():
@@ -311,10 +346,11 @@
     bricks = x.shape[0]
     part = bricks // 4
     slots = send_slot.shape[0]
-    parts = 3
+    parts, parts2 = 6, 3
     sems = pltpu.SemaphoreType.DMA((8, parts))
+    sems2 = pltpu.SemaphoreType.DMA((8, parts2))
     return pl.pallas_call(
-        functools.partial(encode_kernel, parts),
+        functools.partial(encode_kernel, parts, parts2),
         grid=(bricks // BLOCK,),
         out_shape=(
             jax.ShapeDtypeStruct((bricks, 3, 16, 128), BF16),
@@ -327,7 +363,9 @@
             pltpu.VMEM((4, bricks + 8 * part + 1, 3, 16, 128), BF16),
             pltpu.VMEM((bricks + 1, 8, 128), F32),
             pltpu.VMEM((part, 3, 16, 128), BF16),
-            sems, sems, sems, sems,
+            pltpu.VMEM((TAPS + 1, 96, 128), BF16),
+            pltpu.VMEM((wd.shape[0] // 2, 256), BF16),
+            sems, sems, sems2, sems2,
         ],
         compiler_params=pltpu.CompilerParams(
             vmem_limit_bytes=56 * MIB, collective_id=1, has_side_effects=True
@@ -336,7 +374,7 @@
     )(table, count, send_slot, w, wd, x)
 
 
-def raw_kernel(table, w_ref, own, halo_ref, out_ref, rot, sems):
+def raw_kernel(table, w_in, own, halo_ref, after, out_ref, rot, w_ref, sems):
     step = pl.program_id(0)
     bricks = own.shape[0]
     part = halo_ref.shape[1]
@@ -347,6 +385,7 @@
     def _():
         mine = pltpu.make_async_copy(own, rot.at[0, pl.ds(0, bricks)], sems.at[8])
         mine.start()
+        widen(w_ref, w_in)
         piece = lambda slot: pltpu.make_async_copy(
             halo_ref.at[slot], rot.at[0, pl.ds(bricks + slot * part, part)], sems.at[slot]
         )
@@ -381,26 +420,31 @@
         out_ref[:, u] = tile.reshape(BLOCK, 16, 128)
 
 
-def raw_conv(table, w, own, halos):
+def raw_conv(table, w, own, halos, after):
     bricks = own.shape[0]
     total = bricks + 8 * halos.shape[1]
     return pl.pallas_call(
         raw_kernel,
         grid=(bricks // BLOCK,),
         out_shape=jax.ShapeDtypeStruct((bricks, 3, 16, 128), F32),
-        in_specs=[SMEM, VMEM, ANY, ANY],
+        in_specs=[SMEM, VMEM, ANY, ANY, ANY],
         out_specs=pl.BlockSpec((BLOCK, 3, 16, 128), lambda i: (i, 0, 0, 0)),
-        scratch_shapes=[pltpu.VMEM((4, total + 1, 3, 16, 128), BF16), pltpu.SemaphoreType.DMA((9,))],
+        scratch_shapes=[
+            pltpu.VMEM((4, total + 1, 3, 16, 128), BF16),
+            pltpu.VMEM((TAPS + 1, 96, 128), BF16),
+            pltpu.SemaphoreType.DMA((9,)),
+        ],
         compiler_params=pltpu.CompilerParams(vmem_limit_bytes=56 * MIB),
         cost_estimate=pl.CostEstimate(flops=40_000_000_000, bytes_accessed=13_000_000, transcendentals=0),
         name="raw_conv",
-    )(table, w, own, halos)
-
-
-def coarse_kernel(from_slot, to_place, w_ref, in_ref, out_ref, cells, grid, turned):
+    )(table, w, own, halos, after)
+
+
+def coarse_kernel(from_slot, to_place, w_in, in_ref, after, out_ref, cells, grid, turned, w_ref):
     places = from_slot.shape[0]
     groups = places // 8
     grid[...] = jnp.zeros(grid.shape, BF16)
+    widen(w_ref, w_in)
 
     def land(p, carry):
         cells[pl.ds(pl.multiple_of(p * 8, 8), 8)] = in_ref[from_slot[p]].astype(F32)
@@ -426,8 +470,7 @@
             for k in (k0, min(k0 + 1, TAPS - 1)):
                 dz, dy, dx = k // 9, k // 3 % 3, k % 3
                 sides.append(grid[z + dz, dy : dy + 4, dx : dx + 4].reshape(16 * 32, 128))
-            second = w_ref[k0 + 1] if k0 + 1 < TAPS else jnp.zeros((128, 128), BF16)
-            rhs = jnp.concatenate([w_ref[k0], second], axis=0)
+            rhs = jnp.concatenate([w_ref[k0], w_ref[k0 + 1]], axis=0)
             part = jnp.dot(jnp.concatenate(sides, axis=1), rhs, preferred_element_type=F32)
             acc = part if acc is None else acc + part
         acc = acc.reshape(16, 32, 128)
@@ -444,21 +487,22 @@
     lax.fori_loop(0, out_ref.shape[0], reply, 0, unroll=8)
 
 
-def coarse(from_slot, to_place, w, incoming):
+def coarse(from_slot, to_place, w, incoming, after):
     places = from_slot.shape[0]
     return pl.pallas_call(
         coarse_kernel,
         out_shape=jax.ShapeDtypeStruct(incoming.shape, BF16),
-        in_specs=[SMEM, SMEM, VMEM, VMEM],
+        in_specs=[SMEM, SMEM, VMEM, VMEM, ANY],
         out_specs=VMEM,
         scratch_shapes=[
             pltpu.VMEM((places * 8, 128), F32),
             pltpu.VMEM((6, 6, 6, 32, 128), BF16),
             pltpu.VMEM((places * 8 + 8, 128), F32),
+            pltpu.VMEM((TAPS + 1, 128, 128), BF16),
         ],
         compiler_params=pltpu.CompilerParams(vmem_limit_bytes=32 * MIB),
         name="coarse_mix",
-    )(from_slot, to_place, w, incoming)
+    )(from_slot, to_place, w, incoming, after)
 
 
 def spread_kernel(slot, count, in_ref, out_ref, face, landed, sends, recvs):
@@ -475,7 +519,7 @@
     lax.fori_loop(0, part, take, 0, unroll=8)
     face[...] = out_ref[pl.ds(0, part)].reshape(face.shape).astype(BF16)
     ring.meet()
-    ring.start()
+    ring.start(0)
     lax.fori_loop(part, bricks, take, 0, unroll=8)
     out_ref[bricks + 8 * part] = jnp.zeros((8, 128), F32)
     ring.forward(0)
@@ -517,6 +561,42 @@
     )(slot, count, returned)
 
 
+def merge_kernel(up_ref, w_in, out_ref, stack, wide):
+    chans = up_ref.shape[0]
+    out_ref[...] = jnp.zeros(out_ref.shape, BF16)
+    wide[...] = jnp.zeros(wide.shape, BF16)
+    for s in range(8):
+        stack[s * chans : (s + 1) * chans] = up_ref[:, s * chans : (s + 1) * chans]
+    lane = lax.broadcasted_iota(jnp.int32, (chans, 128), 1)
+
+    def body(k, carry):
+        wide[:, :chans] = w_in[k]
+        whole = jnp.dot(stack[...], wide[...], preferred_element_type=F32)
+        for h in range(2):
+            a = [whole[(4 * h + i) * chans : (4 * h + i + 1) * chans] for i in range(4)]
+            r1, r2, r3 = pltpu.roll(a[1], 96, 1), pltpu.roll(a[2], 64, 1), pltpu.roll(a[3], 32, 1)
+            tiles = (jnp.where(lane < 96, a[0], r1), jnp.where(lane < 64, r1, r2), jnp.where(lane < 32, r2, r3))
+            for u in range(3):
+                out_ref[k, :chans, h * 384 + u * 128 : h * 384 + (u + 1) * 128] = tiles[u].astype(BF16)
+        return carry
+
+    lax.fori_loop(0, TAPS, body, 0)
+
+
+def merge(w_up, w):
+    chans = w_up.shape[0]
+    return pl.pallas_call(
+        merge_kernel,
+        out_shape=jax.ShapeDtypeStruct((TAPS + 1, 128, 8 * chans), BF16),
+        in_specs=[VMEM, VMEM],
+        out_specs=VMEM,
+        scratch_shapes=[pltpu.VMEM((8 * chans, chans), BF16), pltpu.VMEM((chans, 128), BF16)],
+        compiler_params=pltpu.CompilerParams(vmem_limit_bytes=24 * MIB),
+        cost_estimate=pl.CostEstimate(flops=8_000_000_000, bytes_accessed=8_000_000, transcendentals=0),
+        name="merge",
+    )(w_up, w)
+
+
 def decode_kernel(table, count, w_ref, up_ref, cells, raw_ref, enc_ref, out_ref):
     step = pl.program_id(0)
     block = enc_ref.shape[0]
@@ -524,13 +604,18 @@
     for g in range(7):
         columns = []
         for j in range(4):
-            rows = [cells[table[(step * block + b) * 28 + 4 * g + j]] for b in range(block)]
-            columns.append(jnp.concatenate(rows, axis=0).astype(BF16))
+            k = 4 * g + j
+            if k < TAPS:
+                rows = [cells[table[k, step * block + b]] for b in range(block)]
+                columns.append(jnp.concatenate(rows, axis=0).astype(BF16))
+            else:
+                columns.append(jnp.zeros((block * 8, 128), BF16))
         lhs = jnp.concatenate(columns, axis=1)
         part_sum = jnp.dot(lhs, w_ref[g * 512 : (g + 1) * 512], preferred_element_type=F32)
         acc = part_sum if acc is None else acc + part_sum
     mine = cells[pl.ds(step * block, block)].reshape(block * 8, 128).astype(BF16)
-    lifted = jnp.dot(mine, up_ref[...], preferred_element_type=F32)
+    up = jnp.concatenate([up_ref[...], jnp.zeros((128 - up_ref.shape[0], up_ref.shape[1]), BF16)], axis=0)
+    lifted = jnp.dot(mine, up, preferred_element_type=F32)
     live = lax.broadcasted_iota(jnp.int32, (block, 8, 128), 0) + step * block < count[0]
     tiles = []
     for u in range(3):
@@ -574,8 +659,6 @@
     devices = lax.axis_size("gz") * lax.axis_size("gx")
     bricks = features.shape[1]
     boundary = bricks // 4
-    chans = w_enc.shape[1]
-    spare = 128 - chans
     capacity = arrival_cell.shape[1] // devices
     slot_count = devices * capacity
     count = active_count[0]
@@ -584,8 +667,7 @@
     side = m // boundary
     n = jnp.where(m >= 4 * boundary, jnp.where(side == 4, m - 4 * boundary, n - boundary), n)
     empty = bricks + 8 * boundary
-    table = jnp.pad(jnp.where(n < 0, empty, n), ((0, 1), (0, 0)), constant_values=empty)
-    table = table.T.reshape(-1)
+    table = jnp.where(n < 0, empty, n)
     target = owner[0]
     index = jnp.arange(bricks, dtype=jnp.int32)
     same = jnp.logical_and(target[:, None] == target[None, :], index[None, :] < index[:, None])
@@ -597,26 +679,14 @@
     from_slot = jnp.sum(
         jnp.where(index[:, None] == to_place[None, :], slot_ids[None, :], 0), axis=1
     )
-    lanes = ((0, 0), (0, 0), (0, spare))
-    pooling = jnp.pad(w_down.reshape(2, 4 * chans, chans), lanes)
-    pooling = pooling.transpose(1, 0, 2).reshape(4 * chans, 256)
-    both = ((0, 0), (0, spare), (0, spare))
-    raising = jnp.pad(w_up, ((0, spare), (0, 0)))
-
-    encoded, outgoing, encoded_halo = encode(
-        table, count, send_slot, jnp.pad(w_enc, lanes), pooling, features[0]
-    )
+    encoded, outgoing, encoded_halo = encode(table, count, send_slot, w_enc, w_down, features[0])
     incoming = relay(outgoing, devices)
-    reply = coarse(from_slot, to_place, jnp.pad(w_mid, both), incoming)
+    lift = merge(w_up, w_dec)
+    reply = coarse(from_slot, to_place, w_mid, incoming, lift)
     returned = relay(reply, devices)
-    raw = raw_conv(table, jnp.pad(w_dec, lanes), encoded, encoded_halo)
-    lift = jnp.einsum(
-        "cse,ked->kcsd", w_up.reshape(chans, 8, chans), w_dec, preferred_element_type=F32
-    )
-    lift = jnp.pad(lift.astype(BF16).reshape(TAPS, chans, 8 * chans), ((0, 1), (0, spare), (0, 0)))
-    lift = lift.reshape(28 * 128, 8 * chans)
+    raw = raw_conv(table, w_dec, encoded, encoded_halo, reply)
     cells = spread(slot, count, returned)
-    decoded = decode(table, count, lift, raising, cells, raw, encoded)
+    decoded = decode(table, count, lift.reshape(-1, lift.shape[2]), w_up, cells, raw, encoded)
     return decoded[None]
 
 

time: 189 us -> 170 us (0.90)
  local copies, waits for them, and re-layouts: 18.5 us -> 6.69 us
  waiting for transfers between devices: 13.3 us -> 4.27 us
  Pallas kernels: 134 us -> 139 us
  matrix products: 3.89 us -> 0 us
    all_to_all x2, waiting for transfers between devices: 13.3 us -> 4.27 us  [relay(): lax.all_to_all(buffer.reshape(devices, -1, 128), ('gz', 'gx'), split_axis...]
    reshape x5 -> x0, local copies, waits for them, and re-layouts: 8.88 us -> none  [the longest x1 6.76 us: on_device(): lift.astype(BF16).reshape(TAPS, chans, 8 * chans)]
    pad x6 -> x0, local copies, waits for them, and re-layouts: 8.8 us -> none  [the longest x1 5.29 us: on_device(): jnp.pad(lift.astype(BF16).reshape(TAPS, chans, 8 * chans), ((0, 1), (0, s...]
    unnamed x15 -> x19, local copies, waits for them, and re-layouts: 0.75 us -> 6.69 us
    pallas_call x1 -> x2, Pallas kernels: 62.3 us -> 68 us  [the longest x1 60.1 us: encode(): pl.pallas_call(functools.partial(encode_kernel, parts, parts2), grid=(bri...]
    dot_general x1 -> x0, matrix products: 3.89 us -> none  [on_device(): jnp.einsum('cse,ked->kcsd', w_up.reshape(chans, 8, chans), w_dec, preferr...]
    pallas_call x1, Pallas kernels: 37.1 us -> 33.6 us  [raw_conv(): pl.pallas_call(raw_kernel, grid=(bricks // BLOCK,), out_shape=jax.ShapeDt...]
    pallas_call x1, Pallas kernels: 16 us -> 17.9 us  [decode(): pl.pallas_call(decode_kernel, grid=(bricks // block,), out_shape=jax.Shap...]
  transfers between devices with their start and end apart: 2 -> 2, of which waited for: 1 -> 1; matrix products, arithmetic and copies ran while one was open for 9% -> 0% of each run, Pallas kernels for 20% -> 24%
where the time goes in v4:
time: 170 us; the launch traced here: 169 us
  Pallas kernels  139 us (82%)
  starting transfers between devices  15.2 us (9%)
  local copies, waits for them, and re-layouts  6.69 us (4%)
  waiting for transfers between devices  4.27 us (3%)
  other arithmetic  3.83 us (2%)
    pallas_call x1, Pallas kernels, encode(): pl.pallas_call(functools.partial(encode_kernel, parts, parts2), grid=(bri...  60.1 us
    pallas_call x1, Pallas kernels, raw_conv(): pl.pallas_call(raw_kernel, grid=(bricks // BLOCK,), out_shape=jax.ShapeDt...  33.6 us
    pallas_call x1, Pallas kernels, decode(): pl.pallas_call(decode_kernel, grid=(bricks // block,), out_shape=jax.Shap...  17.9 us
    all_to_all x2, starting transfers between devices, relay(): lax.all_to_all(buffer.reshape(devices, -1, 128), ('gz', 'gx'), split_axis...  15.2 us
    pallas_call x1, Pallas kernels, spread(): pl.pallas_call(spread_kernel, out_shape=jax.ShapeDtypeStruct((bricks + 8...  12.4 us
    pallas_call x1, Pallas kernels, merge(): pl.pallas_call(merge_kernel, out_shape=jax.ShapeDtypeStruct((TAPS + 1, 12...  7.87 us
    pallas_call x1, Pallas kernels, coarse(): pl.pallas_call(coarse_kernel, out_shape=jax.ShapeDtypeStruct(incoming.sha...  6.87 us
    unnamed x19, local copies, waits for them, and re-layouts  6.69 us
  transfers between devices with their start and end apart: 2, of which 1 were waited for; matrix products, arithmetic and copies ran while one was open for 0% of the time, Pallas kernels for 24%

profile of v4, /device:TPU:40, one launch (start us, length us, event | category | flops | bytes accessed | tf_op | source)
XLA Modules:
  0.0 169.5 jit_solution(7679758622468280924)
XLA Ops:
  0.7 0.9 convert_reduce_fusion
  1.6 0.7 multiply_add_fusion
  2.3 0.6 select_reduce_fusion.send_slot
  2.9 1.4 compare_select_fusion.table
  4.3 1.7 %copy.12.wd_in = bf16[768,96]{1,0:T(8,128)(2,1)} copy(bf16[768,96]{0,1:T(8,128)(2,1)} %param.16) | data formatting | bytes 294912 | tf_op args[6]
  6.0 0.0 copy-start.7
  6.0 0.0 copy-start.8
  6.0 0.0 copy-start.6
  6.1 60.1 %encode.1 = (bf16[192,3,16,128]{3,2,1,0:T(8,128)(2,1)}, bf16[384,8,128]{2,1,0:T(8,128)(2,1)}, bf16[8,48,3,16,128]{4,3,2,1,0:T(8,128)(2,1)}) custom-call(s32[27,192]{1,0:T(8,128)} %compare_select_fusion.table, s32[1]{0:T(128)} %bitcast.34.count, s32[384]{0:T(512)} %select_reduce_fusion.send_slot, bf16[27,96,96]{2,1,0:T(8,128)(2,1)} %w_in.5, ...), custom_call_target="tpu_custom_call" | custom-call | tf_op jit(solution)/shard_map/encode/pallas_call | solution.py:352
  66.1 9.0 %all-to-all-start = ((bf16[128,24,128]{2,1,0:T(8,128)(2,1)}), bf16[128,24,128]{2,1,0:T(8,128)(2,1)S(1)}, u32[]{:S(2)}, u32[]{:S(2)}) async-start(bf16[128,24,128]{2,1,0:T(8,128)(2,1)} %bitcast.41), calls=%async_computation | async-start | bytes 1572864 | tf_op jit(solution)/shard_map/all_to_all | solution.py:650
  75.2 0.0 copy-done.7
  75.2 0.0 copy-done.8
  75.2 0.1 select_reduce_fusion.1.from_slot
  75.4 0.0 copy-done.5
  75.4 0.0 copy-done.6
  75.4 0.0 copy-start.3
  75.4 7.9 %merge.1.after = bf16[28,128,768]{2,1,0:T(8,128)(2,1)S(1)} custom-call(bf16[96,768]{1,0:T(8,128)(2,1)S(1)} %copy-done.5, bf16[27,96,96]{2,1,0:T(8,128)(2,1)S(1)} %copy-done.6), custom_call_target="tpu_custom_call" | custom-call | flops 8000000000 | bytes 8000000 | tf_op jit(solution)/shard_map/merge/pallas_call | solution.py:588
  83.3 0.0 copy-start
  83.3 2.4 %copy-done = bf16[28,128,768]{2,1,0:T(8,128)(2,1)} copy-done((bf16[28,128,768]{2,1,0:T(8,128)(2,1)}, bf16[28,128,768]{2,1,0:T(8,128)(2,1)S(1)}, u32[]{:S(2)}) %copy-start) | copy-done | bytes 5505048
  85.7 4.3 %all-to-all-done = bf16[128,24,128]{2,1,0:T(8,128)(2,1)S(1)} async-done(((bf16[128,24,128]{2,1,0:T(8,128)(2,1)}), bf16[128,24,128]{2,1,0:T(8,128)(2,1)S(1)}, u32[]{:S(2)}, u32[]{:S(2)}) %all-to-all-start) | async-done | bytes 786464 | tf_op jit(solution)/shard_map/all_to_all | solution.py:650
  89.9 0.0 copy-done.3
  89.9 2.6 %copy-done.1 = bf16[28,128,768]{2,1,0:T(8,128)(2,1)S(1)} copy-done((bf16[28,128,768]{2,1,0:T(8,128)(2,1)S(1)}, bf16[28,128,768]{2,1,0:T(8,128)(2,1)}, u32[]{:S(2)}) %copy-start.1) | copy-done | bytes 5505048
  92.5 6.9 %coarse_mix.1.after = bf16[384,8,128]{2,1,0:T(8,128)(2,1)} custom-call(s32[192]{0:T(256)S(1)} %select_reduce_fusion.1.from_slot, s32[384]{0:T(512)S(1)} %fusion.7.to_place, bf16[27,96,96]{2,1,0:T(8,128)(2,1)S(1)} %copy-done.3, bf16[384,8,128]{2,1,0:T(8,128)(2,1)S(1)} %bitcast.38, bf16[28,128,768]{2,1,0:T(8,128)(2,1)S(1)} %copy-done.1), custom_call_target="tpu_custom_call" | custom-call | tf_op jit(solution)/shard_map/coarse_mix/pallas_call | solution.py:492
  99.4 6.2 %all-to-all-start.1 = ((bf16[128,24,128]{2,1,0:T(8,128)(2,1)}), bf16[128,24,128]{2,1,0:T(8,128)(2,1)S(1)}, u32[]{:S(2)}, u32[]{:S(2)}) async-start(bf16[128,24,128]{2,1,0:T(8,128)(2,1)} %bitcast.8), calls=%async_computation.1 | async-start | bytes 1572864 | tf_op jit(solution)/shard_map/all_to_all | solution.py:650
  105.6 33.6 %raw_conv.1.raw_ref = f32[192,3,16,128]{3,2,1,0:T(8,128)} custom-call(s32[27,192]{1,0:T(8,128)} %compare_select_fusion.table, bf16[27,96,96]{2,1,0:T(8,128)(2,1)} %w_in.7, bf16[192,3,16,128]{3,2,1,0:T(8,128)(2,1)} %get-tuple-element.9.own.enc_ref, bf16[8,48,3,16,128]{4,3,2,1,0:T(8,128)(2,1)} %get-tuple-element.10.halo_ref, bf16[384,8,128]{2,1,0:T(8,128)(2,1)} %coarse_mix.1.after), custom_call_target="tpu_custom_call" | custom-call | flops 40000000000 | bytes 13000000 | tf_op jit(solution)/shard_map/raw_conv/pallas_call | solution.py:426
  139.2 0.0 copy-start.2
  139.2 0.0 copy-start.4
  139.2 0.0 all-to-all-done.1
  139.2 12.4 %spread.1.cells = f32[577,8,128]{2,1,0:T(8,128)S(1)} custom-call(s32[192]{0:T(256)S(1)} %multiply_add_fusion.1.slot, s32[1]{0:T(128)} %bitcast.35.count, bf16[384,8,128]{2,1,0:T(8,128)(2,1)S(1)} %bitcast.39), custom_call_target="tpu_custom_call" | custom-call | tf_op jit(solution)/shard_map/spread/pallas_call | solution.py:546
  151.6 0.0 copy-done.2
  151.6 0.0 copy-done.4
  151.6 17.9 %decode.1 = bf16[192,6144]{1,0:T(8,128)(2,1)} custom-call(s32[27,192]{1,0:T(8,128)S(1)} %copy-done.4, s32[1]{0:T(128)} %bitcast.36.count, bf16[3584,768]{1,0:T(8,128)(2,1)} %bitcast.37, bf16[96,768]{1,0:T(8,128)(2,1)S(1)} %copy-done.5, f32[577,8,128]{2,1,0:T(8,128)S(1)} %spread.1.cells, f32[192,3,16,128]{3,2,1,0:T(8,128)} %raw_conv.1.raw_ref, ...), custom_call_target="tpu_custom_call" | custom-call | tf_op jit(solution)/shard_map/decode/pallas_call | solution.py:638
  (5 shorter events, 0.1 us)
Async XLA Ops:
  6.0 69.1 %copy-start.7 = (s32[1,192]{1,0:T(1,128)S(1)}, s32[1,192]{1,0:T(1,128)}, u32[]{:S(2)}) copy-start(s32[1,192]{1,0:T(1,128)} %param.13) | copy-start | bytes 2308
  6.0 69.1 %copy-start.8 = (s32[1,384]{1,0:T(1,128)S(1)}, s32[1,384]{1,0:T(1,128)}, u32[]{:S(2)}) copy-start(s32[1,384]{1,0:T(1,128)} %param.14) | copy-start | bytes 4612
  6.0 69.3 %copy-start.5 = (bf16[96,768]{1,0:T(8,128)(2,1)S(1)}, bf16[96,768]{1,0:T(8,128)(2,1)}, u32[]{:S(2)}) copy-start(bf16[96,768]{1,0:T(8,128)(2,1)} %up_ref.3) | copy-start | bytes 442372
  6.0 69.3 %copy-start.6 = (bf16[27,96,96]{2,1,0:T(8,128)(2,1)S(1)}, bf16[27,96,96]{2,1,0:T(8,128)(2,1)}, u32[]{:S(2)}) copy-start(bf16[27,96,96]{2,1,0:T(8,128)(2,1)} %w_in.7) | copy-start | bytes 1492996
  66.1 23.8 %all-to-all-start = ((bf16[128,24,128]{2,1,0:T(8,128)(2,1)}), bf16[128,24,128]{2,1,0:T(8,128)(2,1)S(1)}, u32[]{:S(2)}, u32[]{:S(2)}) async-start(bf16[128,24,128]{2,1,0:T(8,128)(2,1)} %bitcast.41), calls=%async_computation | async-start | bytes 1572864 | tf_op jit(solution)/shard_map/all_to_all | solution.py:650
  75.4 14.5 %copy-start.3 = (bf16[27,96,96]{2,1,0:T(8,128)(2,1)S(1)}, bf16[27,96,96]{2,1,0:T(8,128)(2,1)}, u32[]{:S(2)}) copy-start(bf16[27,96,96]{2,1,0:T(8,128)(2,1)} %w_in.6) | copy-start | bytes 1492996
  83.3 2.4 %copy-start = (bf16[28,128,768]{2,1,0:T(8,128)(2,1)}, bf16[28,128,768]{2,1,0:T(8,128)(2,1)S(1)}, u32[]{:S(2)}) copy-start(bf16[28,128,768]{2,1,0:T(8,128)(2,1)S(1)} %merge.1.after) | copy-start | bytes 16515076
  89.9 2.6 %copy-start.1 = (bf16[28,128,768]{2,1,0:T(8,128)(2,1)S(1)}, bf16[28,128,768]{2,1,0:T(8,128)(2,1)}, u32[]{:S(2)}) copy-start(bf16[28,128,768]{2,1,0:T(8,128)(2,1)} %copy-done) | copy-start | bytes 16515076
  99.4 39.8 %all-to-all-start.1 = ((bf16[128,24,128]{2,1,0:T(8,128)(2,1)}), bf16[128,24,128]{2,1,0:T(8,128)(2,1)S(1)}, u32[]{:S(2)}, u32[]{:S(2)}) async-start(bf16[128,24,128]{2,1,0:T(8,128)(2,1)} %bitcast.8), calls=%async_computation.1 | async-start | bytes 1572864 | tf_op jit(solution)/shard_map/all_to_all | solution.py:650
  139.2 12.4 %copy-start.2 = (bf16[192,3,16,128]{3,2,1,0:T(8,128)(2,1)S(1)}, bf16[192,3,16,128]{3,2,1,0:T(8,128)(2,1)}, u32[]{:S(2)}) copy-start(bf16[192,3,16,128]{3,2,1,0:T(8,128)(2,1)} %get-tuple-element.9.own.enc_ref) | copy-start | bytes 7077892
  139.2 12.4 %copy-start.4 = (s32[27,192]{1,0:T(8,128)S(1)}, s32[27,192]{1,0:T(8,128)}, u32[]{:S(2)}) copy-start(s32[27,192]{1,0:T(8,128)} %compare_select_fusion.table) | copy-start | bytes 62212

commit v5 on v4

--- a/solution.py
+++ b/solution.py
@@ -374,77 +374,9 @@
     )(table, count, send_slot, w, wd, x)
 
 
-def raw_kernel(table, w_in, own, halo_ref, after, out_ref, rot, w_ref, sems):
-    step = pl.program_id(0)
-    bricks = own.shape[0]
-    part = halo_ref.shape[1]
-    total = bricks + 8 * part
-    side = Exchange(None, None, None, None, 1)
-
-    @pl.when(step == 0)
-    def _():
-        mine = pltpu.make_async_copy(own, rot.at[0, pl.ds(0, bricks)], sems.at[8])
-        mine.start()
-        widen(w_ref, w_in)
-        piece = lambda slot: pltpu.make_async_copy(
-            halo_ref.at[slot], rot.at[0, pl.ds(bricks + slot * part, part)], sems.at[slot]
-        )
-        for slot in range(8):
-
-            @pl.when(side.has(*OFFSETS[slot]))
-            def _():
-                piece(slot).start()
-
-        for j in range(4):
-            rot[j, total] = jnp.zeros((3, 16, 128), BF16)
-        mine.wait()
-        rotate_range(rot, 0, bricks)
-        for slot in range(8):
-            here = side.has(*OFFSETS[slot])
-
-            @pl.when(here)
-            def _():
-                piece(slot).wait()
-
-            @pl.when(jnp.logical_not(here))
-            def _():
-                def clear(n, carry):
-                    rot[0, bricks + slot * part + n] = jnp.zeros((3, 16, 128), BF16)
-                    return carry
-
-                lax.fori_loop(0, part, clear, 0)
-
-        rotate_range(rot, bricks, total)
-
-    for u, tile in enumerate(conv_block(step, table, w_ref, rot)):
-        out_ref[:, u] = tile.reshape(BLOCK, 16, 128)
-
-
-def raw_conv(table, w, own, halos, after):
-    bricks = own.shape[0]
-    total = bricks + 8 * halos.shape[1]
-    return pl.pallas_call(
-        raw_kernel,
-        grid=(bricks // BLOCK,),
-        out_shape=jax.ShapeDtypeStruct((bricks, 3, 16, 128), F32),
-        in_specs=[SMEM, VMEM, ANY, ANY, ANY],
-        out_specs=pl.BlockSpec((BLOCK, 3, 16, 128), lambda i: (i, 0, 0, 0)),
-        scratch_shapes=[
-            pltpu.VMEM((4, total + 1, 3, 16, 128), BF16),
-            pltpu.VMEM((TAPS + 1, 96, 128), BF16),
-            pltpu.SemaphoreType.DMA((9,)),
-        ],
-        compiler_params=pltpu.CompilerParams(vmem_limit_bytes=56 * MIB),
-        cost_estimate=pl.CostEstimate(flops=40_000_000_000, bytes_accessed=13_000_000, transcendentals=0),
-        name="raw_conv",
-    )(table, w, own, halos, after)
-
-
-def coarse_kernel(from_slot, to_place, w_in, in_ref, after, out_ref, cells, grid, turned, w_ref):
+def coarse_mix(from_slot, to_place, w_ref, in_ref, out_ref, cells, grid, turned, mixed):
     places = from_slot.shape[0]
     groups = places // 8
-    grid[...] = jnp.zeros(grid.shape, BF16)
-    widen(w_ref, w_in)
 
     def land(p, carry):
         cells[pl.ds(pl.multiple_of(p * 8, 8), 8)] = in_ref[from_slot[p]].astype(F32)
@@ -478,90 +410,203 @@
             for x in range(4):
                 here = grid[z + 1, y + 1, x + 1].astype(F32) + jnp.maximum(acc[y * 4 + x], 0.0)
                 turned[pl.ds(base(z, y, x), groups, stride=8)] = here[:groups]
-    turned[pl.ds(places * 8, 8)] = jnp.zeros((8, 128), F32)
+    mixed[pl.ds(0, places)] = turned[...].reshape(places, 8, 128)
+    mixed[places] = jnp.zeros((8, 128), F32)
 
     def reply(s, carry):
-        out_ref[s] = turned[pl.ds(pl.multiple_of(to_place[s] * 8, 8), 8)].astype(BF16)
+        out_ref[s] = mixed[to_place[s]].astype(BF16)
         return carry
 
     lax.fori_loop(0, out_ref.shape[0], reply, 0, unroll=8)
 
 
-def coarse(from_slot, to_place, w, incoming, after):
+def each_peer(act):
+    layers, slabs = lax.axis_size("gz"), lax.axis_size("gx")
+    devices = layers * slabs
+    me = lax.axis_index("gz") * slabs + lax.axis_index("gx")
+
+    def body(i, carry):
+        d = (me + i) % devices
+        act(d, (d // slabs, d % slabs))
+        return carry
+
+    lax.fori_loop(1, devices, body, 0)
+
+
+class Relay:
+    def __init__(self, source, landing, sems):
+        self.source, self.landing, self.sems = source, landing, sems
+        self.slabs = lax.axis_size("gx")
+        self.devices = lax.axis_size("gz") * self.slabs
+        self.me = lax.axis_index("gz") * self.slabs + lax.axis_index("gx")
+        self.cap = source.shape[0] // self.devices
+
+    def copy(self, begin, end, rows, peer):
+        return pltpu.make_async_remote_copy(
+            src_ref=self.source.at[pl.ds(begin, rows)],
+            dst_ref=self.landing.at[pl.ds(end, rows)],
+            send_sem=self.sems.at[0],
+            recv_sem=self.sems.at[1],
+            device_id=peer,
+            device_id_type=MESH,
+        )
+
+    def start(self):
+        each_peer(lambda d, peer: self.copy(d * self.cap, self.me * self.cap, self.cap, peer).start())
+        mine = pl.ds(self.me * self.cap, self.cap)
+        self.landing[mine] = self.source[mine]
+
+    def wait(self):
+        peer = (self.me + 1) % self.devices
+        whole = self.copy(0, 0, self.cap * (self.devices - 1), (peer // self.slabs, peer % self.slabs))
+        whole.wait_recv()
+        whole.wait_send()
+
+
+def middle_kernel(
+    table, count, from_slot, to_place, slot, w_dec, w_mid, w_up, outgoing, own, halo_ref,
+    raw_ref, field, lift, rot, w_ref, wm_ref, stack, wide, incoming, reply, returned,
+    cells, grid, turned, mixed, face, landed, local, relays, sends, recvs,
+):
+    step = pl.program_id(0)
+    bricks = own.shape[0]
+    part = bricks // 4
+    total = bricks + 8 * part
+    ring = Exchange(lambda c: face, lambda k, c: landed.at[k], sends, recvs, 1)
+    out = Relay(outgoing, incoming, relays.at[0])
+    back = Relay(reply, returned, relays.at[1])
+
+    @pl.when(step == 0)
+    def _():
+        barrier = pltpu.get_barrier_semaphore()
+        each_peer(
+            lambda d, peer: pl.semaphore_signal(barrier, inc=1, device_id=peer, device_id_type=MESH)
+        )
+        mine = pltpu.make_async_copy(own, rot.at[0, pl.ds(0, bricks)], local.at[8])
+        mine.start()
+        piece = lambda k: pltpu.make_async_copy(
+            halo_ref.at[k], rot.at[0, pl.ds(bricks + k * part, part)], local.at[k]
+        )
+        for k in range(8):
+
+            @pl.when(ring.has(*OFFSETS[k]))
+            def _():
+                piece(k).start()
+
+        pl.semaphore_wait(barrier, out.devices - 1)
+        out.start()
+        for j in range(4):
+            rot[j, total] = jnp.zeros((3, 16, 128), BF16)
+        widen(w_ref, w_dec)
+        widen(wm_ref, w_mid)
+        grid[...] = jnp.zeros(grid.shape, BF16)
+        mine.wait()
+        rotate_range(rot, 0, bricks)
+        for k in range(8):
+            here = ring.has(*OFFSETS[k])
+
+            @pl.when(here)
+            def _():
+                piece(k).wait()
+
+            @pl.when(jnp.logical_not(here))
+            def _():
+                def clear(n, carry):
+                    rot[0, bricks + k * part + n] = jnp.zeros((3, 16, 128), BF16)
+                    return carry
+
+                lax.fori_loop(0, part, clear, 0)
+
+        rotate_range(rot, bricks, total)
+        merge_weights(w_up, w_dec, lift, stack, wide)
+        out.wait()
+        coarse_mix(from_slot, to_place, wm_ref, incoming, reply, cells, grid, turned, mixed)
+        back.start()
+
+    for u, tile in enumerate(conv_block(step, table, w_ref, rot)):
+        raw_ref[:, u] = tile.reshape(BLOCK, 16, 128)
+
+    def take(b, carry):
+        value = returned[slot[b]].astype(F32)
+        field[b] = jnp.where(b < count[0], value, 0.0)
+        return carry
+
+    @pl.when(step == 3)
+    def _():
+        back.wait()
+        lax.fori_loop(0, part, take, 0, unroll=8)
+        face[...] = field[pl.ds(0, part)].reshape(face.shape).astype(BF16)
+        ring.start(0)
+        lax.fori_loop(part, bricks, take, 0, unroll=8)
+        field[total] = jnp.zeros((8, 128), F32)
+
+    @pl.when(step == 4)
+    def _():
+        ring.forward(0)
+
+    @pl.when(step == 5)
+    def _():
+        for k in (3, 4, 1, 6, 0, 2, 5, 7):
+            begin = bricks + k * part
+            here = ring.has(*OFFSETS[k])
+            if OFFSETS[k][1]:
+                ring.arrive(k)
+
+            @pl.when(here)
+            def _():
+                field[pl.ds(begin, part)] = landed[k].astype(F32).reshape(part, 8, 128)
+
+            @pl.when(jnp.logical_not(here))
+            def _():
+                field[pl.ds(begin, part)] = jnp.zeros((part, 8, 128), F32)
+
+        ring.finish()
+
+
+def middle(table, count, from_slot, to_place, slot, w_dec, w_mid, w_up, outgoing, own, halos):
+    bricks = own.shape[0]
+    part = bricks // 4
+    total = bricks + 8 * part
+    chans = w_up.shape[0]
     places = from_slot.shape[0]
+    assert bricks == 6 * BLOCK
+    relayed = pltpu.VMEM(outgoing.shape, BF16)
     return pl.pallas_call(
-        coarse_kernel,
-        out_shape=jax.ShapeDtypeStruct(incoming.shape, BF16),
-        in_specs=[SMEM, SMEM, VMEM, VMEM, ANY],
-        out_specs=VMEM,
+        middle_kernel,
+        grid=(bricks // BLOCK,),
+        out_shape=(
+            jax.ShapeDtypeStruct((bricks, 3, 16, 128), F32),
+            jax.ShapeDtypeStruct((total + 1, 8, 128), F32),
+            jax.ShapeDtypeStruct((TAPS + 1, 128, 8 * chans), BF16),
+        ),
+        in_specs=[SMEM] * 5 + [VMEM] * 4 + [ANY, ANY],
+        out_specs=(pl.BlockSpec((BLOCK, 3, 16, 128), lambda i: (i, 0, 0, 0)), VMEM, VMEM),
         scratch_shapes=[
+            pltpu.VMEM((4, total + 1, 3, 16, 128), BF16),
+            pltpu.VMEM((TAPS + 1, 96, 128), BF16),
+            pltpu.VMEM((TAPS + 1, 128, 128), BF16),
+            pltpu.VMEM((8 * chans, chans), BF16),
+            pltpu.VMEM((chans, 128), BF16),
+            relayed, relayed, relayed,
             pltpu.VMEM((places * 8, 128), F32),
             pltpu.VMEM((6, 6, 6, 32, 128), BF16),
-            pltpu.VMEM((places * 8 + 8, 128), F32),
-            pltpu.VMEM((TAPS + 1, 128, 128), BF16),
-        ],
-        compiler_params=pltpu.CompilerParams(vmem_limit_bytes=32 * MIB),
-        name="coarse_mix",
-    )(from_slot, to_place, w, incoming, after)
-
-
-def spread_kernel(slot, count, in_ref, out_ref, face, landed, sends, recvs):
-    bricks = slot.shape[0]
-    part = bricks // 4
-    ring = Exchange(lambda c: face, lambda k, c: landed.at[k], sends, recvs, 1)
-    ring.greet()
-
-    def take(b, carry):
-        value = in_ref[slot[b]].astype(F32)
-        out_ref[b] = jnp.where(b < count[0], value, 0.0)
-        return carry
-
-    lax.fori_loop(0, part, take, 0, unroll=8)
-    face[...] = out_ref[pl.ds(0, part)].reshape(face.shape).astype(BF16)
-    ring.meet()
-    ring.start(0)
-    lax.fori_loop(part, bricks, take, 0, unroll=8)
-    out_ref[bricks + 8 * part] = jnp.zeros((8, 128), F32)
-    ring.forward(0)
-    for k in (3, 4, 1, 6, 0, 2, 5, 7):
-        begin = bricks + k * part
-        here = ring.has(*OFFSETS[k])
-        if OFFSETS[k][1]:
-            ring.arrive(k)
-
-        @pl.when(here)
-        def _():
-            out_ref[pl.ds(begin, part)] = landed[k].astype(F32).reshape(part, 8, 128)
-
-        @pl.when(jnp.logical_not(here))
-        def _():
-            out_ref[pl.ds(begin, part)] = jnp.zeros((part, 8, 128), F32)
-
-    ring.finish()
-
-
-def spread(slot, count, returned):
-    bricks = slot.shape[0]
-    part = bricks // 4
-    return pl.pallas_call(
-        spread_kernel,
-        out_shape=jax.ShapeDtypeStruct((bricks + 8 * part + 1, 8, 128), F32),
-        in_specs=[SMEM, SMEM, VMEM],
-        out_specs=VMEM,
-        scratch_shapes=[
+            pltpu.VMEM((places * 8, 128), F32),
+            pltpu.VMEM((places + 1, 8, 128), F32),
             pltpu.VMEM((part // 2, 16, 128), BF16),
             pltpu.VMEM((8, part // 2, 16, 128), BF16),
+            pltpu.SemaphoreType.DMA((9,)),
+            pltpu.SemaphoreType.DMA((2, 2)),
             pltpu.SemaphoreType.DMA((8, 1)),
             pltpu.SemaphoreType.DMA((8, 1)),
         ],
         compiler_params=pltpu.CompilerParams(
-            vmem_limit_bytes=16 * MIB, collective_id=2, has_side_effects=True
+            vmem_limit_bytes=60 * MIB, collective_id=2, has_side_effects=True
         ),
-        name="spread",
-    )(slot, count, returned)
-
-
-def merge_kernel(up_ref, w_in, out_ref, stack, wide):
+        name="middle",
+    )(table, count, from_slot, to_place, slot, w_dec, w_mid, w_up, outgoing, own, halos)
+
+
+def merge_weights(up_ref, w_in, out_ref, stack, wide):
     chans = up_ref.shape[0]
     out_ref[...] = jnp.zeros(out_ref.shape, BF16)
     wide[...] = jnp.zeros(wide.shape, BF16)
@@ -581,20 +626,6 @@
         return carry
 
     lax.fori_loop(0, TAPS, body, 0)
-
-
-def merge(w_up, w):
-    chans = w_up.shape[0]
-    return pl.pallas_call(
-        merge_kernel,
-        out_shape=jax.ShapeDtypeStruct((TAPS + 1, 128, 8 * chans), BF16),
-        in_specs=[VMEM, VMEM],
-        out_specs=VMEM,
-        scratch_shapes=[pltpu.VMEM((8 * chans, chans), BF16), pltpu.VMEM((chans, 128), BF16)],
-        compiler_params=pltpu.CompilerParams(vmem_limit_bytes=24 * MIB),
-        cost_estimate=pl.CostEstimate(flops=8_000_000_000, bytes_accessed=8_000_000, transcendentals=0),
-        name="merge",
-    )(w_up, w)
 
 
 def decode_kernel(table, count, w_ref, up_ref, cells, raw_ref, enc_ref, out_ref):
@@ -680,12 +711,9 @@
         jnp.where(index[:, None] == to_place[None, :], slot_ids[None, :], 0), axis=1
     )
     encoded, outgoing, encoded_halo = encode(table, count, send_slot, w_enc, w_down, features[0])
-    incoming = relay(outgoing, devices)
-    lift = merge(w_up, w_dec)
-    reply = coarse(from_slot, to_place, w_mid, incoming, lift)
-    returned = relay(reply, devices)
-    raw = raw_conv(table, w_dec, encoded, encoded_halo, reply)
-    cells = spread(slot, count, returned)
+    raw, cells, lift = middle(
+        table, count, from_slot, to_place, slot, w_dec, w_mid, w_up, outgoing, encoded, encoded_halo
+    )
     decoded = decode(table, count, lift.reshape(-1, lift.shape[2]), w_up, cells, raw, encoded)
     return decoded[None]
 

time: 170 us -> 154 us (0.906); the launches traced: 169 us -> 150 us
  starting transfers between devices: 15.2 us -> 0 us
  waiting for transfers between devices: 4.27 us -> 0 us
  local copies, waits for them, and re-layouts: 6.69 us -> 3.4 us
  other arithmetic: 3.83 us -> 7 us
    all_to_all x2 -> x0, starting transfers between devices: 15.2 us -> none  [relay(): lax.all_to_all(buffer.reshape(devices, -1, 128), ('gz', 'gx'), split_axis...]
    all_to_all x2 -> x0, waiting for transfers between devices: 4.27 us -> none  [relay(): lax.all_to_all(buffer.reshape(devices, -1, 128), ('gz', 'gx'), split_axis...]
    unnamed x19 -> x9, local copies, waits for them, and re-layouts: 6.69 us -> 3.4 us
    pallas_call x4 -> x1, Pallas kernels: 60.7 us -> 61.7 us  [middle(): pl.pallas_call(middle_kernel, grid=(bricks // BLOCK,), out_shape=(jax.Sha...]
  transfers between devices with their start and end apart: 2 -> 0, of which waited for: 1 -> 0; matrix products, arithmetic and copies ran while one was open for 0% -> 0% of each run, Pallas kernels for 24% -> 0%
where the time goes in v5:
time: 154 us; the launch traced here: 150 us
  Pallas kernels  139 us (90%)
  other arithmetic  7 us (5%)
  local copies, waits for them, and re-layouts  3.4 us (2%)
    pallas_call x1, Pallas kernels, middle(): pl.pallas_call(middle_kernel, grid=(bricks // BLOCK,), out_shape=(jax.Sha...  61.7 us
    pallas_call x1, Pallas kernels, encode(): pl.pallas_call(functools.partial(encode_kernel, parts, parts2), grid=(bri...  60 us
    pallas_call x1, Pallas kernels, decode(): pl.pallas_call(decode_kernel, grid=(bricks // block,), out_shape=jax.Shap...  17.7 us
    unnamed x9, local copies, waits for them, and re-layouts  3.4 us

profile of v5, /device:TPU:40, one launch (start us, length us, event | category | flops | bytes accessed | tf_op | source)
XLA Modules:
  0.0 150.5 jit_solution(9373129113084149781)
XLA Ops:
  0.7 0.9 convert_reduce_fusion
  1.6 0.7 multiply_add_fusion
  2.3 0.7 select_reduce_fusion.send_slot
  3.0 1.3 multiply_add_fusion.1.slot
  4.3 0.7 fusion.14
  5.0 0.6 fusion.7.to_place
  5.6 0.7 select_reduce_fusion.1.from_slot
  6.3 1.4 compare_select_fusion.table
  7.7 1.7 %copy.12.wd_in = bf16[768,96]{1,0:T(8,128)(2,1)} copy(bf16[768,96]{0,1:T(8,128)(2,1)} %param.16) | data formatting | bytes 294912 | tf_op args[6]
  9.4 60.0 %encode.1 = (bf16[192,3,16,128]{3,2,1,0:T(8,128)(2,1)}, bf16[384,8,128]{2,1,0:T(8,128)(2,1)}, bf16[8,48,3,16,128]{4,3,2,1,0:T(8,128)(2,1)}) custom-call(s32[27,192]{1,0:T(8,128)} %compare_select_fusion.table, s32[1]{0:T(128)} %bitcast.30.count, s32[384]{0:T(512)} %select_reduce_fusion.send_slot, bf16[27,96,96]{2,1,0:T(8,128)(2,1)} %w_in.1, ...), custom_call_target="tpu_custom_call" | custom-call | tf_op jit(solution)/shard_map/encode/pallas_call | solution.py:352
  69.3 0.0 copy-start
  69.4 0.0 copy-start.2
  69.4 0.0 copy-start.3
  69.4 61.7 %middle.1 = (f32[192,3,16,128]{3,2,1,0:T(8,128)}, f32[577,8,128]{2,1,0:T(8,128)}, bf16[28,128,768]{2,1,0:T(8,128)(2,1)}) custom-call(s32[27,192]{1,0:T(8,128)} %compare_select_fusion.table, s32[1]{0:T(128)} %bitcast.31.count, s32[192]{0:T(256)} %select_reduce_fusion.1.from_slot, s32[384]{0:T(512)} %fusion.7.to_place, s32[192]{0:T(256)} %multiply_add_fusion.1.slot, ...), custom_call_target="tpu_custom_call" | custom-call | tf_op jit(solution)/shard_map/middle/pallas_call | solution.py:574
  131.1 0.0 copy-done
  131.1 0.0 copy-done.2
  131.1 0.0 copy-done.3
  131.1 0.0 copy-start.1
  131.1 1.7 %copy-done.1 = f32[577,8,128]{2,1,0:T(8,128)S(1)} copy-done((f32[577,8,128]{2,1,0:T(8,128)S(1)}, f32[577,8,128]{2,1,0:T(8,128)}, u32[]{:S(2)}) %copy-start.1) | copy-done | bytes 2363416
  132.8 17.7 %decode.1 = bf16[192,6144]{1,0:T(8,128)(2,1)} custom-call(s32[27,192]{1,0:T(8,128)S(1)} %copy-done.3, s32[1]{0:T(128)} %bitcast.32.count, bf16[3584,768]{1,0:T(8,128)(2,1)} %bitcast.33, bf16[96,768]{1,0:T(8,128)(2,1)S(1)} %copy-done.2, f32[577,8,128]{2,1,0:T(8,128)S(1)} %copy-done.1, f32[192,3,16,128]{3,2,1,0:T(8,128)} %get-tuple-element.16.raw_ref, ...), custom_call_target="tpu_custom_call" | custom-call | tf_op jit(solution)/shard_map/decode/pallas_call | solution.py:669
Async XLA Ops:
  69.3 61.7 %copy-start = (bf16[192,3,16,128]{3,2,1,0:T(8,128)(2,1)S(1)}, bf16[192,3,16,128]{3,2,1,0:T(8,128)(2,1)}, u32[]{:S(2)}) copy-start(bf16[192,3,16,128]{3,2,1,0:T(8,128)(2,1)} %get-tuple-element.12.own.enc_ref) | copy-start | bytes 7077892
  69.4 61.7 %copy-start.2 = (bf16[96,768]{1,0:T(8,128)(2,1)S(1)}, bf16[96,768]{1,0:T(8,128)(2,1)}, u32[]{:S(2)}) copy-start(bf16[96,768]{1,0:T(8,128)(2,1)} %up_ref.1) | copy-start | bytes 442372
  69.4 61.7 %copy-start.3 = (s32[27,192]{1,0:T(8,128)S(1)}, s32[27,192]{1,0:T(8,128)}, u32[]{:S(2)}) copy-start(s32[27,192]{1,0:T(8,128)} %compare_select_fusion.table) | copy-start | bytes 62212
  131.1 1.7 %copy-start.1 = (f32[577,8,128]{2,1,0:T(8,128)S(1)}, f32[577,8,128]{2,1,0:T(8,128)}, u32[]{:S(2)}) copy-start(f32[577,8,128]{2,1,0:T(8,128)} %get-tuple-element.15.cells) | copy-start | bytes 7090180

commit v6 on v5

--- a/solution.py
+++ b/solution.py
@@ -266,10 +266,11 @@
             rot[j, total] = jnp.zeros((3, 16, 128), BF16)
         pooled[bricks] = jnp.zeros((8, 128), F32)
         widen(w_ref, w_in)
-        wd_ref[...] = jnp.zeros(wd_ref.shape, BF16)
-        half, chans = wd_in.shape[0] // 2, wd_in.shape[1]
-        wd_ref[:, :chans] = wd_in[:half]
-        wd_ref[:, 128 : 128 + chans] = wd_in[half:]
+        chans, half = wd_in.shape[0], wd_in.shape[1] // 2
+        for h in range(2):
+            side = wd_in[:, h * half : (h + 1) * half].astype(F32)
+            side = jnp.concatenate([side, jnp.zeros((128 - chans, half), F32)], axis=0)
+            wd_ref[:, h * 128 : (h + 1) * 128] = side.T.astype(BF16)
         densify(part, 2 * part)
         first.forward(0)
         densify(2 * part, 3 * part)
@@ -310,20 +311,20 @@
     def _():
         face[pl.ds(BLOCK, part - BLOCK)] = enc_ref[: part - BLOCK]
         second.start(2)
+        second.forward(0)
 
     @pl.when(step == 2)
     def _():
-        second.forward(0)
+        second.forward(1)
 
     @pl.when(step == 3)
     def _():
-        second.forward(1)
         second.forward(2)
 
     @pl.when(step == pl.num_programs(0) - 1)
     def _():
         def place(s, carry):
-            out_ref[s] = pooled[send_slot[s]].astype(BF16)
+            out_ref[s] = pooled[send_slot[0, s]].astype(BF16)
             return carry
 
         lax.fori_loop(0, out_ref.shape[0], place, 0, unroll=8)
@@ -345,7 +346,7 @@
 def encode(table, count, send_slot, w, wd, x):
     bricks = x.shape[0]
     part = bricks // 4
-    slots = send_slot.shape[0]
+    slots = send_slot.shape[1]
     parts, parts2 = 6, 3
     sems = pltpu.SemaphoreType.DMA((8, parts))
     sems2 = pltpu.SemaphoreType.DMA((8, parts2))
@@ -364,7 +365,7 @@
             pltpu.VMEM((bricks + 1, 8, 128), F32),
             pltpu.VMEM((part, 3, 16, 128), BF16),
             pltpu.VMEM((TAPS + 1, 96, 128), BF16),
-            pltpu.VMEM((wd.shape[0] // 2, 256), BF16),
+            pltpu.VMEM((wd.shape[1] // 2, 256), BF16),
             sems, sems, sems2, sems2,
         ],
         compiler_params=pltpu.CompilerParams(
@@ -375,11 +376,11 @@
 
 
 def coarse_mix(from_slot, to_place, w_ref, in_ref, out_ref, cells, grid, turned, mixed):
-    places = from_slot.shape[0]
+    places = from_slot.shape[1]
     groups = places // 8
 
     def land(p, carry):
-        cells[pl.ds(pl.multiple_of(p * 8, 8), 8)] = in_ref[from_slot[p]].astype(F32)
+        cells[pl.ds(pl.multiple_of(p * 8, 8), 8)] = in_ref[from_slot[0, p]].astype(F32)
         return carry
 
     lax.fori_loop(0, places, land, 0, unroll=8)
@@ -414,7 +415,7 @@
     mixed[places] = jnp.zeros((8, 128), F32)
 
     def reply(s, carry):
-        out_ref[s] = mixed[to_place[s]].astype(BF16)
+        out_ref[s] = mixed[to_place[0, s]].astype(BF16)
         return carry
 
     lax.fori_loop(0, out_ref.shape[0], reply, 0, unroll=8)
@@ -527,7 +528,7 @@
         raw_ref[:, u] = tile.reshape(BLOCK, 16, 128)
 
     def take(b, carry):
-        value = returned[slot[b]].astype(F32)
+        value = returned[slot[0, b]].astype(F32)
         field[b] = jnp.where(b < count[0], value, 0.0)
         return carry
 
@@ -568,7 +569,7 @@
     part = bricks // 4
     total = bricks + 8 * part
     chans = w_up.shape[0]
-    places = from_slot.shape[0]
+    places = from_slot.shape[1]
     assert bricks == 6 * BLOCK
     relayed = pltpu.VMEM(outgoing.shape, BF16)
     return pl.pallas_call(
@@ -684,33 +685,61 @@
     return moved.reshape(-1, 8, 128)
 
 
+def route_kernel(cap, owner, arrival, near, send_ref, slot_ref, from_ref, place_ref, table_ref):
+    bricks, slots = owner.shape[1], arrival.shape[1]
+    part = bricks // 4
+    n = near[:, 0]
+    m = n - bricks
+    moved = jnp.where(m >= 5 * part, n - part, jnp.where(m >= 4 * part, m - 4 * part, n))
+    table_ref[...] = jnp.where(n < 0, bricks + 8 * part, moved)
+    wide = 256
+    row = jnp.concatenate([owner[...].astype(F32), jnp.full((1, wide - bricks), -1.0, F32)], axis=1)
+    row = jnp.broadcast_to(row, (wide, wide))
+    column = row.T
+    down = lax.broadcasted_iota(jnp.int32, (wide, wide), 0)
+    across = lax.broadcasted_iota(jnp.int32, (wide, wide), 1)
+    same = row == column
+    one = lambda x: jnp.where(x, 1.0, 0.0)
+    slot_row = row[:1] * cap + jnp.sum(one(same & (down < across)), axis=0, keepdims=True)
+    slot_column = column[:, :1] * cap + jnp.sum(one(same & (across < down)), axis=1, keepdims=True)
+    slot_ref[...] = slot_row[:, :bricks].astype(jnp.int32)
+    ids = lax.broadcasted_iota(jnp.int32, (bricks, slots), 1).astype(F32)
+    brick = lax.broadcasted_iota(jnp.int32, (bricks, slots), 0).astype(F32)
+    found = jnp.where(slot_column[:bricks] == ids, brick, float(bricks))
+    send_ref[...] = jnp.min(found, axis=0, keepdims=True).astype(jnp.int32)
+    cell = arrival[...]
+    place = jnp.where(cell < 0, bricks, (cell & 7) * (bricks // 8) + (cell >> 3))
+    place_ref[...] = place
+    turned = jnp.broadcast_to(place.astype(F32), (128, slots)).T[:, :1]
+    places = lax.broadcasted_iota(jnp.int32, (slots, bricks), 1).astype(F32)
+    source = lax.broadcasted_iota(jnp.int32, (slots, bricks), 0).astype(F32)
+    from_ref[...] = jnp.sum(
+        jnp.where(turned == places, source, 0.0), axis=0, keepdims=True
+    ).astype(jnp.int32)
+
+
+def route(cap, owner, arrival, near):
+    bricks, slots = owner.shape[1], arrival.shape[1]
+    one = lambda n: jax.ShapeDtypeStruct((1, n), jnp.int32)
+    return pl.pallas_call(
+        functools.partial(route_kernel, cap),
+        out_shape=(one(slots), one(bricks), one(bricks), one(slots), jax.ShapeDtypeStruct((near.shape[0], bricks), jnp.int32)),
+        in_specs=[VMEM, VMEM, VMEM],
+        out_specs=(VMEM, VMEM, VMEM, VMEM, VMEM),
+        name="route",
+    )(owner, arrival, near)
+
+
 def on_device(
     features, active_count, neighbors, owner, arrival_cell, w_enc, w_down, w_mid, w_up, w_dec
 ):
     devices = lax.axis_size("gz") * lax.axis_size("gx")
-    bricks = features.shape[1]
-    boundary = bricks // 4
-    capacity = arrival_cell.shape[1] // devices
-    slot_count = devices * capacity
     count = active_count[0]
-    n = neighbors[0]
-    m = n - bricks
-    side = m // boundary
-    n = jnp.where(m >= 4 * boundary, jnp.where(side == 4, m - 4 * boundary, n - boundary), n)
-    empty = bricks + 8 * boundary
-    table = jnp.where(n < 0, empty, n)
-    target = owner[0]
-    index = jnp.arange(bricks, dtype=jnp.int32)
-    same = jnp.logical_and(target[:, None] == target[None, :], index[None, :] < index[:, None])
-    slot = target * capacity + jnp.sum(same.astype(jnp.int32), axis=1)
-    slot_ids = jnp.arange(slot_count, dtype=jnp.int32)
-    send_slot = jnp.min(jnp.where(slot_ids[:, None] == slot[None, :], index[None, :], bricks), axis=1)
-    arrivals = arrival_cell[0]
-    to_place = jnp.where(arrivals < 0, bricks, arrivals % 8 * (bricks // 8) + arrivals // 8)
-    from_slot = jnp.sum(
-        jnp.where(index[:, None] == to_place[None, :], slot_ids[None, :], 0), axis=1
+    near = neighbors.reshape(neighbors.shape[1], 1, neighbors.shape[2])
+    send_slot, slot, from_slot, to_place, table = route(
+        arrival_cell.shape[1] // devices, owner, arrival_cell, near
     )
-    encoded, outgoing, encoded_halo = encode(table, count, send_slot, w_enc, w_down, features[0])
+    encoded, outgoing, encoded_halo = encode(table, count, send_slot, w_enc, w_down.T, features[0])
     raw, cells, lift = middle(
         table, count, from_slot, to_place, slot, w_dec, w_mid, w_up, outgoing, encoded, encoded_halo
     )

time: 154 us -> 146 us (0.948); the launches traced: 150 us -> 144 us
  other arithmetic: 7 us -> 0 us
  Pallas kernels: 139 us -> 142 us
  local copies, waits for them, and re-layouts: 3.4 us -> 1.68 us
    select_n x2 -> x0, other arithmetic: 1.98 us -> none  [the longest x1 1.39 us: on_device(): table = jnp.where(n < 0, empty, n)]
    add x2 -> x0, other arithmetic: 1.95 us -> none  [on_device(): slot = target * capacity + jnp.sum(same.astype(jnp.int32), axis=1)]
    pallas_call x0 -> x1, Pallas kernels: none -> 1.86 us  [route(): pl.pallas_call(functools.partial(route_kernel, cap), out_shape=(one(slots...]
    unnamed x9 -> x8, local copies, waits for them, and re-layouts: 3.4 us -> 1.68 us
    reduce_sum x2 -> x0, other arithmetic: 1.65 us -> none  [the longest x1 0.94 us: on_device(): slot = target * capacity + jnp.sum(same.astype(jnp.int32), axis=1)]
where the time goes in v6:
time: 146 us; the launch traced here: 144 us
  Pallas kernels  142 us (97%)
  local copies, waits for them, and re-layouts  1.68 us (1%)
    pallas_call x1, Pallas kernels, encode(): pl.pallas_call(functools.partial(encode_kernel, parts, parts2), grid=(bri...  61.3 us
    pallas_call x1, Pallas kernels, middle(): pl.pallas_call(middle_kernel, grid=(bricks // BLOCK,), out_shape=(jax.Sha...  60.9 us
    pallas_call x1, Pallas kernels, decode(): pl.pallas_call(decode_kernel, grid=(bricks // block,), out_shape=jax.Shap...  17.7 us

profile of v6, /device:TPU:40, one launch (start us, length us, event | category | flops | bytes accessed | tf_op | source)
XLA Modules:
  0.0 144.2 jit_solution(5014825434462952639)
XLA Ops:
  0.7 1.9 %route.1 = (s32[1,384]{1,0:T(1,128)}, s32[1,192]{1,0:T(1,128)}, s32[1,192]{1,0:T(1,128)}, s32[1,384]{1,0:T(1,128)}, s32[27,192]{1,0:T(8,128)}) custom-call(s32[1,192]{1,0:T(1,128)} %owner.1, s32[1,384]{1,0:T(1,128)} %arrival.1, s32[27,1,192]{2,1,0:T(1,128)} %bitcast.12), custom_call_target="tpu_custom_call" | custom-call | tf_op jit(solution)/shard_map/route/pallas_call | solution.py:724
  2.5 61.3 %encode.1 = (bf16[192,3,16,128]{3,2,1,0:T(8,128)(2,1)}, bf16[384,8,128]{2,1,0:T(8,128)(2,1)}, bf16[8,48,3,16,128]{4,3,2,1,0:T(8,128)(2,1)}) custom-call(s32[27,192]{1,0:T(8,128)} %get-tuple-element.16.table, s32[1]{0:T(128)} %bitcast.6.count, s32[1,384]{1,0:T(1,128)} %get-tuple-element.20.send_slot, bf16[27,96,96]{2,1,0:T(8,128)(2,1)} %w_in.1, ...), custom_call_target="tpu_custom_call" | custom-call | tf_op jit(solution)/shard_map/encode/pallas_call | solution.py:353
  63.9 0.0 copy-start
  63.9 0.0 copy-start.2
  63.9 0.0 copy-start.3
  63.9 60.9 %middle.1 = (f32[192,3,16,128]{3,2,1,0:T(8,128)}, f32[577,8,128]{2,1,0:T(8,128)}, bf16[28,128,768]{2,1,0:T(8,128)(2,1)}) custom-call(s32[27,192]{1,0:T(8,128)} %get-tuple-element.16.table, s32[1]{0:T(128)} %bitcast.7.count, s32[1,192]{1,0:T(1,128)} %get-tuple-element.17.from_slot, s32[1,384]{1,0:T(1,128)} %get-tuple-element.18.to_place, ...), custom_call_target="tpu_custom_call" | custom-call | tf_op jit(solution)/shard_map/middle/pallas_call | solution.py:575
  124.8 0.0 copy-done
  124.9 0.0 copy-done.2
  124.9 0.0 copy-done.3
  124.9 0.0 copy-start.1
  124.9 1.7 %copy-done.1 = f32[577,8,128]{2,1,0:T(8,128)S(1)} copy-done((f32[577,8,128]{2,1,0:T(8,128)S(1)}, f32[577,8,128]{2,1,0:T(8,128)}, u32[]{:S(2)}) %copy-start.1) | copy-done | bytes 2363416
  126.5 17.7 %decode.1 = bf16[192,6144]{1,0:T(8,128)(2,1)} custom-call(s32[27,192]{1,0:T(8,128)S(1)} %copy-done.3, s32[1]{0:T(128)} %bitcast.8.count, bf16[3584,768]{1,0:T(8,128)(2,1)} %bitcast.9, bf16[96,768]{1,0:T(8,128)(2,1)S(1)} %copy-done.2, f32[577,8,128]{2,1,0:T(8,128)S(1)} %copy-done.1, f32[192,3,16,128]{3,2,1,0:T(8,128)} %get-tuple-element.26.raw_ref, ...), custom_call_target="tpu_custom_call" | custom-call | tf_op jit(solution)/shard_map/decode/pallas_call | solution.py:670
Async XLA Ops:
  63.9 61.0 %copy-start = (bf16[192,3,16,128]{3,2,1,0:T(8,128)(2,1)S(1)}, bf16[192,3,16,128]{3,2,1,0:T(8,128)(2,1)}, u32[]{:S(2)}) copy-start(bf16[192,3,16,128]{3,2,1,0:T(8,128)(2,1)} %get-tuple-element.22.own.enc_ref) | copy-start | bytes 7077892
  63.9 61.0 %copy-start.2 = (bf16[96,768]{1,0:T(8,128)(2,1)S(1)}, bf16[96,768]{1,0:T(8,128)(2,1)}, u32[]{:S(2)}) copy-start(bf16[96,768]{1,0:T(8,128)(2,1)} %up_ref.1) | copy-start | bytes 442372
  63.9 61.0 %copy-start.3 = (s32[27,192]{1,0:T(8,128)S(1)}, s32[27,192]{1,0:T(8,128)}, u32[]{:S(2)}) copy-start(s32[27,192]{1,0:T(8,128)} %get-tuple-element.16.table) | copy-start | bytes 62212
  124.9 1.7 %copy-start.1 = (f32[577,8,128]{2,1,0:T(8,128)S(1)}, f32[577,8,128]{2,1,0:T(8,128)}, u32[]{:S(2)}) copy-start(f32[577,8,128]{2,1,0:T(8,128)} %get-tuple-element.25.cells) | copy-start | bytes 7090180

commit v7 on v6

--- a/solution.py
+++ b/solution.py
@@ -54,8 +54,9 @@
 
 
 class Exchange:
-    def __init__(self, own, landing, send, recv, chunks):
+    def __init__(self, own, landing, send, recv, chunks, late=()):
         self.own, self.landing, self.send, self.recv, self.chunks = own, landing, send, recv, chunks
+        self.late = late
         self.z, self.x = lax.axis_index("gz"), lax.axis_index("gx")
         self.layers, self.slabs = lax.axis_size("gz"), lax.axis_size("gx")
 
@@ -75,16 +76,30 @@
             return jnp.logical_and(*sides)
         return self.has(-dz, -dx)
 
-    def copy(self, slot, c):
+    def turns(self, dx):
+        return self.x % 2 == (1 if dx > 0 else 0)
+
+    def passes(self, slot, c):
+        if c in self.late and all(OFFSETS[slot]):
+            return jnp.logical_and(self.sends(slot), self.turns(OFFSETS[slot][1]))
+        return self.sends(slot)
+
+    def crosses(self, slot):
         dz, dx = OFFSETS[slot]
-        if dz and dx:
+        return jnp.logical_and(jnp.logical_and(self.has(0, dx), self.has(-dz, 0)), self.turns(dx))
+
+    def copy(self, slot, c, across=False):
+        dz, dx = OFFSETS[slot]
+        if across:
+            source, target = self.landing(OFFSETS.index((0, dx)), c), (self.z - dz, self.x)
+        elif dz and dx:
             source, target = self.landing(OFFSETS.index((dz, 0)), c), (self.z, self.x - dx)
         else:
             source, target = self.own(c), (self.z - dz, self.x - dx)
         return pltpu.make_async_remote_copy(
             src_ref=source,
             dst_ref=self.landing(slot, c),
-            send_sem=self.send.at[slot, c],
+            send_sem=self.send.at[slot + 8 if across else slot, c],
             recv_sem=self.recv.at[slot, c],
             device_id=target,
             device_id_type=MESH,
@@ -105,12 +120,12 @@
         pl.semaphore_wait(pltpu.get_barrier_semaphore(), peers)
 
     def start(self, *chunks):
-        for c in chunks:
+        for c, d in zip(chunks, chunks[::-1] if self.late and self.late[0] else chunks):
             for slot in (1, 6, 3, 4):
 
                 @pl.when(self.sends(slot))
                 def _():
-                    self.copy(slot, c).start()
+                    self.copy(slot, d if slot in (3, 4) else c).start()
 
     def forward(self, c):
         for slot, corners in ((1, (0, 2)), (6, (5, 7))):
@@ -121,23 +136,43 @@
 
             for corner in corners:
 
-                @pl.when(self.sends(corner))
+                @pl.when(self.passes(corner, c))
                 def _():
                     self.copy(corner, c).start()
+
+    def across(self, c):
+        for slot, corners in ((3, (0, 5)), (4, (2, 7))):
+
+            @pl.when(self.has(*OFFSETS[slot]))
+            def _():
+                self.copy(slot, c).wait_recv()
+
+            for corner in corners:
+
+                @pl.when(self.crosses(corner))
+                def _():
+                    self.copy(corner, c, True).start()
 
     def arrive(self, slot):
         @pl.when(self.has(*OFFSETS[slot]))
         def _():
             for c in range(self.chunks):
-                self.copy(slot, c).wait_recv()
+                if OFFSETS[slot][0] or c not in self.late:
+                    self.copy(slot, c).wait_recv()
 
     def finish(self):
         for slot in range(8):
-
-            @pl.when(self.sends(slot))
-            def _():
-                for c in range(self.chunks):
+            for c in range(self.chunks):
+
+                @pl.when(self.passes(slot, c))
+                def _():
                     self.copy(slot, c).wait_send()
+
+                if c in self.late and all(OFFSETS[slot]):
+
+                    @pl.when(self.crosses(slot))
+                    def _():
+                        self.copy(slot, c, True).wait_send()
 
 
 def rotate_range(rot, start, stop, size=48):
@@ -223,12 +258,12 @@
     first = Exchange(
         lambda c: rot.at[0, pl.ds(c * size, size)],
         lambda slot, c: rot.at[0, pl.ds(bricks + slot * part + c * size, size)],
-        sends, recvs, parts,
+        sends, recvs, parts, (parts - 1, parts - 2),
     )
     second = Exchange(
         lambda c: face.at[pl.ds(c * size2, size2)],
         lambda slot, c: halo_ref.at[slot, pl.ds(c * size2, size2)],
-        sends2, recvs2, parts2,
+        sends2, recvs2, parts2, (0,),
     )
 
     def fill(slot):
@@ -275,6 +310,8 @@
         first.forward(0)
         densify(2 * part, 3 * part)
         first.forward(1)
+        first.across(5)
+        first.across(4)
         densify(3 * part, bricks)
         first.forward(2)
         rotate_range(rot, 0, 2 * part)
@@ -312,6 +349,7 @@
         face[pl.ds(BLOCK, part - BLOCK)] = enc_ref[: part - BLOCK]
         second.start(2)
         second.forward(0)
+        second.across(0)
 
     @pl.when(step == 2)
     def _():
@@ -348,8 +386,8 @@
     part = bricks // 4
     slots = send_slot.shape[1]
     parts, parts2 = 6, 3
-    sems = pltpu.SemaphoreType.DMA((8, parts))
-    sems2 = pltpu.SemaphoreType.DMA((8, parts2))
+    sems = pltpu.SemaphoreType.DMA((16, parts))
+    sems2 = pltpu.SemaphoreType.DMA((16, parts2))
     return pl.pallas_call(
         functools.partial(encode_kernel, parts, parts2),
         grid=(bricks // BLOCK,),
@@ -466,7 +504,7 @@
 
 def middle_kernel(
     table, count, from_slot, to_place, slot, w_dec, w_mid, w_up, outgoing, own, halo_ref,
-    raw_ref, field, lift, rot, w_ref, wm_ref, stack, wide, incoming, reply, returned,
+    raw_ref, field, lift_out, rot, lift, w_ref, wm_ref, stack, wide, incoming, reply, returned,
     cells, grid, turned, mixed, face, landed, local, relays, sends, recvs,
 ):
     step = pl.program_id(0)
@@ -520,6 +558,7 @@
 
         rotate_range(rot, bricks, total)
         merge_weights(w_up, w_dec, lift, stack, wide)
+        pltpu.make_async_copy(lift, lift_out, local.at[9]).start()
         out.wait()
         coarse_mix(from_slot, to_place, wm_ref, incoming, reply, cells, grid, turned, mixed)
         back.start()
@@ -562,6 +601,7 @@
                 field[pl.ds(begin, part)] = jnp.zeros((part, 8, 128), F32)
 
         ring.finish()
+        pltpu.make_async_copy(lift, lift_out, local.at[9]).wait()
 
 
 def middle(table, count, from_slot, to_place, slot, w_dec, w_mid, w_up, outgoing, own, halos):
@@ -581,9 +621,10 @@
             jax.ShapeDtypeStruct((TAPS + 1, 128, 8 * chans), BF16),
         ),
         in_specs=[SMEM] * 5 + [VMEM] * 4 + [ANY, ANY],
-        out_specs=(pl.BlockSpec((BLOCK, 3, 16, 128), lambda i: (i, 0, 0, 0)), VMEM, VMEM),
+        out_specs=(pl.BlockSpec((BLOCK, 3, 16, 128), lambda i: (i, 0, 0, 0)), VMEM, ANY),
         scratch_shapes=[
             pltpu.VMEM((4, total + 1, 3, 16, 128), BF16),
+            pltpu.VMEM((TAPS + 1, 128, 8 * chans), BF16),
             pltpu.VMEM((TAPS + 1, 96, 128), BF16),
             pltpu.VMEM((TAPS + 1, 128, 128), BF16),
             pltpu.VMEM((8 * chans, chans), BF16),
@@ -595,7 +636,7 @@
             pltpu.VMEM((places + 1, 8, 128), F32),
             pltpu.VMEM((part // 2, 16, 128), BF16),
             pltpu.VMEM((8, part // 2, 16, 128), BF16),
-            pltpu.SemaphoreType.DMA((9,)),
+            pltpu.SemaphoreType.DMA((10,)),
             pltpu.SemaphoreType.DMA((2, 2)),
             pltpu.SemaphoreType.DMA((8, 1)),
             pltpu.SemaphoreType.DMA((8, 1)),

time: 146 us -> 146 us (level)
    pallas_call x1, Pallas kernels: 61.3 us -> 59.6 us  [encode(): pl.pallas_call(functools.partial(encode_kernel, parts, parts2), grid=(bri...]
where the time goes in v7:
time: 146 us; the launch traced here: 143 us
  Pallas kernels  141 us (97%)
  local copies, waits for them, and re-layouts  1.68 us (1%)
    pallas_call x1, Pallas kernels, middle(): pl.pallas_call(middle_kernel, grid=(bricks // BLOCK,), out_shape=(jax.Sha...  61.5 us
    pallas_call x1, Pallas kernels, encode(): pl.pallas_call(functools.partial(encode_kernel, parts, parts2), grid=(bri...  59.6 us
    pallas_call x1, Pallas kernels, decode(): pl.pallas_call(decode_kernel, grid=(bricks // block,), out_shape=jax.Shap...  17.7 us

profile of v7, /device:TPU:40, one launch (start us, length us, event | category | flops | bytes accessed | tf_op | source)
XLA Modules:
  0.0 143.0 jit_solution(2728931455998683881)
XLA Ops:
  0.7 1.9 %route.1 = (s32[1,384]{1,0:T(1,128)}, s32[1,192]{1,0:T(1,128)}, s32[1,192]{1,0:T(1,128)}, s32[1,384]{1,0:T(1,128)}, s32[27,192]{1,0:T(8,128)}) custom-call(s32[1,192]{1,0:T(1,128)} %owner.1, s32[1,384]{1,0:T(1,128)} %arrival.1, s32[27,1,192]{2,1,0:T(1,128)} %bitcast.12), custom_call_target="tpu_custom_call" | custom-call | tf_op jit(solution)/shard_map/route/pallas_call | solution.py:765
  2.5 59.6 %encode.1 = (bf16[192,3,16,128]{3,2,1,0:T(8,128)(2,1)}, bf16[384,8,128]{2,1,0:T(8,128)(2,1)}, bf16[8,48,3,16,128]{4,3,2,1,0:T(8,128)(2,1)}) custom-call(s32[27,192]{1,0:T(8,128)} %get-tuple-element.16.table, s32[1]{0:T(128)} %bitcast.6.count, s32[1,384]{1,0:T(1,128)} %get-tuple-element.20.send_slot, bf16[27,96,96]{2,1,0:T(8,128)(2,1)} %w_in.1, ...), custom_call_target="tpu_custom_call" | custom-call | tf_op jit(solution)/shard_map/encode/pallas_call | solution.py:391
  62.1 0.0 copy-start
  62.1 0.0 copy-start.2
  62.1 0.0 copy-start.3
  62.1 61.5 %middle.1 = (f32[192,3,16,128]{3,2,1,0:T(8,128)}, f32[577,8,128]{2,1,0:T(8,128)}, bf16[28,128,768]{2,1,0:T(8,128)(2,1)}) custom-call(s32[27,192]{1,0:T(8,128)} %get-tuple-element.16.table, s32[1]{0:T(128)} %bitcast.7.count, s32[1,192]{1,0:T(1,128)} %get-tuple-element.17.from_slot, s32[1,384]{1,0:T(1,128)} %get-tuple-element.18.to_place, ...), custom_call_target="tpu_custom_call" | custom-call | tf_op jit(solution)/shard_map/middle/pallas_call | solution.py:615
  123.6 0.0 copy-done
  123.6 0.0 copy-done.2
  123.6 0.0 copy-done.3
  123.6 0.0 copy-start.1
  123.7 1.7 %copy-done.1 = f32[577,8,128]{2,1,0:T(8,128)S(1)} copy-done((f32[577,8,128]{2,1,0:T(8,128)S(1)}, f32[577,8,128]{2,1,0:T(8,128)}, u32[]{:S(2)}) %copy-start.1) | copy-done | bytes 2363416
  125.3 17.7 %decode.1 = bf16[192,6144]{1,0:T(8,128)(2,1)} custom-call(s32[27,192]{1,0:T(8,128)S(1)} %copy-done.3, s32[1]{0:T(128)} %bitcast.8.count, bf16[3584,768]{1,0:T(8,128)(2,1)} %bitcast.9, bf16[96,768]{1,0:T(8,128)(2,1)S(1)} %copy-done.2, f32[577,8,128]{2,1,0:T(8,128)S(1)} %copy-done.1, f32[192,3,16,128]{3,2,1,0:T(8,128)} %get-tuple-element.26.raw_ref, ...), custom_call_target="tpu_custom_call" | custom-call | tf_op jit(solution)/shard_map/decode/pallas_call | solution.py:711
Async XLA Ops:
  62.1 61.5 %copy-start = (bf16[192,3,16,128]{3,2,1,0:T(8,128)(2,1)S(1)}, bf16[192,3,16,128]{3,2,1,0:T(8,128)(2,1)}, u32[]{:S(2)}) copy-start(bf16[192,3,16,128]{3,2,1,0:T(8,128)(2,1)} %get-tuple-element.22.own.enc_ref) | copy-start | bytes 7077892
  62.1 61.5 %copy-start.2 = (bf16[96,768]{1,0:T(8,128)(2,1)S(1)}, bf16[96,768]{1,0:T(8,128)(2,1)}, u32[]{:S(2)}) copy-start(bf16[96,768]{1,0:T(8,128)(2,1)} %up_ref.1) | copy-start | bytes 442372
  62.1 61.5 %copy-start.3 = (s32[27,192]{1,0:T(8,128)S(1)}, s32[27,192]{1,0:T(8,128)}, u32[]{:S(2)}) copy-start(s32[27,192]{1,0:T(8,128)} %get-tuple-element.16.table) | copy-start | bytes 62212
  123.6 1.7 %copy-start.1 = (f32[577,8,128]{2,1,0:T(8,128)S(1)}, f32[577,8,128]{2,1,0:T(8,128)}, u32[]{:S(2)}) copy-start(f32[577,8,128]{2,1,0:T(8,128)} %get-tuple-element.25.cells) | copy-start | bytes 7090180
